TPU v7x, 32 devices: a whole 2x2x4 slice. The times are simulated.
32 devices in a mesh: shard: 4 (over y, core), ctx: 2 (over x), tp: 4 (over z).
Axes of the slice: x: 2, y: 2, z: 4, core: 2. Of those that a mesh axis runs over, the one named last changes fastest.
Arguments:
- hidden_in: bfloat16 [6144, 1536], P(('shard', 'ctx')), may hold values from -6 to 6
- seq_lengths: int32 [4], P('shard'), may hold values from 384 to 1536, as said below
- attn_gain: bfloat16 [1536], P(('shard', 'ctx')), may hold values from 0.5 to 1.5
- ffn_gain: bfloat16 [1536], P(('shard', 'ctx')), may hold values from 0.5 to 1.5
- query_gain: bfloat16 [64], replicated, may hold values from 0.5 to 1.5
- key_gain: bfloat16 [64], replicated, may hold values from 0.5 to 1.5
- w_query: bfloat16 [1536, 1536], P(('shard', 'ctx'), 'tp'), may hold values from -0.15625 to 0.15625
- w_key: bfloat16 [1536, 512], P(('shard', 'ctx'), 'tp'), may hold values from -0.15625 to 0.15625
- w_value: bfloat16 [1536, 512], P(('shard', 'ctx'), 'tp'), may hold values from -0.15625 to 0.15625
- w_out: bfloat16 [1536, 1536], P('tp', ('shard', 'ctx')), may hold values from -1.25 to 1.25
- w_gate: bfloat16 [1536, 6912], P(('shard', 'ctx'), 'tp'), may hold values from -0.15625 to 0.15625
- w_up: bfloat16 [1536, 6912], P(('shard', 'ctx'), 'tp'), may hold values from -0.15625 to 0.15625
- w_down: bfloat16 [6912, 1536], P('tp', ('shard', 'ctx')), may hold values from -0.078125 to 0.078125
- out_grad: bfloat16 [6144, 1536], P(('shard', 'ctx')), may hold values from -6 to 6
Outputs:
- block_out: bfloat16 [6144, 1536], P(('shard', 'ctx'))
- input_grad: float32 [6144, 1536], P(('shard', 'ctx'))
- attn_gain_grad: float32 [1536], P(('shard', 'ctx'))
- ffn_gain_grad: float32 [1536], P(('shard', 'ctx'))
- query_gain_grad: float32 [64], replicated
- key_gain_grad: float32 [64], replicated
- w_query_grad: float32 [1536, 1536], P(('shard', 'ctx'), 'tp')
- w_key_grad: float32 [1536, 512], P(('shard', 'ctx'), 'tp')
- w_value_grad: float32 [1536, 512], P(('shard', 'ctx'), 'tp')
- w_out_grad: float32 [1536, 1536], P('tp', ('shard', 'ctx'))
- w_gate_grad: float32 [1536, 6912], P(('shard', 'ctx'), 'tp')
- w_up_grad: float32 [1536, 6912], P(('shard', 'ctx'), 'tp')
- w_down_grad: float32 [6912, 1536], P('tp', ('shard', 'ctx'))
Inputs may be any that keep to these rules, and one draw needn't show every extreme that they name: `seq_lengths`: one sequence, drawn from the seed, has all 1536 positions valid; every sequence has at least a quarter of them.
All inputs are finite; a program needn't handle non-finite values.
Results may differ from a plain program's by a relative error of at most 0.013.
Values may be sent and summed in bfloat16 or wider, within the bound.
A program may use at most 192 MiB of HBM per device.

v0:
```python
import math

import jax
import jax.numpy as jnp
from jax import lax
from jax.sharding import PartitionSpec as P

EPSILON = 1e-05
ROPE_BASE = 1000000.0


def norm_rows(value, gain):
    scale = lax.rsqrt(jnp.mean(value * value, axis=-1, keepdims=True) + EPSILON)
    return value * scale * gain


def rotate(values, positions):
    half = values.shape[-1] // 2
    freq = ROPE_BASE ** (-jnp.arange(half, dtype=jnp.float32) / half)
    angle = positions.astype(jnp.float32)[:, None] * freq[None, :]
    cosine = jnp.cos(angle)[:, None, :]
    sine = jnp.sin(angle)[:, None, :]
    first = values[..., :half]
    second = values[..., half:]
    return jnp.concatenate(
        [first * cosine - second * sine, second * cosine + first * sine], axis=-1
    )


def head_prep(proj, gain, positions):
    heads = proj.reshape(proj.shape[0], -1, gain.shape[0])
    return rotate(norm_rows(heads, gain), positions)


def activation(gate_in, up_in):
    return jax.nn.silu(gate_in) * up_in


def forward_product(left, right):
    return jnp.dot(left, right, preferred_element_type=jnp.float32)


def outer_product(left, right):
    return lax.dot_general(
        left, right, (((0,), (0,)), ((), ())), preferred_element_type=jnp.float32
    )


def back_product(grad, weight):
    return lax.dot_general(
        grad, weight, (((1,), (1,)), ((), ())), preferred_element_type=jnp.float32
    )


def body(
    hidden_in,
    seq_lengths,
    attn_gain,
    ffn_gain,
    query_gain,
    key_gain,
    w_query,
    w_key,
    w_value,
    w_out,
    w_gate,
    w_up,
    w_down,
    out_grad,
):
    rows = hidden_in.shape[0]
    head_dim = query_gain.shape[0]
    kv_heads = w_key.shape[1] // head_dim
    q_heads = w_query.shape[1] // head_dim
    group = q_heads // kv_heads
    pieces = lax.axis_size("ctx")
    scale = 1.0 / math.sqrt(head_dim)
    positions = lax.axis_index("ctx") * rows + jnp.arange(rows, dtype=jnp.int32)
    length = seq_lengths[0]
    valid = (positions < length).astype(jnp.float32)[:, None]
    live_blocks = jnp.minimum(lax.axis_index("ctx"), (length - 1) // rows) + 1
    gathered = (
        lax.all_gather(attn_gain, ("shard", "ctx"), axis=0, tiled=True),
        lax.all_gather(ffn_gain, ("shard", "ctx"), axis=0, tiled=True),
        lax.all_gather(w_query, ("shard", "ctx"), axis=0, tiled=True),
        lax.all_gather(w_key, ("shard", "ctx"), axis=0, tiled=True),
        lax.all_gather(w_value, ("shard", "ctx"), axis=0, tiled=True),
        lax.all_gather(w_gate, ("shard", "ctx"), axis=0, tiled=True),
        lax.all_gather(w_up, ("shard", "ctx"), axis=0, tiled=True),
        lax.all_gather(w_out, ("shard", "ctx"), axis=1, tiled=True),
        lax.all_gather(w_down, ("shard", "ctx"), axis=1, tiled=True),
    )
    gain_one = gathered[0].astype(jnp.float32)
    gain_two = gathered[1].astype(jnp.float32)
    full_query, full_key, full_value, full_gate, full_up, full_out, full_down = gathered[2:]
    q_gain = query_gain.astype(jnp.float32)
    k_gain = key_gain.astype(jnp.float32)
    hidden = hidden_in.astype(jnp.float32)
    normed_one = norm_rows(hidden, gain_one).astype(jnp.bfloat16)
    query_proj = forward_product(normed_one, full_query)
    key_proj = forward_product(normed_one, full_key)
    value_proj = forward_product(normed_one, full_value)
    queries = (
        head_prep(query_proj, q_gain, positions)
        .astype(jnp.bfloat16)
        .reshape(rows, kv_heads, group, head_dim)
    )
    keys_own = head_prep(key_proj, k_gain, positions).astype(jnp.bfloat16)
    values_own = value_proj.reshape(rows, kv_heads, head_dim).astype(jnp.bfloat16)
    keys_all, values_all = (
        lax.all_gather(keys_own, "ctx", axis=0, tiled=True),
        lax.all_gather(values_own, "ctx", axis=0, tiled=True),
    )
    key_blocks = keys_all.reshape(pieces, rows, kv_heads, head_dim)
    value_blocks = values_all.reshape(pieces, rows, kv_heads, head_dim)

    def key_at(index):
        return lax.dynamic_index_in_dim(key_blocks, index, 0, keepdims=False)

    def value_at(index):
        return lax.dynamic_index_in_dim(value_blocks, index, 0, keepdims=False)

    def block_scores(key_block, index):
        key_pos = index * rows + jnp.arange(rows, dtype=jnp.int32)
        mask = ((key_pos[None, :] <= positions[:, None]) & (key_pos[None, :] < length))[None, None]
        raw = (
            jnp.einsum("tkgd,skd->kgts", queries, key_block, preferred_element_type=jnp.float32)
            * scale
        )
        return (jnp.where(mask, raw, -1e30), mask)

    def stats_step(index, carry):
        top, total = carry
        masked, mask = block_scores(key_at(index), index)
        new_top = jnp.maximum(top, jnp.max(masked, axis=-1))
        weight = jnp.where(mask, jnp.exp(masked - new_top[..., None]), 0.0)
        total = total * jnp.exp(top - new_top) + jnp.sum(weight, axis=-1)
        return (new_top, total)

    start = (
        jnp.full((kv_heads, group, rows), -1e30, jnp.float32),
        jnp.zeros((kv_heads, group, rows), jnp.float32),
    )
    top, total = lax.fori_loop(0, live_blocks, stats_step, start)
    log_total = top + jnp.log(total)

    def probs_of(key_block, index):
        masked, mask = block_scores(key_block, index)
        return jnp.where(mask, jnp.exp(masked - log_total[..., None]), 0.0)

    def mix_step(index, accum):
        probs = probs_of(key_at(index), index).astype(jnp.bfloat16)
        return accum + jnp.einsum(
            "kgts,skd->tkgd", probs, value_at(index), preferred_element_type=jnp.float32
        )

    head_zeros = jnp.zeros((rows, kv_heads, group, head_dim), jnp.float32)
    mixed = lax.fori_loop(0, live_blocks, mix_step, head_zeros)
    heads_out = mixed.reshape(rows, -1).astype(jnp.bfloat16)
    attn_term = forward_product(heads_out, full_out)
    resid = hidden + lax.psum(attn_term, "tp")
    normed_two = norm_rows(resid, gain_two).astype(jnp.bfloat16)
    gate = forward_product(normed_two, full_gate)
    up = forward_product(normed_two, full_up)
    middle = activation(gate, up).astype(jnp.bfloat16)
    ffn_term = forward_product(middle, full_down)
    ffn = lax.psum(ffn_term.astype(jnp.bfloat16), "tp").astype(jnp.float32)
    block_out = (valid * (resid + ffn)).astype(jnp.bfloat16)
    grad_top = valid * out_grad.astype(jnp.float32)
    grad_low = grad_top.astype(jnp.bfloat16)
    down_wgrad = outer_product(middle, grad_low)
    mid_grad = back_product(grad_low, full_down)
    _, pull_act = jax.vjp(activation, gate, up)
    gate_float, up_float = pull_act(mid_grad)
    gate_low = gate_float.astype(jnp.bfloat16)
    up_low = up_float.astype(jnp.bfloat16)
    gate_wgrad = outer_product(normed_two, gate_low)
    up_wgrad = outer_product(normed_two, up_low)
    normed_two_part = back_product(gate_low, full_gate) + back_product(up_low, full_up)
    normed_two_grad = lax.psum(normed_two_part, "tp")
    _, pull_two = jax.vjp(norm_rows, resid, gain_two)
    resid_part, gain_two_grad = pull_two(normed_two_grad)
    resid_grad = grad_top + resid_part
    attn_low = resid_grad.astype(jnp.bfloat16)
    out_wgrad = outer_product(heads_out, attn_low)
    heads_grad = (
        back_product(attn_low, full_out)
        .astype(jnp.bfloat16)
        .reshape(rows, kv_heads, group, head_dim)
    )

    def delta_step(index, accum):
        probs = probs_of(key_at(index), index)
        prob_grad = jnp.einsum(
            "tkgd,skd->kgts", heads_grad, value_at(index), preferred_element_type=jnp.float32
        )
        return accum + jnp.sum(probs * prob_grad, axis=-1)

    delta = lax.fori_loop(
        0, live_blocks, delta_step, jnp.zeros((kv_heads, group, rows), jnp.float32)
    )

    def grad_step(index, carry):
        accum, key_store, value_store = carry
        key_block = key_at(index)
        probs = probs_of(key_block, index)
        prob_grad = jnp.einsum(
            "tkgd,skd->kgts", heads_grad, value_at(index), preferred_element_type=jnp.float32
        )
        score_grad = (probs * (prob_grad - delta[..., None])).astype(jnp.bfloat16)
        accum = (
            accum
            + jnp.einsum(
                "kgts,skd->tkgd", score_grad, key_block, preferred_element_type=jnp.float32
            )
            * scale
        )
        key_grad = (
            jnp.einsum("kgts,tkgd->skd", score_grad, queries, preferred_element_type=jnp.float32)
            * scale
        )
        value_grad = jnp.einsum(
            "kgts,tkgd->skd",
            probs.astype(jnp.bfloat16),
            heads_grad,
            preferred_element_type=jnp.float32,
        )
        key_store = lax.dynamic_update_index_in_dim(key_store, key_grad, index, 0)
        value_store = lax.dynamic_update_index_in_dim(value_store, value_grad, index, 0)
        return (accum, key_store, value_store)

    store_zeros = jnp.zeros((pieces, rows, kv_heads, head_dim), jnp.float32)
    query_grad, key_grads, value_grads = lax.fori_loop(
        0, live_blocks, grad_step, (head_zeros, store_zeros, store_zeros)
    )
    key_grad_own, value_grad_own = (
        lax.psum_scatter(
            key_grads.reshape(pieces * rows, kv_heads, head_dim),
            "ctx",
            scatter_dimension=0,
            tiled=True,
        ),
        lax.psum_scatter(
            value_grads.reshape(pieces * rows, kv_heads, head_dim),
            "ctx",
            scatter_dimension=0,
            tiled=True,
        ),
    )

    def query_prep(proj, gain):
        return head_prep(proj, gain, positions)

    _, pull_query = jax.vjp(query_prep, query_proj, q_gain)
    query_proj_grad, q_gain_grad = pull_query(query_grad.reshape(rows, q_heads, head_dim))
    _, pull_key = jax.vjp(query_prep, key_proj, k_gain)
    key_proj_grad, k_gain_grad = pull_key(key_grad_own)
    query_low = query_proj_grad.astype(jnp.bfloat16)
    key_low = key_proj_grad.astype(jnp.bfloat16)
    value_low = value_grad_own.reshape(rows, -1).astype(jnp.bfloat16)
    query_wgrad = outer_product(normed_one, query_low)
    key_wgrad = outer_product(normed_one, key_low)
    value_wgrad = outer_product(normed_one, value_low)
    normed_one_part = (
        back_product(query_low, full_query)
        + back_product(key_low, full_key)
        + back_product(value_low, full_value)
    )
    normed_one_grad = lax.psum(normed_one_part, "tp")
    _, pull_one = jax.vjp(norm_rows, hidden, gain_one)
    hidden_part, gain_one_grad = pull_one(normed_one_grad)
    input_grad = resid_grad + hidden_part
    head_sums = lax.psum((q_gain_grad, k_gain_grad), ("shard", "ctx", "tp"))
    summed = (
        lax.psum_scatter(gain_one_grad, ("shard", "ctx"), scatter_dimension=0, tiled=True),
        lax.psum_scatter(gain_two_grad, ("shard", "ctx"), scatter_dimension=0, tiled=True),
        lax.psum_scatter(query_wgrad, ("shard", "ctx"), scatter_dimension=0, tiled=True),
        lax.psum_scatter(key_wgrad, ("shard", "ctx"), scatter_dimension=0, tiled=True),
        lax.psum_scatter(value_wgrad, ("shard", "ctx"), scatter_dimension=0, tiled=True),
        lax.psum_scatter(gate_wgrad, ("shard", "ctx"), scatter_dimension=0, tiled=True),
        lax.psum_scatter(up_wgrad, ("shard", "ctx"), scatter_dimension=0, tiled=True),
        lax.psum_scatter(out_wgrad, ("shard", "ctx"), scatter_dimension=1, tiled=True),
        lax.psum_scatter(down_wgrad, ("shard", "ctx"), scatter_dimension=1, tiled=True),
    )
    (
        gain_one_out,
        gain_two_out,
        query_out,
        key_out,
        value_out,
        gate_out,
        up_out,
        out_out,
        down_out,
    ) = summed
    return (
        block_out,
        input_grad,
        gain_one_out,
        gain_two_out,
        head_sums[0],
        head_sums[1],
        query_out,
        key_out,
        value_out,
        out_out,
        gate_out,
        up_out,
        down_out,
    )


def solution(mesh):
    placed = (
        P(("shard", "ctx"), None),
        P("shard"),
        P(("shard", "ctx")),
        P(("shard", "ctx")),
        P(),
        P(),
        P(("shard", "ctx"), "tp"),
        P(("shard", "ctx"), "tp"),
        P(("shard", "ctx"), "tp"),
        P("tp", ("shard", "ctx")),
        P(("shard", "ctx"), "tp"),
        P(("shard", "ctx"), "tp"),
        P("tp", ("shard", "ctx")),
        P(("shard", "ctx"), None),
    )
    return jax.shard_map(
        body,
        mesh=mesh,
        in_specs=placed,
        out_specs=(
            P(("shard", "ctx"), None),
            P(("shard", "ctx"), None),
            P(("shard", "ctx")),
            P(("shard", "ctx")),
            P(),
            P(),
            P(("shard", "ctx"), "tp"),
            P(("shard", "ctx"), "tp"),
            P(("shard", "ctx"), "tp"),
            P("tp", ("shard", "ctx")),
            P(("shard", "ctx"), "tp"),
            P(("shard", "ctx"), "tp"),
            P("tp", ("shard", "ctx")),
        ),
        check_vma=False,
    )
```

profile of v0, /device:TPU:0, one launch (start us, length us, event | category | flops | bytes accessed | tf_op | source)
XLA Modules:
  0.0 1544.9 jit_solution(17164770383775556939)
XLA Ops:
  13.1 15.7 %all-reduce.10 = (bf16[1536]{0:T(1024)(128)(2,1)S(1)}, bf16[1536]{0:T(1024)(128)(2,1)S(1)}) all-reduce(bf16[1536]{0:T(1024)(128)(2,1)S(1)} %dynamic-update-slice, bf16[1536]{0:T(1024)(128)(2,1)S(1)} %dynamic-update-slice.1), channel_id=1, replica_groups=mesh['shard'=4,'ctx'=2,'tp'=4] {'shard','ctx'}, use_global_device_ids=true, to_apply=%add.4 | all-reduce | flops 3072 | bytes 12288
  31.9 15.8 %all_gather.34 = bf16[1536,128]{1,0:T(8,128)(2,1)S(1)} all-gather(bf16[192,128]{1,0:T(8,128)(2,1)} %param.30), channel_id=1, replica_groups=mesh['shard'=4,'ctx'=2,'tp'=4] {'shard','ctx'}, dimensions={0}, use_global_device_ids=true | all-gather | bytes 442368 | tf_op jit(solution)/shard_map/all_gather | solution.py:87
  51.0 9.5 all_gather.35
  61.3 16.4 %all_gather.36 = bf16[1536,128]{1,0:T(8,128)(2,1)S(1)} all-gather(bf16[192,128]{1,0:T(8,128)(2,1)S(1)} %copy-done.40), channel_id=1, replica_groups=mesh['shard'=4,'ctx'=2,'tp'=4] {'shard','ctx'}, dimensions={0}, use_global_device_ids=true | all-gather | bytes 442368 | tf_op jit(solution)/shard_map/all_gather | solution.py:86
  91.9 16.3 %while.50 = (s32[]{:T(128)}, f32[2,3,768]{2,1,0:T(4,128)S(1)}, f32[2,3,768]{2,1,0:T(4,128)S(1)}, s32[]{:T(128)}, s32[]{:T(128)}, /*index=5*/bf16[2,768,2,64]{1,3...) while((s32[]{:T(128)}, f32[2,3,768]{2,1,0:T(4,128)S(1)}, ...), condition=%wide.region_6.7_spmd.clone, body=%wide.region_3.6_spmd.clone.sunk | while | flops 482488320 | bytes 31121088 | solution.py:144
  123.4 194.2 %all-reduce.16.cloned.1.call-done = f32[768,1536]{1,0:T(8,128)} async-done(((f32[768,1536]{1,0:T(8,128)}), f32[768,1536]{1,0:T(8,128)}) %all-reduce.16.cloned.1.call-update) | async-done | bytes 4718608 | tf_op jit(solution)/shard_map/psum | solution.py:161
  323.3 37.3 %all-gather.10.cloned.1.call-done = bf16[1536,1728]{1,0:T(8,128)(2,1)} async-done(((bf16[192,1728]{1,0:T(8,128)(2,1)}), bf16[1536,1728]{1,0:T(8,128)(2,1)}) %all-gather.10.cloned.1.call-update) | async-done | bytes 5308432 | tf_op jit(solution)/shard_map/all_gather | solution.py:88
  360.6 9.3 fusion.111
  369.8 34.7 %all-gather.12.cloned.1.call-done = bf16[1536,1728]{1,0:T(8,128)(2,1)} async-done(((bf16[192,1728]{1,0:T(8,128)(2,1)}), bf16[1536,1728]{1,0:T(8,128)(2,1)}) %all-gather.12.cloned.1.call-update) | async-done | bytes 5308432 | tf_op jit(solution)/shard_map/all_gather | solution.py:89
  404.5 10.0 fusion.112
  414.6 33.9 %all-gather.14.cloned.1.call-done = bf16[1728,1536]{0,1:T(8,128)(2,1)} async-done(((bf16[1728,192]{0,1:T(8,128)(2,1)}), bf16[1728,1536]{0,1:T(8,128)(2,1)}) %all-gather.14.cloned.1.call-update) | async-done | bytes 5308432 | tf_op jit(solution)/shard_map/all_gather | solution.py:91
  448.5 14.1 multiply_convert_fusion
  462.6 8.5 fusion.113
  478.0 9.3 convolution_convert_fusion
  487.4 162.3 %all-reduce.20.cloned.1.call-done = f32[768,1536]{1,0:T(8,128)} async-done(((f32[768,1536]{1,0:T(8,128)}), f32[768,1536]{1,0:T(8,128)}) %all-reduce.20.cloned.1.call-update) | async-done | bytes 4718608 | tf_op jit(solution)/shard_map/psum | solution.py:180
  655.1 92.1 %all-reduce.18.cloned.1.call-done = bf16[768,1536]{1,0:T(8,128)(2,1)} async-done(((bf16[768,1536]{1,0:T(8,128)(2,1)}), bf16[768,1536]{1,0:T(8,128)(2,1)}) %all-reduce.18.cloned.1.call-update) | async-done | bytes 2359312 | tf_op jit(solution)/shard_map/psum | solution.py:167
  757.9 17.2 %while.52 = (s32[]{:T(128)}, f32[2,3,768]{2,1,0:T(4,128)S(1)}, s32[]{:T(128)}, s32[]{:T(128)}, bf16[2,768,2,64]{1,3,2,0:T(8,128)(2,1)S(1)}, /*index=5*/bf16[768,...) while((s32[]{:T(128)}, f32[2,3,768]{2,1,0:T(4,128)S(1)}, ...), condition=%wide.region_16.17_spmd.clone, body=%wide.region_14.16_spmd.clone.sunk | while | flops 928386048 | bytes 31176404 | solution.py:199
  777.4 44.5 %while.53 = (s32[]{:T(128)}, f32[768,2,3,64]{0,3,2,1:T(8,128)S(1)}, f32[2,768,2,64]{1,0,3,2:T(2,128)}, f32[2,768,2,64]{1,0,3,2:T(2,128)}, s32[]{:T(128)}, /*inde...) while((s32[]{:T(128)}, f32[768,2,3,64]{0,3,2,1:T(8,128)S(1)}, ...), condition=%wide.region_18.19_spmd.clone, body=%wide.region_17.18_spmd.clone.sunk | while | flops 2309262336 | bytes 77213488 | solution.py:233
  833.8 69.2 %reduce-scatter.10.cloned.1.call-done = f32[768,2,64]{0,2,1:T(8,128)} async-done(((f32[1536,2,64]{0,2,1:T(8,128)}), f32[768,2,64]{0,2,1:T(8,128)}) %reduce-scatter.10.cloned.1.call-update) | async-done | bytes 393232 | tf_op jit(solution)/shard_map/reduce_scatter | solution.py:237
  907.4 15.8 %reduce-scatter.12.cloned.1.call-done = f32[768,2,64]{0,2,1:T(8,128)} async-done(((f32[1536,2,64]{0,2,1:T(8,128)}), f32[768,2,64]{0,2,1:T(8,128)}) %reduce-scatter.12.cloned.1.call-update) | async-done | bytes 393232 | tf_op jit(solution)/shard_map/reduce_scatter | solution.py:243
  944.6 8.9 fusion.119
  953.8 8.9 fusion.120
  964.4 9.0 fusion.96
  974.3 47.0 %all-reduce.8 = (f32[64]{0:T(128)}, f32[64]{0:T(128)}) all-reduce(f32[64]{0:T(128)S(1)} %get-tuple-element.424, f32[64]{0:T(128)S(1)} %get-tuple-element.426), channel_id=1, replica_groups=mesh['shard'=4,'ctx'=2,'tp'=4] {'shard','ctx','tp'}, use_global_device_ids=true, to_apply=%region_30.31 | all-reduce | flops 128 | bytes 1024 | tf_op jit(solution)/shard_map/psum | solution.py:273
  1021.2 82.8 %all-reduce.22.cloned.1.call-done = f32[768,1536]{1,0:T(8,128)} async-done(((f32[768,1536]{1,0:T(8,128)}), f32[768,1536]{1,0:T(8,128)}) %all-reduce.22.cloned.1.call-update) | async-done | bytes 4718608 | tf_op jit(solution)/shard_map/psum | solution.py:269
  1107.9 24.3 %all-reduce.9 = (f32[1536]{0:T(1024)S(1)}, f32[1536]{0:T(1024)S(1)}) all-reduce(f32[1536]{0:T(1024)S(1)} %get-tuple-element.422, f32[1536]{0:T(1024)S(1)} %copy-done.43), channel_id=4, replica_groups=mesh['shard'=4,'ctx'=2,'tp'=4] {'shard','ctx'}, use_global_device_ids=true, to_apply=%region_26.27.clone | all-reduce | flops 3072 | bytes 24576
  1141.7 38.7 %reduce-scatter.18.cloned.1.call-done = f32[192,128]{1,0:T(8,128)} async-done(((f32[1536,128]{1,0:T(8,128)}), f32[192,128]{1,0:T(8,128)}) %reduce-scatter.18.cloned.1.call-update) | async-done | bytes 98320 | tf_op jit(solution)/shard_map/reduce_scatter | solution.py:279
  1180.5 46.3 %reduce-scatter.14.cloned.1.call-done = f32[192,384]{1,0:T(8,128)} async-done(((f32[1536,384]{1,0:T(8,128)}), f32[192,384]{1,0:T(8,128)}) %reduce-scatter.14.cloned.1.call-update) | async-done | bytes 294928 | tf_op jit(solution)/shard_map/reduce_scatter | solution.py:277
  1226.8 46.7 %reduce-scatter.20.cloned.1.call-done = f32[384,192]{0,1:T(8,128)} async-done(((f32[384,1536]{0,1:T(8,128)}), f32[384,192]{0,1:T(8,128)}) %reduce-scatter.20.cloned.1.call-update) | async-done | bytes 294928 | tf_op jit(solution)/shard_map/reduce_scatter | solution.py:282
  1273.4 88.1 %reduce-scatter.22.cloned.1.call-done = f32[192,1728]{1,0:T(8,128)} async-done(((f32[1536,1728]{1,0:T(8,128)}), f32[192,1728]{1,0:T(8,128)}) %reduce-scatter.22.cloned.1.call-update) | async-done | bytes 1327120 | tf_op jit(solution)/shard_map/reduce_scatter | solution.py:280
  1361.5 88.0 %reduce-scatter.24.cloned.1.call-done = f32[192,1728]{1,0:T(8,128)} async-done(((f32[1536,1728]{1,0:T(8,128)}), f32[192,1728]{1,0:T(8,128)}) %reduce-scatter.24.cloned.1.call-update) | async-done | bytes 1327120 | tf_op jit(solution)/shard_map/reduce_scatter | solution.py:281
  1449.6 88.1 %reduce-scatter.26.cloned.1.call-done = f32[1728,192]{0,1:T(8,128)} async-done(((f32[1728,1536]{0,1:T(8,128)}), f32[1728,192]{0,1:T(8,128)}) %reduce-scatter.26.cloned.1.call-update) | async-done | bytes 1327120 | tf_op jit(solution)/shard_map/reduce_scatter | solution.py:283
  (256 shorter events, 208.5 us)
Async XLA Ops:
  7.2 80.3 %all-gather.6.cloned.1.call-start = ((), (), s32[]{:S(2)}) async-start(), calls=%async_computation.9 | async-start | bytes 1327104 | tf_op jit(solution)/shard_map/all_gather | solution.py:85
  7.9 107.9 %all-gather.8.cloned.1.call-start = ((), (), s32[]{:S(2)}) async-start(), calls=%async_computation.10 | async-start | bytes 1327104 | tf_op jit(solution)/shard_map/all_gather | solution.py:90
  8.7 308.9 %all-reduce.16.cloned.1.call-start = ((), (), s32[]{:S(2)}) async-start(), calls=%async_computation.11 | async-start | bytes 9437184 | tf_op jit(solution)/shard_map/psum | solution.py:161
  121.5 196.1 %copy-start.4 = (bf16[768,1536]{1,0:T(8,128)(2,1)S(1)}, bf16[768,1536]{1,0:T(8,128)(2,1)}, u32[]{:S(2)}) copy-start(bf16[768,1536]{1,0:T(8,128)(2,1)} %param.22) | copy-start | bytes 7077892
  121.6 239.0 %all-gather.10.cloned.1.call-start = ((), (), s32[]{:S(2)}) async-start(), calls=%async_computation.12 | async-start | bytes 6193152 | tf_op jit(solution)/shard_map/all_gather | solution.py:88
  122.1 282.4 %all-gather.12.cloned.1.call-start = ((), (), s32[]{:S(2)}) async-start(), calls=%async_computation.13 | async-start | bytes 6193152 | tf_op jit(solution)/shard_map/all_gather | solution.py:89
  122.7 325.8 %all-gather.14.cloned.1.call-start = ((), (), s32[]{:S(2)}) async-start(), calls=%async_computation.14 | async-start | bytes 6193152 | tf_op jit(solution)/shard_map/all_gather | solution.py:91
  123.3 526.3 %all-reduce.20.cloned.1.call-start = ((), (), s32[]{:S(2)}) async-start(), calls=%async_computation.16 | async-start | bytes 9437184 | tf_op jit(solution)/shard_map/psum | solution.py:180
  123.4 623.9 %copy-start.46 = (f32[768]{0:T(1024)}, f32[768]{0:T(1024)S(1)}, u32[]{:S(2)}) copy-start(f32[768]{0:T(1024)S(1)} %fusion.104) | copy-start | bytes 9220
  369.8 78.7 %copy-start.24 = (bf16[768,1536]{1,0:T(8,128)(2,1)S(1)}, bf16[768,1536]{1,0:T(8,128)(2,1)}, u32[]{:S(2)}) copy-start(bf16[768,1536]{1,0:T(8,128)(2,1)} %param.35) | copy-start | bytes 7077892
  477.5 269.7 %all-reduce.18.cloned.1.call-start = ((), (), s32[]{:S(2)}) async-start(), calls=%async_computation.15 | async-start | bytes 4718592 | tf_op jit(solution)/shard_map/psum | solution.py:167
  487.3 415.7 %reduce-scatter.10.cloned.1.call-start = ((), (), s32[]{:S(2)}) async-start(), calls=%async_computation.17 | async-start | bytes 1179648 | tf_op jit(solution)/shard_map/reduce_scatter | solution.py:237
  655.1 101.6 %copy-start.13 = (bf16[384,1536]{0,1:T(8,128)(2,1)S(1)}, bf16[384,1536]{0,1:T(8,128)(2,1)}, u32[]{:S(2)}) copy-start(bf16[384,1536]{0,1:T(8,128)(2,1)} %all-gather.8.cloned.1.call-done) | copy-start | bytes 3538948
  824.8 98.4 %reduce-scatter.12.cloned.1.call-start = ((), (), s32[]{:S(2)}) async-start(), calls=%async_computation.18 | async-start | bytes 1179648 | tf_op jit(solution)/shard_map/reduce_scatter | solution.py:243
  828.7 75.4 %copy-start.10 = (f32[768,128]{0,1:T(8,128)S(1)}, f32[768,128]{0,1:T(8,128)}, u32[]{:S(2)}) copy-start(f32[768,128]{0,1:T(8,128)} %copy-done.9) | copy-start | bytes 1179652
  828.7 75.4 %copy-start.35 = (f32[768,2]{0,1:T(2,128)S(1)}, f32[768,2]{0,1:T(2,128)}, u32[]{:S(2)}) copy-start(f32[768,2]{0,1:T(2,128)} %copy-done.34) | copy-start | bytes 18436
  828.8 275.3 %all-reduce.22.cloned.1.call-start = ((), (), s32[]{:S(2)}) async-start(), calls=%async_computation.19 | async-start | bytes 9437184 | tf_op jit(solution)/shard_map/psum | solution.py:269
  828.8 75.5 %copy-start.39 = (f32[768,2]{0,1:T(2,128)S(1)}, f32[768,2]{0,1:T(2,128)}, u32[]{:S(2)}) copy-start(f32[768,2]{0,1:T(2,128)} %copy-done.38) | copy-start | bytes 18436
  828.8 75.6 %copy-start.17 = (bf16[1536,128]{1,0:T(8,128)(2,1)S(1)}, bf16[1536,128]{1,0:T(8,128)(2,1)}, u32[]{:S(2)}) copy-start(bf16[1536,128]{1,0:T(8,128)(2,1)} %copy-done.16) | copy-start | bytes 1179652
  833.8 90.5 %copy-start.15 = (bf16[1536,128]{1,0:T(8,128)(2,1)S(1)}, bf16[1536,128]{1,0:T(8,128)(2,1)}, u32[]{:S(2)}) copy-start(bf16[1536,128]{1,0:T(8,128)(2,1)} %copy-done.14) | copy-start | bytes 1179652
  931.0 210.7 %reduce-scatter.16.cloned.1.call-start = ((), (), s32[]{:S(2)}) async-start(), calls=%async_computation.21 | async-start | bytes 884736 | tf_op jit(solution)/shard_map/reduce_scatter | solution.py:278
  934.4 246.1 %reduce-scatter.18.cloned.1.call-start = ((), (), s32[]{:S(2)}) async-start(), calls=%async_computation.22 | async-start | bytes 884736 | tf_op jit(solution)/shard_map/reduce_scatter | solution.py:279
  936.1 290.6 %reduce-scatter.14.cloned.1.call-start = ((), (), s32[]{:S(2)}) async-start(), calls=%async_computation.20 | async-start | bytes 2654208 | tf_op jit(solution)/shard_map/reduce_scatter | solution.py:277
  939.1 334.3 %reduce-scatter.20.cloned.1.call-start = ((), (), s32[]{:S(2)}) async-start(), calls=%async_computation.23 | async-start | bytes 2654208 | tf_op jit(solution)/shard_map/reduce_scatter | solution.py:282
  944.5 417.0 %reduce-scatter.22.cloned.1.call-start = ((), (), s32[]{:S(2)}) async-start(), calls=%async_computation.24 | async-start | bytes 12386304 | tf_op jit(solution)/shard_map/reduce_scatter | solution.py:280
  953.5 496.0 %reduce-scatter.24.cloned.1.call-start = ((), (), s32[]{:S(2)}) async-start(), calls=%async_computation.25 | async-start | bytes 12386304 | tf_op jit(solution)/shard_map/reduce_scatter | solution.py:281
  962.8 574.8 %reduce-scatter.26.cloned.1.call-start = ((), (), s32[]{:S(2)}) async-start(), calls=%async_computation.26 | async-start | bytes 12386304 | tf_op jit(solution)/shard_map/reduce_scatter | solution.py:283
  973.4 130.7 %copy-start.5 = (bf16[768,1536]{1,0:T(8,128)(2,1)S(1)}, bf16[768,1536]{1,0:T(8,128)(2,1)}, u32[]{:S(2)}) copy-start(bf16[768,1536]{1,0:T(8,128)(2,1)} %param.22) | copy-start | bytes 7077892
  973.4 130.7 %copy-start.33 = (f32[1536]{0:T(1024)S(1)}, f32[1536]{0:T(1024)}, u32[]{:S(2)}) copy-start(f32[1536]{0:T(1024)} %copy-done.32) | copy-start | bytes 18436
  973.4 130.7 %copy-start.37 = (f32[768]{0:T(1024)S(1)}, f32[768]{0:T(1024)}, u32[]{:S(2)}) copy-start(f32[768]{0:T(1024)} %copy-done.36) | copy-start | bytes 9220
  973.5 134.4 %copy-start.43 = (f32[1536]{0:T(1024)S(1)}, f32[1536]{0:T(1024)}, u32[]{:S(2)}) copy-start(f32[1536]{0:T(1024)} %get-tuple-element.420) | copy-start | bytes 18436
  973.5 159.9 %copy-start.42 = (f32[768]{0:T(1024)S(1)}, f32[768]{0:T(1024)}, u32[]{:S(2)}) copy-start(f32[768]{0:T(1024)} %copy-done.41) | copy-start | bytes 9220
  (43 other events, 749.0 us)
Sparse Core Ops, SparseCore 0:
  9.9 26.8 all-gather.5
  38.7 25.4 all-gather.7
  121.7 195.8 all-reduce.15
  319.3 41.2 all-gather.9
  362.3 42.2 all-gather.11
  406.3 42.2 all-gather.13
  477.7 171.9 all-reduce.19
  652.6 94.6 all-reduce.17
  825.0 78.0 reduce-scatter.9
  905.8 17.4 reduce-scatter.11
  931.1 172.9 all-reduce.21
  1107.7 34.0 reduce-scatter.15
  1145.4 34.9 reduce-scatter.17
  1184.3 42.4 reduce-scatter.13
  1230.9 42.4 reduce-scatter.19
  1277.5 83.9 reduce-scatter.21
  1365.5 83.9 reduce-scatter.23
  1453.6 83.9 reduce-scatter.25
where the time goes:
time: 1550 us; the launch traced here: 1540 us
  waiting for transfers between devices  1120 us (72%)
  matrix products  176 us (11%)
  blocking collectives  136 us (9%)
  other arithmetic  49.3 us (3%)
  local copies, waits for them, and re-layouts  40.4 us (3%)
  between operations  17.7 us (1%)
    psum x1, waiting for transfers between devices, body(): resid = hidden + lax.psum(attn_term, 'tp')  194 us
    psum x1, waiting for transfers between devices, body(): normed_two_grad = lax.psum(normed_two_part, 'tp')  162 us
    psum x1, waiting for transfers between devices, body(): ffn = lax.psum(ffn_term.astype(jnp.bfloat16), 'tp').astype(jnp.float32)  92.1 us
    reduce_scatter x1, waiting for transfers between devices, body(): lax.psum_scatter(gate_wgrad, ('shard', 'ctx'), scatter_dimension=0, tiled...  88.1 us
    reduce_scatter x1, waiting for transfers between devices, body(): lax.psum_scatter(down_wgrad, ('shard', 'ctx'), scatter_dimension=1, tiled...  88.1 us
    reduce_scatter x1, waiting for transfers between devices, body(): lax.psum_scatter(up_wgrad, ('shard', 'ctx'), scatter_dimension=0, tiled=T...  88 us
    psum x1, waiting for transfers between devices, body(): normed_one_grad = lax.psum(normed_one_part, 'tp')  82.8 us
    reduce_scatter x1, waiting for transfers between devices, body(): lax.psum_scatter(key_grads.reshape(pieces * rows, kv_heads, head_dim), 'c...  69.2 us
  transfers between devices with their start and end apart: 18, of which 16 were waited for; matrix products, arithmetic and copies ran while one was open for 9% of the time, Pallas kernels for 0%

commit v1 on v0

--- a/solution.py
+++ b/solution.py
@@ -1,12 +1,20 @@
+import functools
 import math
 
 import jax
 import jax.numpy as jnp
+import numpy as np
 from jax import lax
+from jax.experimental import pallas as pl
+from jax.experimental.pallas import tpu as pltpu
 from jax.sharding import PartitionSpec as P
 
 EPSILON = 1e-05
 ROPE_BASE = 1000000.0
+MESH = pl.DeviceIdType.MESH
+F32 = jnp.float32
+BF16 = jnp.bfloat16
+VMEM_LIMIT = 60 << 20
 
 
 def norm_rows(value, gain):
@@ -310,7 +318,611 @@
     )
 
 
+def remote(src, dst, send, recv, dev):
+    return pltpu.make_async_remote_copy(
+        src_ref=src,
+        dst_ref=dst,
+        send_sem=send,
+        recv_sem=recv,
+        device_id=dev,
+        device_id_type=MESH,
+    )
+
+
+def mm(a, b):
+    return jnp.dot(a, b, preferred_element_type=F32)
+
+
+def mm_nt(a, b):
+    return lax.dot_general(a, b, (((1,), (1,)), ((), ())), preferred_element_type=F32)
+
+
+class Place:
+    def __init__(self, n_shard, n_tp):
+        s = lax.axis_index("shard")
+        c = lax.axis_index("ctx")
+        t = lax.axis_index("tp")
+        self.s, self.c, self.t = s, c, t
+        self.core = lax.rem(s, 2)
+        sib = s + 1 - 2 * self.core
+        far = lax.rem(s + 2, n_shard)
+        far_sib = far + 1 - 2 * self.core
+        self.sib = (sib, c, t)
+        self.x = (s, 1 - c, t)
+        self.y = (far, c, t)
+        first = 1 - self.core
+        self.relay = (
+            first * s + self.core * far,
+            first * (1 - c) + self.core * c,
+            t,
+        )
+        slot = lambda a, b: a * 2 + b
+        self.own = slot(s, c)
+        self.slots = {
+            "S": slot(sib, c),
+            "X": slot(s, 1 - c),
+            "Y": slot(far, c),
+            "D": slot(far, 1 - c),
+            "SX": slot(sib, 1 - c),
+            "SY": slot(far_sib, c),
+            "SD": slot(far_sib, 1 - c),
+        }
+        self.relayed = first * self.slots["Y"] + self.core * self.slots["X"]
+        self.n_tp = n_tp
+
+    def z(self, t):
+        return (self.s, self.c, t)
+
+    def greet(self):
+        peers = [self.sib, self.x, self.y]
+        peers += [
+            self.z(lax.rem(self.t + d, self.n_tp)) for d in range(1, self.n_tp)
+        ]
+        barrier = pltpu.get_barrier_semaphore()
+        for peer in peers:
+            pl.semaphore_signal(barrier, inc=1, device_id=peer, device_id_type=MESH)
+        pl.semaphore_wait(barrier, len(peers))
+
+
+ROLES = ("S", "X", "Y", "D", "SX", "SY", "SD")
+
+
+class Gather:
+    def __init__(self, at, own, full, send, recv, index):
+        self.at, self.own, self.full = at, own, full
+        self.send, self.recv, self.index = send, recv, index
+        self.rows = own.shape[0]
+
+    def block(self, slot):
+        return self.full.at[pl.ds(pl.multiple_of(slot * self.rows, self.rows), self.rows)]
+
+    def copy(self, role, src, slot, dev):
+        k = ROLES.index(role)
+        return remote(
+            src,
+            self.block(slot),
+            self.send.at[self.index, k],
+            self.recv.at[self.index, k],
+            dev,
+        )
+
+    def arrived(self, role):
+        slot = self.at.slots[role]
+        self.copy(role, self.block(slot), slot, self.at.sib).wait_recv()
+
+    def start_x(self):
+        self.copy("X", self.own, self.at.own, self.at.x).start()
+
+    def start_y(self):
+        self.copy("Y", self.own, self.at.own, self.at.y).start()
+
+    def start_s(self):
+        self.copy("S", self.own, self.at.own, self.at.sib).start()
+
+    def start(self):
+        self.start_x()
+        self.start_y()
+        self.start_s()
+
+    def relay(self):
+        at = self.at
+        self.arrived("X")
+        self.arrived("Y")
+        self.copy("D", self.block(at.relayed), at.relayed, at.relay).start()
+        for role in ("X", "Y"):
+            slot = at.slots[role]
+            self.copy("S" + role, self.block(slot), slot, at.sib).start()
+
+    def relay_last(self):
+        self.arrived("D")
+        slot = self.at.slots["D"]
+        self.copy("SD", self.block(slot), slot, self.at.sib).start()
+
+    def finish(self):
+        for role in ("S", "SX", "SY", "SD"):
+            self.arrived(role)
+        for role in ROLES:
+            self.copy(role, self.own, self.at.own, self.at.sib).wait_send()
+
+
+def column(row_ref, n):
+    wide = jnp.broadcast_to(row_ref[...].astype(F32), (8, n))
+    return wide.T[:, 0:1]
+
+
+def kernel_a(
+    shape,
+    length_ref,
+    hid_ref,
+    gain_one_ref,
+    gain_two_ref,
+    q_gain_ref,
+    k_gain_ref,
+    wq_ref,
+    wk_ref,
+    wv_ref,
+    wo_ref,
+    wg_ref,
+    wu_ref,
+    wd_ref,
+    cos_ref,
+    sin_ref,
+    wqkv_full,
+    wo_full,
+    wg_full,
+    wu_full,
+    wd_full,
+    heads_all,
+    q_t,
+    kv_all,
+    inv_den,
+    proj_t,
+    s_qkv,
+    s_woz,
+    s_wg,
+    s_wu,
+    h1,
+    k_own,
+    k_off,
+    v_own,
+    v_off,
+    acc,
+    g_send,
+    g_recv,
+    z_send,
+    z_recv,
+    h_send,
+    h_recv,
+    kv_sem,
+    loc_sem,
+):
+    n_shard, n_tp, hd = shape
+    at = Place(n_shard, n_tp)
+    c, t = at.c, at.t
+    rows, width = hid_ref.shape
+    q_cols, kv_cols = wq_ref.shape[1], wk_ref.shape[1]
+    q_heads, kv_heads = q_cols // hd, kv_cols // hd
+    group = q_heads // kv_heads
+    half = hd // 2
+    at.greet()
+
+    col_one = column(gain_one_ref, gain_one_ref.shape[1])
+    s_qkv[:, 0:q_cols] = (wq_ref[...].astype(F32) * col_one).astype(BF16)
+    s_qkv[:, q_cols : q_cols + kv_cols] = (wk_ref[...].astype(F32) * col_one).astype(BF16)
+    s_qkv[:, q_cols + kv_cols :] = (wv_ref[...].astype(F32) * col_one).astype(BF16)
+    qkv = Gather(at, s_qkv, wqkv_full, g_send, g_recv, 0)
+    out = Gather(at, s_woz, wo_full, g_send, g_recv, 1)
+    gate = Gather(at, s_wg, wg_full, g_send, g_recv, 2)
+    up = Gather(at, s_wu, wu_full, g_send, g_recv, 3)
+    down = Gather(at, wd_ref, wd_full, g_send, g_recv, 4)
+    gathers = (qkv, out, gate, up, down)
+    local = [
+        pltpu.make_async_copy(g.own, g.block(at.own), loc_sem.at[i])
+        for i, g in enumerate(gathers)
+    ]
+    qkv.start()
+    local[0].start()
+
+    wo_cols = pl.ds(pl.multiple_of(t * q_cols, q_cols), q_cols)
+    s_woz[:, wo_cols] = wo_ref[...]
+
+    def wo_part(d, owner):
+        cols = pl.ds(pl.multiple_of(owner * q_cols, q_cols), q_cols)
+        return remote(
+            s_woz.at[:, cols],
+            s_woz.at[:, cols],
+            z_send.at[d],
+            z_recv.at[d],
+            at.z(lax.rem(t + d + 1, n_tp)),
+        )
+
+    for d in range(n_tp - 1):
+        wo_part(d, t).start()
+
+    def norm_one(i, _):
+        r = pl.ds(pl.multiple_of(i * 64, 64), 64)
+        x = hid_ref[r, :].astype(F32)
+        scale = lax.rsqrt(jnp.mean(x * x, axis=-1, keepdims=True) + EPSILON)
+        h1[r, :] = (x * scale).astype(BF16)
+        return 0
+
+    lax.fori_loop(0, rows // 64, norm_one, 0)
+    qkv.relay()
+    col_two = column(gain_two_ref, gain_two_ref.shape[1])
+    s_wg[...] = (wg_ref[...].astype(F32) * col_two).astype(BF16)
+    s_wu[...] = (wu_ref[...].astype(F32) * col_two).astype(BF16)
+    qkv.relay_last()
+    for d in range(n_tp - 1):
+        wo_part(d, lax.rem(t + n_tp - d - 1, n_tp)).wait_recv()
+    out.start_y()
+    out.start_s()
+    gate.start_y()
+    local[0].wait()
+    for cp in local[1:]:
+        cp.start()
+    qkv.finish()
+
+    def project(i, _):
+        r = pl.ds(pl.multiple_of(i * 256, 256), 256)
+        proj_t[:, r] = mm(h1[r, :], wqkv_full[...]).T
+        return 0
+
+    lax.fori_loop(0, rows // 256, project, 0)
+    here = pl.ds(pl.multiple_of(c * rows, rows), rows)
+    k_gain = column(k_gain_ref, hd)
+    q_gain = column(q_gain_ref, hd)
+
+    def prepared(row, gain, factor):
+        x = proj_t[pl.ds(pl.multiple_of(row, hd), hd), :]
+        scale = lax.rsqrt(jnp.mean(x * x, axis=0, keepdims=True) + EPSILON)
+        y = x * (scale * factor) * gain
+        a, b = y[:half], y[half:]
+        cosine, sine = cos_ref[:, here], sin_ref[:, here]
+        return jnp.concatenate([a * cosine - b * sine, b * cosine + a * sine], axis=0)
+
+    for g in range(kv_heads):
+        key = prepared(q_cols + g * hd, k_gain, 1.0).astype(BF16)
+        kv_all[c, g * hd : (g + 1) * hd, :] = key
+    kv_all[c, kv_cols:, :] = proj_t[q_cols + kv_cols :, :].astype(BF16)
+    kv_copy = remote(kv_all.at[c], kv_all.at[c], kv_sem.at[0], kv_sem.at[1], at.x)
+    kv_back = remote(
+        kv_all.at[1 - c], kv_all.at[1 - c], kv_sem.at[0], kv_sem.at[1], at.x
+    )
+
+    @pl.when(c == 0)
+    def _():
+        kv_copy.start()
+
+    out.start_x()
+    gate.start_x()
+    gate.start_s()
+
+    def prep_q(h, _):
+        r = pl.multiple_of(h * hd, hd)
+        q_t[pl.ds(r, hd), :] = prepared(r, q_gain, 1.0 / math.sqrt(hd)).astype(BF16)
+        return 0
+
+    lax.fori_loop(0, q_heads, prep_q, 0)
+    length = length_ref[0]
+
+    def load_block(index, k_nat, v_ext):
+        pos = index * rows + lax.broadcasted_iota(jnp.int32, (1, rows), 1)
+        live = (pos < length).astype(F32)
+        first = (lax.broadcasted_iota(jnp.int32, (16, rows), 0) == 0).astype(F32)
+        for g in range(kv_heads):
+            k_nat[g] = kv_all[index, g * hd : (g + 1) * hd, :].astype(F32).T.astype(BF16)
+            v = kv_all[index, kv_cols + g * hd : kv_cols + (g + 1) * hd, :].astype(F32)
+            v_ext[g, 0:hd, :] = (v * live).astype(BF16)
+            v_ext[g, hd:, :] = (first * live).astype(BF16)
+
+    load_block(c, k_own, v_own)
+    below = lax.broadcasted_iota(jnp.int32, (256, 256), 0) <= lax.broadcasted_iota(
+        jnp.int32, (256, 256), 1
+    )
+
+    def own_block(h, _):
+        g = h // group
+        qh = q_t[pl.ds(pl.multiple_of(h * hd, hd), hd), :]
+        for i in range(rows // 256):
+            qi = qh[:, i * 256 : (i + 1) * 256]
+            top = i * 256
+            e = jnp.exp(mm(k_own[g, top : top + 256, :], qi))
+            e = jnp.where(below, e, 0.0).astype(BF16)
+            total = mm(v_own[g, :, top : top + 256], e)
+            if i:
+                e = jnp.exp(mm(k_own[g, 0:top, :], qi)).astype(BF16)
+                total += mm(v_own[g, :, 0:top], e)
+            acc[h, :, top : top + 256] = total
+        return 0
+
+    lax.fori_loop(0, q_heads, own_block, 0)
+
+    @pl.when(c == 1)
+    def _():
+        kv_back.wait_recv()
+        load_block(1 - c, k_off, v_off)
+
+        def other_block(h, _):
+            g = h // group
+            qh = q_t[pl.ds(pl.multiple_of(h * hd, hd), hd), :]
+            for i in range(rows // 256):
+                cols = slice(i * 256, (i + 1) * 256)
+                e = jnp.exp(mm(k_off[g], qh[:, cols])).astype(BF16)
+                acc[h, :, cols] += mm(v_off[g], e)
+            return 0
+
+        lax.fori_loop(0, q_heads, other_block, 0)
+
+    out.relay()
+    up.start()
+
+    def chunk_cols(owner, j):
+        return pl.ds(pl.multiple_of(owner * q_cols + j * 128, 128), 128)
+
+    def along(owner, j, way):
+        ref = heads_all.at[:, chunk_cols(owner, j)]
+        dev = at.z(jnp.minimum(t + 1, n_tp - 1) if way == 0 else jnp.maximum(t - 1, 0))
+        return remote(ref, ref, h_send.at[way, owner, j], h_recv.at[way, owner, j], dev)
+
+    chunks = q_cols // 128
+
+    def pass_on(owner, j, way):
+        @pl.when(t < n_tp - 1 if way == 0 else t > 0)
+        def _():
+            along(owner, j, way).start()
+
+    for j in range(chunks):
+        parts = []
+        for h in range(2 * j, 2 * j + 2):
+            inverse = 1.0 / acc[h, hd : hd + 1, :]
+            inv_den[h : h + 1, :] = inverse
+            parts.append(acc[h, 0:hd, :] * inverse)
+        pair = jnp.concatenate(parts, axis=0)
+        heads_all[:, chunk_cols(t, j)] = pair.T.astype(BF16)
+        for way in (0, 1):
+            pass_on(t, j, way)
+    inv_den[q_heads:, :] = jnp.zeros((8 - q_heads, rows), F32)
+
+    for d in range(1, n_tp):
+        for j in range(chunks):
+
+            @pl.when(t >= d)
+            def _():
+                along(t - d, j, 0).wait_recv()
+                pass_on(t - d, j, 0)
+
+            @pl.when(t + d < n_tp)
+            def _():
+                along(t + d, j, 1).wait_recv()
+                pass_on(t + d, j, 1)
+
+            step = (d - 1) * chunks + j
+            if step == 2:
+                gate.relay()
+                down.start()
+            if step == 4:
+                out.relay_last()
+            if step == 7:
+                up.relay()
+
+    gate.relay_last()
+    down.relay()
+    up.relay_last()
+    down.relay_last()
+    for g in gathers[1:]:
+        g.finish()
+    for cp in local[1:]:
+        cp.wait()
+    for owner in range(n_tp):
+        for j in range(chunks):
+
+            @pl.when(jnp.logical_and(t < n_tp - 1, owner <= t))
+            def _():
+                along(owner, j, 0).wait_send()
+
+            @pl.when(jnp.logical_and(t > 0, owner >= t))
+            def _():
+                along(owner, j, 1).wait_send()
+
+    for d in range(n_tp - 1):
+        wo_part(d, t).wait_send()
+
+    @pl.when(c == 0)
+    def _():
+        kv_copy.wait_send()
+        kv_all[1 - c] = jnp.zeros(kv_all.shape[1:], BF16)
+
+
+def rope_tables(positions, hd):
+    freq = ROPE_BASE ** (-np.arange(hd // 2, dtype=np.float64) / (hd // 2))
+    angle = freq[:, None] * np.arange(positions, dtype=np.float64)[None, :]
+    return np.cos(angle).astype(np.float32), np.sin(angle).astype(np.float32)
+
+
+def call_a(mesh, args):
+    (hidden_in, seq_lengths, attn_gain, ffn_gain, query_gain, key_gain,
+     w_query, w_key, w_value, w_out, w_gate, w_up, w_down) = args
+    n_shard, n_ctx, n_tp = mesh.shape["shard"], mesh.shape["ctx"], mesh.shape["tp"]
+    rows, width = hidden_in.shape
+    hd = query_gain.shape[0]
+    q_cols, kv_cols = w_query.shape[1], w_key.shape[1]
+    q_heads, kv_heads = q_cols // hd, kv_cols // hd
+    block = w_query.shape[0]
+    hidden_units = w_gate.shape[1]
+    cosine, sine = rope_tables(n_ctx * rows, hd)
+    vm = pl.BlockSpec(memory_space=pltpu.VMEM)
+    hbm = pl.BlockSpec(memory_space=pltpu.HBM)
+    sm = pl.BlockSpec(memory_space=pltpu.SMEM)
+    qkv_cols = q_cols + 2 * kv_cols
+    S = jax.ShapeDtypeStruct
+    dma = pltpu.SemaphoreType.DMA
+    chunks = q_cols // 128
+    return pl.pallas_call(
+        functools.partial(kernel_a, (n_shard, n_tp, hd)),
+        out_shape=(
+            S((width, qkv_cols), BF16),
+            S((width, n_tp * q_cols), BF16),
+            S((width, hidden_units), BF16),
+            S((width, hidden_units), BF16),
+            S((width, hidden_units), BF16),
+            S((rows, n_tp * q_cols), BF16),
+            S((q_cols, rows), BF16),
+            S((n_ctx, 2 * kv_cols, rows), BF16),
+            S((8, rows), F32),
+            S((qkv_cols, rows), F32),
+        ),
+        in_specs=[sm] + [vm] * 14,
+        out_specs=(vm, hbm, hbm, hbm, hbm, vm, vm, vm, vm, vm),
+        scratch_shapes=[
+            pltpu.VMEM((block, qkv_cols), BF16),
+            pltpu.VMEM((block, n_tp * q_cols), BF16),
+            pltpu.VMEM((block, hidden_units), BF16),
+            pltpu.VMEM((block, hidden_units), BF16),
+            pltpu.VMEM((rows, width), BF16),
+            pltpu.VMEM((kv_heads, rows, hd), BF16),
+            pltpu.VMEM((kv_heads, rows, hd), BF16),
+            pltpu.VMEM((kv_heads, hd + 16, rows), BF16),
+            pltpu.VMEM((kv_heads, hd + 16, rows), BF16),
+            pltpu.VMEM((q_heads, hd + 16, rows), F32),
+            dma((5, 7)),
+            dma((5, 7)),
+            dma((n_tp - 1,)),
+            dma((n_tp - 1,)),
+            dma((2, n_tp, chunks)),
+            dma((2, n_tp, chunks)),
+            dma((2,)),
+            dma((5,)),
+        ],
+        compiler_params=pltpu.CompilerParams(
+            collective_id=0, has_side_effects=True, vmem_limit_bytes=VMEM_LIMIT
+        ),
+    )(
+        seq_lengths, hidden_in, attn_gain.reshape(1, -1), ffn_gain.reshape(1, -1),
+        query_gain.reshape(1, -1), key_gain.reshape(1, -1), w_query, w_key, w_value,
+        w_out.T, w_gate, w_up, w_down.T, jnp.asarray(cosine), jnp.asarray(sine),
+    )
+
+
+def fast_body(mesh, *args):
+    (hidden_in, seq_lengths, attn_gain, ffn_gain, query_gain, key_gain,
+     w_query, w_key, w_value, w_out, w_gate, w_up, w_down, out_grad) = args
+    (wqkv_full, wo_full, wg_full, wu_full, wd_full, heads_all, q_t, kv_all, inv_den,
+     proj_t) = call_a(mesh, args[:13])
+    rows = hidden_in.shape[0]
+    hd = query_gain.shape[0]
+    q_cols, kv_cols = w_query.shape[1], w_key.shape[1]
+    kv_heads, q_heads = kv_cols // hd, q_cols // hd
+    group = q_heads // kv_heads
+    scale = 1.0 / math.sqrt(hd)
+    t = lax.axis_index("tp")
+    positions = lax.axis_index("ctx") * rows + jnp.arange(rows, dtype=jnp.int32)
+    length = seq_lengths[0]
+    valid = (positions < length).astype(F32)[:, None]
+    hidden = hidden_in.astype(F32)
+
+    def rms(v):
+        return v * lax.rsqrt(jnp.mean(v * v, axis=-1, keepdims=True) + EPSILON)
+
+    def psum16(v):
+        return lax.psum(v.astype(BF16), "tp").astype(F32)
+
+    resid = hidden + back_product(heads_all, wo_full)
+    h2 = rms(resid).astype(BF16)
+    gate = forward_product(h2, wg_full)
+    up = forward_product(h2, wu_full)
+    middle = activation(gate, up).astype(BF16)
+    ffn = psum16(back_product(middle, wd_full))
+    block_out = (valid * (resid + ffn)).astype(BF16)
+    grad_top = valid * out_grad.astype(F32)
+    grad_low = grad_top.astype(BF16)
+    down_wgrad = outer_product(grad_low, middle)
+    mid_grad = forward_product(grad_low, wd_full)
+    _, pull_act = jax.vjp(activation, gate, up)
+    gate_low, up_low = (v.astype(BF16) for v in pull_act(mid_grad))
+    gate_wgrad = outer_product(h2, gate_low)
+    up_wgrad = outer_product(h2, up_low)
+    d2 = psum16(back_product(gate_low, wg_full) + back_product(up_low, wu_full))
+    _, pull_two = jax.vjp(rms, resid)
+    resid_grad = grad_top + pull_two(d2)[0]
+    attn_low = resid_grad.astype(BF16)
+    heads_own = lax.dynamic_slice_in_dim(heads_all, t * q_cols, q_cols, 1)
+    wo_own = lax.dynamic_slice_in_dim(wo_full, t * q_cols, q_cols, 1)
+    out_wgrad = outer_product(attn_low, heads_own)
+    heads_grad = forward_product(attn_low, wo_own).astype(BF16)
+    delta = jnp.sum(
+        (heads_grad.astype(F32) * heads_own.astype(F32)).reshape(rows, q_heads, hd), -1
+    ).T.reshape(kv_heads, group, 1, rows)
+    keys = kv_all[:, :kv_cols].reshape(-1, kv_heads, hd, rows)
+    values = kv_all[:, kv_cols:].reshape(-1, kv_heads, hd, rows)
+    q4 = q_t.reshape(kv_heads, group, hd, rows)
+    g4 = heads_grad.T.reshape(kv_heads, group, hd, rows)
+    score = jnp.einsum("ckds,kgdt->kgcst", keys, q4, preferred_element_type=F32)
+    pos_k = jnp.arange(keys.shape[0] * rows, dtype=jnp.int32).reshape(-1, rows, 1)
+    mask = (pos_k <= positions) & (pos_k < length)
+    probs = jnp.where(mask, jnp.exp(score), 0.0) * inv_den[:q_heads].reshape(
+        kv_heads, group, 1, 1, rows
+    )
+    prob_grad = jnp.einsum("ckds,kgdt->kgcst", values, g4, preferred_element_type=F32)
+    score_grad = (probs * (prob_grad - delta[:, :, None])).astype(BF16)
+    query_grad = (
+        jnp.einsum("kgcst,ckds->tkgd", score_grad, keys, preferred_element_type=F32) * scale
+    )
+    key_grads = jnp.einsum("kgcst,kgdt->cskd", score_grad, q4, preferred_element_type=F32)
+    value_grads = jnp.einsum(
+        "kgcst,kgdt->cskd", probs.astype(BF16), g4, preferred_element_type=F32
+    )
+    both = jnp.concatenate(
+        [key_grads.reshape(-1, kv_cols), value_grads.reshape(-1, kv_cols)], axis=1
+    )
+    both = lax.psum_scatter(both, "ctx", scatter_dimension=0, tiled=True)
+
+    def query_prep(proj, gain):
+        return head_prep(proj, gain, positions)
+
+    q_gain, k_gain = query_gain.astype(F32), key_gain.astype(F32)
+    proj = proj_t.T
+    _, pull_query = jax.vjp(query_prep, proj[:, :q_cols], q_gain)
+    dq, q_gain_grad = pull_query(query_grad.reshape(rows, q_heads, hd))
+    _, pull_key = jax.vjp(query_prep, proj[:, q_cols : q_cols + kv_cols], k_gain)
+    dk, k_gain_grad = pull_key(both[:, :kv_cols].reshape(rows, kv_heads, hd))
+    dqkv = jnp.concatenate([dq, dk, both[:, kv_cols:]], axis=1).astype(BF16)
+    h1 = rms(hidden).astype(BF16)
+    qkv_wgrad = outer_product(h1, dqkv)
+    d1 = psum16(back_product(dqkv, wqkv_full))
+    _, pull_one = jax.vjp(rms, hidden)
+    input_grad = resid_grad + pull_one(d1)[0]
+    q_sum, k_sum = lax.psum((q_gain_grad, k_gain_grad), ("shard", "ctx", "tp"))
+
+    def scatter(v):
+        v = lax.psum_scatter(
+            v.astype(BF16), ("shard", "ctx"), scatter_dimension=0, tiled=True
+        )
+        return v.astype(F32)
+
+    qkv_g, gate_g, up_g, down_g, out_g = (
+        scatter(v) for v in (qkv_wgrad, gate_wgrad, up_wgrad, down_wgrad, out_wgrad)
+    )
+    g_one, g_two = attn_gain.astype(F32)[:, None], ffn_gain.astype(F32)[:, None]
+    w_one = jnp.concatenate([w_query, w_key, w_value], axis=1).astype(F32)
+    gains = jnp.stack(
+        [
+            jnp.sum(w_one * qkv_g, axis=1),
+            jnp.sum(w_gate.astype(F32) * gate_g + w_up.astype(F32) * up_g, axis=1),
+        ]
+    )
+    gains = lax.psum(gains, "tp")
+    qkv_g = qkv_g * g_one
+    return (
+        block_out, input_grad, gains[0], gains[1], q_sum, k_sum,
+        qkv_g[:, :q_cols], qkv_g[:, q_cols : q_cols + kv_cols], qkv_g[:, q_cols + kv_cols :],
+        out_g.T, gate_g * g_two, up_g * g_two, down_g.T,
+    )
+
+
 def solution(mesh):
+    sizes = mesh.shape
+    plane_of_eight = sizes["shard"] == 4 and sizes["ctx"] == 2 and sizes["tp"] > 1
+    run = functools.partial(fast_body, mesh) if plane_of_eight else body
     placed = (
         P(("shard", "ctx"), None),
         P("shard"),
@@ -328,7 +940,7 @@
         P(("shard", "ctx"), None),
     )
     return jax.shard_map(
-        body,
+        run,
         mesh=mesh,
         in_specs=placed,
         out_specs=(

time: 1550 us -> 845 us (0.55)
  waiting for transfers between devices: 1120 us -> 428 us
  Pallas kernels: 0 us -> 124 us
  blocking collectives: 136 us -> 51.3 us
  local copies, waits for them, and re-layouts: 40.4 us -> 23 us
  matrix products: 176 us -> 160 us
    psum x4 -> x2, waiting for transfers between devices: 531 us -> 217 us  [psum16(): return lax.psum(v.astype(BF16), 'tp').astype(F32)]
    reduce_scatter x9 -> x6, waiting for transfers between devices: 482 us -> 211 us  [the longest x5 206 us: scatter(): lax.psum_scatter(v.astype(BF16), ('shard', 'ctx'), scatter_dimension=0, t...]
    pallas_call x0 -> x1, Pallas kernels: none -> 124 us  [call_a(): pl.pallas_call(functools.partial(kernel_a, (n_shard, n_tp, hd)), out_shap...]
    all_gather x5 -> x0, waiting for transfers between devices: 106 us -> none  [the longest x1 37.3 us: body(): lax.all_gather(w_gate, ('shard', 'ctx'), axis=0, tiled=True)]
    all_gather x4 -> x0, blocking collectives: 49.5 us -> none  [the longest x1 16.4 us: body(): lax.all_gather(w_key, ('shard', 'ctx'), axis=0, tiled=True)]
    unnamed x2 -> x0, blocking collectives: 40 us -> none
    dynamic_update_slice x4 -> x0, local copies, waits for them, and re-layouts: 16.9 us -> none  [the longest x2 8.45 us: grad_step(): lax.dynamic_update_index_in_dim(value_store, value_grad, index, 0)]
    dot_general x7 -> x5, matrix products: 44.8 us -> 36.5 us  [back_product(): lax.dot_general(grad, weight, (((1,), (1,)), ((), ())), preferred_element...]
  transfers between devices with their start and end apart: 18 -> 8, of which waited for: 16 -> 8; matrix products, arithmetic and copies ran while one was open for 9% -> 11% of each run, Pallas kernels for 0% -> 0%
where the time goes in v1:
time: 845 us; the launch traced here: 840 us
  waiting for transfers between devices  428 us (51%)
  matrix products  160 us (19%)
  Pallas kernels  124 us (15%)
  blocking collectives  51.3 us (6%)
  other arithmetic  37.1 us (4%)
  local copies, waits for them, and re-layouts  23 us (3%)
  between operations  15.8 us (2%)
    psum x2, waiting for transfers between devices, psum16(): return lax.psum(v.astype(BF16), 'tp').astype(F32)  217 us
    reduce_scatter x5, waiting for transfers between devices, scatter(): lax.psum_scatter(v.astype(BF16), ('shard', 'ctx'), scatter_dimension=0, t...  206 us
    pallas_call x1, Pallas kernels, call_a(): pl.pallas_call(functools.partial(kernel_a, (n_shard, n_tp, hd)), out_shap...  124 us
    psum x1, blocking collectives, fast_body(): q_sum, k_sum = lax.psum((q_gain_grad, k_gain_grad), ('shard', 'ctx', 'tp'))  39.6 us
    dot_general x5, matrix products, back_product(): lax.dot_general(grad, weight, (((1,), (1,)), ((), ())), preferred_element...  36.5 us
    dot_general x5, matrix products, outer_product(): lax.dot_general(left, right, (((0,), (0,)), ((), ())), preferred_element_...  33.6 us
    dot_general x4, matrix products, forward_product(): return jnp.dot(left, right, preferred_element_type=jnp.float32)  30.6 us
    dot_general x1, matrix products, fast_body(): jnp.einsum('ckds,kgdt->kgcst', values, g4, preferred_element_type=F32)  18.8 us
  transfers between devices with their start and end apart: 8, of which 8 were waited for; matrix products, arithmetic and copies ran while one was open for 11% of the time, Pallas kernels for 0%

profile of v1, /device:TPU:0, one launch (start us, length us, event | category | flops | bytes accessed | tf_op | source)
XLA Modules:
  0.0 840.3 jit_solution(9014102744112070698)
XLA Ops:
  10.5 123.9 %shard_map.255 = (bf16[1536,640]{1,0:T(8,128)(2,1)}, bf16[1536,1536]{1,0:T(8,128)(2,1)}, bf16[1536,1728]{1,0:T(8,128)(2,1)}, bf16[1536,1728]{1,0:T(8,128)(2,1)},...) custom-call(s32[1]{0:T(128)} %copy.82.length_ref, ...), custom_call_target="tpu_custom_call" | custom-call | tf_op jit(solution)/shard_map/pallas_call | solution.py:760
  134.4 6.8 multiply_reduce_fusion
  146.3 6.3 fusion.53
  152.6 6.2 fusion.52
  158.9 13.9 %multiply_convert_fusion = (bf16[768,1728]{0,1:T(8,128)(2,1)S(1)}, bf16[768,1728]{0,1:T(8,128)(2,1)S(1)}, bf16[768,1728]{0,1:T(8,128)(2,1)}) fusion(f32[768,1728]{0,1:T(8,128)} %fusion.52, f32[768,1728]{0,1:T(8,128)} %fusion.53, bf16[1536,1728]{1,0:T(8,128)(2,1)} %get-tuple-element.27, bf16[768,1536]{1,0:T(8,128)(2,1)S(1)} %copy-done.10, ...), kind=kOutput, calls=%fused_computation.24 | convolution fusion | flops 4101636096 | bytes 26250240 | tf_op jit(solution)/shard_map/dot_general | solution.py:48
  172.7 8.5 %fusion.54 = f32[768,1536]{1,0:T(8,128)S(1)} fusion(bf16[768,1728]{0,1:T(8,128)(2,1)S(1)} %get-tuple-element.44, bf16[1536,1728]{1,0:T(8,128)(2,1)} %get-tuple-element.25), kind=kOutput, calls=%fused_computation.122 | convolution fusion | flops 4076863488 | bytes 12681216 | tf_op jit(solution)/shard_map/dot_general | solution.py:58
  181.3 8.4 add_convert_fusion
  198.1 11.5 %fusion.36 = f32[2,3,768,2,768]{4,2,3,1,0:T(8,128)} fusion(bf16[2,3,64,768,1]{3,2,4,1,0:T(8,128)(2,1)S(1)} %bitcast.127, bf16[2,2,64,768,1]{3,2,1,0,4:T(8,128)(2,1)S(1)} %bitcast.135), kind=kOutput, calls=%fused_computation.85 | convolution fusion | flops 905969664 | bytes 29294592 | tf_op jit(solution)/shard_map/ckds,kgdt->kgcst/dot_general | solution.py:859
  209.6 77.2 %all-reduce.9.cloned.1.call-done = bf16[768,1536]{1,0:T(8,128)(2,1)} async-done(((bf16[768,1536]{1,0:T(8,128)(2,1)}), bf16[768,1536]{1,0:T(8,128)(2,1)}) %all-reduce.9.cloned.1.call-update) | async-done | bytes 2359312 | tf_op jit(solution)/shard_map/psum | solution.py:827
  286.9 3.8 fusion.10
  294.7 4.2 convert_multiply_fusion.12
  301.9 12.1 %fusion.22 = f32[2,768,2,64]{1,3,0,2:T(8,128)S(1)} fusion(bf16[2,3,64,768,1]{3,2,4,1,0:T(8,128)(2,1)S(1)} %bitcast.150, f32[2,3,768,2,768]{4,2,3,1,0:T(8,128)} %fusion.36, f32[2,3,768]{2,1,0:T(4,128)} %mul.385, pred[2,768,768]{1,2,0:T(8,128)(4,1)} %compare_and_fusion), kind=kOutput, calls=%fused_computation.59 | convolution fusion | flops 927203328 | bytes 30885888 | tf_op jit(solution)/shard_map/kgcst,kgdt->cskd/dot_general | solution.py:871
  315.5 18.8 %fusion = bf16[2,3,2,768,768]{3,4,2,1,0:T(8,128)(2,1)} fusion(f32[2,3,768,2,768]{4,2,3,1,0:T(8,128)} %fusion.36, bf16[2,3,64,768,1]{3,2,4,1,0:T(8,128)(2,1)S(1)} %bitcast.151, f32[2,3,768]{2,1,0:T(4,128)S(1)} %sub.18, f32[2,3,768]{2,1,0:T(4,128)S(1)} %copy-done.26, pred[2,768,768]{1,2,0:T(8,128)(4,1)S(1)} %copy-done.16, ...), kind=kOutput, calls=%fused_computation.1 | convolution fusion | flops 941359104 | bytes 44666880 | tf_op jit(solution)/shard_map/ckds,kgdt->kgcst/dot_general | solution.py:865
  334.3 7.6 convolution_bitcast_fusion.1
  343.9 9.3 %convolution_convert_fusion.4 = bf16[768,1536]{1,0:T(8,128)(2,1)} fusion(bf16[768,1728]{0,1:T(8,128)(2,1)} %get-tuple-element.45, bf16[1536,1728]{1,0:T(8,128)(2,1)} %get-tuple-element.27), kind=kOutput, calls=%fused_computation.42 | convolution fusion | flops 4078043136 | bytes 10321920 | tf_op jit(solution)/shard_map/dot_general | solution.py:58
  353.2 9.5 %fusion.19 = f32[2,64,3,768]{3,1,2,0:T(8,128)S(1)} fusion(bf16[2,3,2,768,768]{3,4,2,1,0:T(8,128)(2,1)} %fusion, bf16[2,2,64,768,1]{3,2,1,0,4:T(8,128)(2,1)S(1)} %bitcast.136), kind=kOutput, calls=%fused_computation.53 | convolution fusion | flops 906264576 | bytes 15728640 | tf_op jit(solution)/shard_map/kgcst,ckds->tkgd/dot_general | solution.py:868
  363.6 5.4 reduce-scatter.7.cloned.1.call-done
  377.5 5.1 convolution_convert_fusion.6
  382.7 8.5 %convolution_convert_fusion.1 = bf16[1536,1728]{1,0:T(8,128)(2,1)} fusion(bf16[768,1536]{1,0:T(8,128)(2,1)S(1)} %copy-done.14, bf16[768,1728]{0,1:T(8,128)(2,1)} %copy-done.33), kind=kOutput, calls=%fused_computation.14 | convolution fusion | flops 4079517696 | bytes 10321920 | tf_op jit(solution)/shard_map/dot_general | solution.py:52
  391.3 8.1 convolution_convert_fusion.2
  401.1 8.4 convolution_convert_fusion
  409.8 139.9 %all-reduce.11.cloned.1.call-done = (bf16[768,1536]{1,0:T(8,128)(2,1)}, bf16[768,1536]{1,0:T(8,128)(2,1)}) async-done(((bf16[768,1536]{1,0:T(8,128)(2,1)}, bf16[768,1536]{1,0:T(8,128)(2,1)}), (bf16[768,1536]{1,0:T(8,128)(2,1)}, bf16[768,1536]{1,0:T(8,128)(2,1)})) %all-reduce.11.cloned.1.call-update) | async-done | bytes 4718608 | tf_op jit(solution)/shard_map/psum | solution.py:827
  552.5 3.6 convolution_convert_fusion.5
  556.1 33.5 %reduce-scatter.15.cloned.1.call-done = bf16[192,384]{1,0:T(8,128)(2,1)} async-done(((bf16[1536,384]{1,0:T(8,128)(2,1)}), bf16[192,384]{1,0:T(8,128)(2,1)}) %reduce-scatter.15.cloned.1.call-update) | async-done | bytes 147472 | tf_op jit(solution)/shard_map/reduce_scatter | solution.py:897
  591.2 39.6 %all-reduce.4 = (f32[64]{0:T(128)}, f32[64]{0:T(128)}) all-reduce(f32[64]{0:T(128)S(1)} %get-tuple-element.33, f32[64]{0:T(128)S(1)} %get-tuple-element.57), channel_id=1, replica_groups=mesh['shard'=4,'ctx'=2,'tp'=4] {'shard','ctx','tp'}, use_global_device_ids=true, to_apply=%region_20.21 | all-reduce | flops 128 | bytes 1024 | tf_op jit(solution)/shard_map/psum | solution.py:894
  630.8 20.5 %reduce-scatter.13.cloned.1.call-done = bf16[192,1728]{1,0:T(8,128)(2,1)} async-done(((bf16[1536,1728]{1,0:T(8,128)(2,1)}), bf16[192,1728]{1,0:T(8,128)(2,1)}) %reduce-scatter.13.cloned.1.call-update) | async-done | bytes 663568 | tf_op jit(solution)/shard_map/reduce_scatter | solution.py:897
  651.3 61.6 %reduce-scatter.11.cloned.1.call-done = bf16[192,1728]{1,0:T(8,128)(2,1)} async-done(((bf16[1536,1728]{1,0:T(8,128)(2,1)}), bf16[192,1728]{1,0:T(8,128)(2,1)}) %reduce-scatter.11.cloned.1.call-update) | async-done | bytes 663568 | tf_op jit(solution)/shard_map/reduce_scatter | solution.py:897
  712.9 3.8 convert_multiply_fusion.8
  716.7 57.5 %reduce-scatter.17.cloned.1.call-done = bf16[192,1728]{1,0:T(8,128)(2,1)} async-done(((bf16[1536,1728]{1,0:T(8,128)(2,1)}), bf16[192,1728]{1,0:T(8,128)(2,1)}) %reduce-scatter.17.cloned.1.call-update) | async-done | bytes 663568 | tf_op jit(solution)/shard_map/reduce_scatter | solution.py:897
  776.5 5.2 multiply_convert_fusion.2
  785.8 32.5 %reduce-scatter.9.cloned.1.call-done = bf16[192,640]{1,0:T(8,128)(2,1)} async-done(((bf16[1536,640]{1,0:T(8,128)(2,1)}), bf16[192,640]{1,0:T(8,128)(2,1)}) %reduce-scatter.9.cloned.1.call-update) | async-done | bytes 245776 | tf_op jit(solution)/shard_map/reduce_scatter | solution.py:897
  820.9 11.7 %psum.45 = f32[2,192]{1,0:T(2,128)S(1)} all-reduce(f32[2,192]{1,0:T(2,128)S(1)} %pad_maximum_fusion.4), channel_id=1, replica_groups=mesh['shard'=4,'ctx'=2,'tp'=4] {'tp'}, use_global_device_ids=true, to_apply=%region_18.19 | all-reduce | flops 384 | bytes 3072 | tf_op jit(solution)/shard_map/psum | solution.py:913
  (149 shorter events, 51.8 us)
Async XLA Ops:
  7.2 127.2 %copy-start.2 = (bf16[768,1536]{1,0:T(8,128)(2,1)S(1)}, bf16[768,1536]{1,0:T(8,128)(2,1)}, u32[]{:S(2)}) copy-start(bf16[768,1536]{1,0:T(8,128)(2,1)} %hid_ref.1) | copy-start | bytes 7077892
  7.2 279.7 %all-reduce.9.cloned.1.call-start = ((), (), s32[]{:S(2)}) async-start(), calls=%async_computation.6 | async-start | bytes 4718592 | tf_op jit(solution)/shard_map/psum | solution.py:827
  141.2 11.4 %slice-start.2 = ((s8[5505024]{0:T(1024)(128)(4,1)}), s8[4194304]{0:T(1024)(128)(4,1)S(1)}, s32[]{:S(2)}) async-start(s8[5505024]{0:T(1024)(128)(4,1)} %bitcast.164), calls=%async_computation.16 | async-start | bytes 8388608
  143.6 9.0 %copy-start.13 = (bf16[768,1536]{1,0:T(8,128)(2,1)}, bf16[768,1536]{1,0:T(8,128)(2,1)S(1)}, u32[]{:S(2)}) copy-start(bf16[768,1536]{1,0:T(8,128)(2,1)S(1)} %multiply_convert_fusion.3) | copy-start | bytes 7077892
  146.3 6.3 slice-start.3
  152.6 6.2 copy-start.10
  172.7 8.5 %copy-start.34 = (bf16[768,1728]{0,1:T(8,128)(2,1)}, bf16[768,1728]{0,1:T(8,128)(2,1)S(1)}, u32[]{:S(2)}) copy-start(bf16[768,1728]{0,1:T(8,128)(2,1)S(1)} %get-tuple-element.44) | copy-start | bytes 7962628
  172.7 8.5 %copy-start.33 = (bf16[768,1728]{0,1:T(8,128)(2,1)}, bf16[768,1728]{0,1:T(8,128)(2,1)S(1)}, u32[]{:S(2)}) copy-start(bf16[768,1728]{0,1:T(8,128)(2,1)S(1)} %get-tuple-element.43) | copy-start | bytes 7962628
  181.2 8.5 %copy-start.27 = (bf16[64]{0:T(256)(128)(2,1)S(1)}, bf16[64]{0:T(256)(128)(2,1)}, u32[]{:S(2)}) copy-start(bf16[64]{0:T(256)(128)(2,1)} %param.20) | copy-start | bytes 388
  181.2 8.5 %copy-start.28 = (bf16[64]{0:T(256)(128)(2,1)S(1)}, bf16[64]{0:T(256)(128)(2,1)}, u32[]{:S(2)}) copy-start(bf16[64]{0:T(256)(128)(2,1)} %param.21) | copy-start | bytes 388
  189.7 5.8 copy-start.19
  189.7 179.4 %reduce-scatter.7.cloned.1.call-start = ((), (), s32[]{:S(2)}) async-start(), calls=%async_computation.7 | async-start | bytes 2359296 | tf_op jit(solution)/shard_map/reduce_scatter | solution.py:877
  193.0 5.2 copy-start.4
  343.8 205.9 %all-reduce.11.cloned.1.call-start = ((), (), s32[]{:S(2)}) async-start(), calls=%async_computation.13 | async-start | bytes 9437184 | tf_op jit(solution)/shard_map/psum | solution.py:827
  343.9 9.3 %copy-start.8 = (bf16[2,128,768]{2,1,0:T(8,128)(2,1)S(1)}, bf16[2,128,768]{2,1,0:T(8,128)(2,1)}, u32[]{:S(2)}) copy-start(bf16[2,128,768]{2,1,0:T(8,128)(2,1)} %copy-done.7) | copy-start | bytes 1179652
  353.2 9.5 %copy-start.17 = (f32[768,32]{0,1:T(8,128)S(1)}, f32[768,32]{0,1:T(8,128)}, u32[]{:S(2)}) copy-start(f32[768,32]{0,1:T(8,128)} %get-tuple-element.63) | copy-start | bytes 294916
  353.2 9.5 %copy-start.18 = (f32[768,32]{0,1:T(8,128)S(1)}, f32[768,32]{0,1:T(8,128)}, u32[]{:S(2)}) copy-start(f32[768,32]{0,1:T(8,128)} %get-tuple-element.64) | copy-start | bytes 294916
  363.3 8.1 copy-start.15
  377.3 5.4 copy-start.14
  377.3 212.3 %reduce-scatter.15.cloned.1.call-start = ((), (), s32[]{:S(2)}) async-start(), calls=%async_computation.11 | async-start | bytes 1327104 | tf_op jit(solution)/shard_map/reduce_scatter | solution.py:897
  382.6 268.7 %reduce-scatter.13.cloned.1.call-start = ((), (), s32[]{:S(2)}) async-start(), calls=%async_computation.10 | async-start | bytes 6193152 | tf_op jit(solution)/shard_map/reduce_scatter | solution.py:897
  391.2 321.7 %reduce-scatter.11.cloned.1.call-start = ((), (), s32[]{:S(2)}) async-start(), calls=%async_computation.9 | async-start | bytes 6193152 | tf_op jit(solution)/shard_map/reduce_scatter | solution.py:897
  399.4 374.8 %reduce-scatter.17.cloned.1.call-start = ((), (), s32[]{:S(2)}) async-start(), calls=%async_computation.12 | async-start | bytes 6193152 | tf_op jit(solution)/shard_map/reduce_scatter | solution.py:897
  409.5 140.3 %copy-start.3 = (bf16[768,1536]{1,0:T(8,128)(2,1)S(1)}, bf16[768,1536]{1,0:T(8,128)(2,1)}, u32[]{:S(2)}) copy-start(bf16[768,1536]{1,0:T(8,128)(2,1)} %hid_ref.1) | copy-start | bytes 7077892
  409.5 408.8 %reduce-scatter.9.cloned.1.call-start = ((), (), s32[]{:S(2)}) async-start(), calls=%async_computation.8 | async-start | bytes 2211840 | tf_op jit(solution)/shard_map/reduce_scatter | solution.py:897
  556.0 156.9 %copy-start.9 = (bf16[192,1728]{1,0:T(8,128)(2,1)S(1)}, bf16[192,1728]{1,0:T(8,128)(2,1)}, u32[]{:S(2)}) copy-start(bf16[192,1728]{1,0:T(8,128)(2,1)} %wg_ref.1) | copy-start | bytes 1990660
  776.5 5.2 slice-start
  776.5 5.2 slice-start.1
  776.5 6.0 copy-start.6
  782.5 35.8 %copy-start.20 = (bf16[192,384]{1,0:T(8,128)(2,1)S(1)}, bf16[192,384]{1,0:T(8,128)(2,1)}, u32[]{:S(2)}) copy-start(bf16[192,384]{1,0:T(8,128)(2,1)} %wq_ref.1) | copy-start | bytes 442372
  782.5 35.8 %copy-start.23 = (bf16[192,128]{1,0:T(8,128)(2,1)S(1)}, bf16[192,128]{1,0:T(8,128)(2,1)}, u32[]{:S(2)}) copy-start(bf16[192,128]{1,0:T(8,128)(2,1)} %wk_ref.1) | copy-start | bytes 147460
  782.5 35.8 %copy-start.24 = (bf16[192,128]{1,0:T(8,128)(2,1)S(1)}, bf16[192,128]{1,0:T(8,128)(2,1)}, u32[]{:S(2)}) copy-start(bf16[192,128]{1,0:T(8,128)(2,1)} %wv_ref.1) | copy-start | bytes 147460
  (15 other events, 44.2 us)
Sparse Core Ops, SparseCore 0:
  189.8 97.0 all-reduce.8
  344.0 25.0 reduce-scatter.6
  377.4 172.3 all-reduce.10
  553.7 35.7 reduce-scatter.14
  592.9 58.3 reduce-scatter.12
  655.0 57.8 reduce-scatter.10
  716.4 57.7 reduce-scatter.16
  778.0 40.2 reduce-scatter.8

commit v2 on v1

--- a/solution.py
+++ b/solution.py
@@ -337,6 +337,10 @@
     return lax.dot_general(a, b, (((1,), (1,)), ((), ())), preferred_element_type=F32)
 
 
+def round_up(units):
+    return -(-units // 256) * 256
+
+
 class Place:
     def __init__(self, n_shard, n_tp):
         s = lax.axis_index("shard")
@@ -464,14 +468,12 @@
     wo_ref,
     wg_ref,
     wu_ref,
-    wd_ref,
     cos_ref,
     sin_ref,
     wqkv_full,
     wo_full,
     wg_full,
     wu_full,
-    wd_full,
     heads_all,
     q_t,
     kv_all,
@@ -514,8 +516,7 @@
     out = Gather(at, s_woz, wo_full, g_send, g_recv, 1)
     gate = Gather(at, s_wg, wg_full, g_send, g_recv, 2)
     up = Gather(at, s_wu, wu_full, g_send, g_recv, 3)
-    down = Gather(at, wd_ref, wd_full, g_send, g_recv, 4)
-    gathers = (qkv, out, gate, up, down)
+    gathers = (qkv, out, gate, up)
     local = [
         pltpu.make_async_copy(g.own, g.block(at.own), loc_sem.at[i])
         for i, g in enumerate(gathers)
@@ -549,8 +550,10 @@
     lax.fori_loop(0, rows // 64, norm_one, 0)
     qkv.relay()
     col_two = column(gain_two_ref, gain_two_ref.shape[1])
-    s_wg[...] = (wg_ref[...].astype(F32) * col_two).astype(BF16)
-    s_wu[...] = (wu_ref[...].astype(F32) * col_two).astype(BF16)
+    units = wg_ref.shape[1]
+    for src, dst in ((wg_ref, s_wg), (wu_ref, s_wu)):
+        dst[:, 0:units] = (src[...].astype(F32) * col_two).astype(BF16)
+        dst[:, units:] = jnp.zeros((dst.shape[0], dst.shape[1] - units), BF16)
     qkv.relay_last()
     for d in range(n_tp - 1):
         wo_part(d, lax.rem(t + n_tp - d - 1, n_tp)).wait_recv()
@@ -699,16 +702,13 @@
             step = (d - 1) * chunks + j
             if step == 2:
                 gate.relay()
-                down.start()
             if step == 4:
                 out.relay_last()
             if step == 7:
                 up.relay()
 
     gate.relay_last()
-    down.relay()
     up.relay_last()
-    down.relay_last()
     for g in gathers[1:]:
         g.finish()
     for cp in local[1:]:
@@ -741,14 +741,14 @@
 
 def call_a(mesh, args):
     (hidden_in, seq_lengths, attn_gain, ffn_gain, query_gain, key_gain,
-     w_query, w_key, w_value, w_out, w_gate, w_up, w_down) = args
+     w_query, w_key, w_value, w_out, w_gate, w_up) = args
     n_shard, n_ctx, n_tp = mesh.shape["shard"], mesh.shape["ctx"], mesh.shape["tp"]
     rows, width = hidden_in.shape
     hd = query_gain.shape[0]
     q_cols, kv_cols = w_query.shape[1], w_key.shape[1]
     q_heads, kv_heads = q_cols // hd, kv_cols // hd
     block = w_query.shape[0]
-    hidden_units = w_gate.shape[1]
+    padded = round_up(w_gate.shape[1])
     cosine, sine = rope_tables(n_ctx * rows, hd)
     vm = pl.BlockSpec(memory_space=pltpu.VMEM)
     hbm = pl.BlockSpec(memory_space=pltpu.HBM)
@@ -762,36 +762,35 @@
         out_shape=(
             S((width, qkv_cols), BF16),
             S((width, n_tp * q_cols), BF16),
-            S((width, hidden_units), BF16),
-            S((width, hidden_units), BF16),
-            S((width, hidden_units), BF16),
+            S((width, padded), BF16),
+            S((width, padded), BF16),
             S((rows, n_tp * q_cols), BF16),
             S((q_cols, rows), BF16),
             S((n_ctx, 2 * kv_cols, rows), BF16),
             S((8, rows), F32),
             S((qkv_cols, rows), F32),
         ),
-        in_specs=[sm] + [vm] * 14,
-        out_specs=(vm, hbm, hbm, hbm, hbm, vm, vm, vm, vm, vm),
+        in_specs=[sm] + [vm] * 13,
+        out_specs=(vm, hbm, hbm, hbm, vm, vm, vm, vm, vm),
         scratch_shapes=[
             pltpu.VMEM((block, qkv_cols), BF16),
             pltpu.VMEM((block, n_tp * q_cols), BF16),
-            pltpu.VMEM((block, hidden_units), BF16),
-            pltpu.VMEM((block, hidden_units), BF16),
+            pltpu.VMEM((block, padded), BF16),
+            pltpu.VMEM((block, padded), BF16),
             pltpu.VMEM((rows, width), BF16),
             pltpu.VMEM((kv_heads, rows, hd), BF16),
             pltpu.VMEM((kv_heads, rows, hd), BF16),
             pltpu.VMEM((kv_heads, hd + 16, rows), BF16),
             pltpu.VMEM((kv_heads, hd + 16, rows), BF16),
             pltpu.VMEM((q_heads, hd + 16, rows), F32),
-            dma((5, 7)),
-            dma((5, 7)),
+            dma((4, 7)),
+            dma((4, 7)),
             dma((n_tp - 1,)),
             dma((n_tp - 1,)),
             dma((2, n_tp, chunks)),
             dma((2, n_tp, chunks)),
             dma((2,)),
-            dma((5,)),
+            dma((4,)),
         ],
         compiler_params=pltpu.CompilerParams(
             collective_id=0, has_side_effects=True, vmem_limit_bytes=VMEM_LIMIT
@@ -799,123 +798,1015 @@
     )(
         seq_lengths, hidden_in, attn_gain.reshape(1, -1), ffn_gain.reshape(1, -1),
         query_gain.reshape(1, -1), key_gain.reshape(1, -1), w_query, w_key, w_value,
-        w_out.T, w_gate, w_up, w_down.T, jnp.asarray(cosine), jnp.asarray(sine),
-    )
+        w_out.T, w_gate, w_up, jnp.asarray(cosine), jnp.asarray(sine),
+    )
+
+
+class Line:
+    def __init__(self, at, part, landing, send, recv, chunks):
+        self.at, self.part, self.landing = at, part, landing
+        self.send, self.recv, self.chunks = send, recv, chunks
+        self.half = landing.shape[1]
+        self.size = self.half // chunks
+        self.last = at.n_tp - 1
+
+    def pos(self, way):
+        return self.at.t if way == 0 else self.last - self.at.t
+
+    def dev(self, way, step):
+        to = self.at.t + (step if way == 0 else -step)
+        return self.at.z(jnp.clip(to, 0, self.last))
+
+    def local(self, k):
+        return pl.ds(pl.multiple_of(k * self.size, self.size), self.size)
+
+    def rows(self, way, k):
+        start = (1 - way) * self.half + k * self.size
+        return pl.ds(pl.multiple_of(start, self.size), self.size)
+
+    def copy(self, way, k):
+        return remote(
+            self.part.at[self.rows(way, k)],
+            self.landing.at[way, self.local(k)],
+            self.send.at[way, k],
+            self.recv.at[way, k],
+            self.dev(way, 1),
+        )
+
+    def reduce(self, step, final):
+        for way in (0, 1):
+            pos = self.pos(way)
+            k = step - pos
+            live = jnp.logical_and(k >= 0, k < self.chunks)
+
+            @pl.when(jnp.logical_and(live, pos > 0))
+            def _():
+                self.copy(way, k).wait_recv()
+                value = self.part[self.rows(way, k), :].astype(F32)
+                value += self.landing[way, self.local(k), :].astype(F32)
+
+                @pl.when(pos < self.last)
+                def _():
+                    self.part[self.rows(way, k), :] = value.astype(BF16)
+
+                @pl.when(pos == self.last)
+                def _():
+                    final(way, k, value)
+
+            @pl.when(jnp.logical_and(live, pos < self.last))
+            def _():
+                self.copy(way, k).start()
+
+    def drain(self):
+        for way in (0, 1):
+
+            @pl.when(self.pos(way) < self.last)
+            def _():
+                def one(k, _):
+                    self.copy(way, k).wait_send()
+                    return 0
+
+                lax.fori_loop(0, self.chunks, one, 0)
+
+
+class Back:
+    def __init__(self, line, whole, send, recv, source=None):
+        self.line, self.whole, self.send, self.recv = line, whole, send, recv
+        self.source = source
+
+    def copy(self, way, k, first=False):
+        line = self.line
+        dst = self.whole.at[line.rows(way, k)]
+        src = self.source.at[line.local(k)] if first and self.source is not None else dst
+        return remote(src, dst, self.send.at[way, k], self.recv.at[way, k], line.dev(way, -1))
+
+    def step(self, step):
+        line = self.line
+        for way in (0, 1):
+            pos = line.pos(way)
+            k = step - (line.last - pos)
+            live = jnp.logical_and(k >= 0, k < line.chunks)
+
+            @pl.when(jnp.logical_and(live, pos < line.last))
+            def _():
+                self.copy(way, k).wait_recv()
+
+                @pl.when(pos > 0)
+                def _():
+                    self.copy(way, k).start()
+
+            @pl.when(jnp.logical_and(live, pos == line.last))
+            def _():
+                self.copy(way, k, True).start()
+
+    def drain(self):
+        line = self.line
+        for way in (0, 1):
+
+            @pl.when(line.pos(way) > 0)
+            def _():
+                def one(k, _):
+                    self.copy(way, k).wait_send()
+                    return 0
+
+                lax.fori_loop(0, line.chunks, one, 0)
+
+
+def kernel_b(
+    shape,
+    length_ref,
+    hid_ref,
+    heads_ref,
+    og_ref,
+    wd_ref,
+    wo_hbm,
+    wg_hbm,
+    wu_hbm,
+    attn_low,
+    rg_own,
+    blk_own,
+    wgrads,
+    wo,
+    wg,
+    wu,
+    wd,
+    resid,
+    h2,
+    gl,
+    act,
+    land_f,
+    land_d,
+    stage,
+    g_send,
+    g_recv,
+    f_send,
+    f_recv,
+    d_send,
+    d_recv,
+    b_send,
+    b_recv,
+    loc_sem,
+    st_sem,
+):
+    n_shard, n_tp, chunks = shape
+    at = Place(n_shard, n_tp)
+    rows, width = hid_ref.shape
+    units, padded = wd_ref.shape[1], wd.shape[1]
+    block = wd_ref.shape[0]
+    half = rows // 2
+    tiles = padded // 256
+    loads = [
+        pltpu.make_async_copy(src, dst, loc_sem.at[i])
+        for i, (src, dst) in enumerate(((wo_hbm, wo), (wg_hbm, wg), (wu_hbm, wu)))
+    ]
+    for cp in loads:
+        cp.start()
+    own = pl.ds(pl.multiple_of(at.own * block, block), block)
+    wd[own, 0:units] = wd_ref[...]
+    wd[own, units:] = jnp.zeros((block, padded - units), BF16)
+    at.greet()
+    down = Gather(at, wd.at[own], wd, g_send, g_recv, 0)
+    down.start()
+    length = length_ref[0]
+
+    def live_rows(start, n):
+        pos = at.c * rows + start + lax.broadcasted_iota(jnp.int32, (n, 1), 0)
+        return (pos < length).astype(F32)
+
+    def mask_grad(i, _):
+        start = pl.multiple_of(i * 64, 64)
+        r = pl.ds(start, 64)
+        gl[r, :] = (og_ref[r, :].astype(F32) * live_rows(start, 64)).astype(BF16)
+        return 0
+
+    lax.fori_loop(0, rows // 64, mask_grad, 0)
+    loads[0].wait()
+
+    def residual(i, _):
+        r = pl.ds(pl.multiple_of(i * 128, 128), 128)
+        x = hid_ref[r, :].astype(F32) + mm_nt(heads_ref[r, :], wo[...])
+        resid[r, :] = x
+        scale = lax.rsqrt(jnp.mean(x * x, axis=-1, keepdims=True) + EPSILON)
+        h2[r, :] = (x * scale).astype(BF16)
+        return 0
+
+    lax.fori_loop(0, rows // 128, residual, 0)
+    loads[1].wait()
+    loads[2].wait()
+
+    def gate_up(f, _):
+        cols = pl.ds(pl.multiple_of(f * 256, 256), 256)
+        for i in (0, 1):
+            r = slice(i * half, (i + 1) * half)
+            g = mm(h2[r, :], wg[:, cols])
+            u = mm(h2[r, :], wu[:, cols])
+            s = 1.0 / (1.0 + jnp.exp(-g))
+            silu = g * s
+            act[0, r, cols] = (silu * u).astype(BF16)
+            act[1, r, cols] = (u * (s * (1.0 + g * (1.0 - s)))).astype(BF16)
+            act[2, r, cols] = silu.astype(BF16)
+
+        @pl.when(f == 2)
+        def _():
+            down.relay()
+
+        @pl.when(f == tiles - 1)
+        def _():
+            down.relay_last()
+
+        return 0
+
+    lax.fori_loop(0, tiles, gate_up, 0)
+    down.finish()
+
+    f_part, d_part = wo.at[0:rows], wo.at[rows:]
+    quarter = half // 2
+    ffn = Line(at, f_part, land_f, f_send, f_recv, chunks)
+    d2 = Line(at, d_part, land_d, d_send, d_recv, chunks)
+    back = Back(d2, attn_low, b_send, b_recv)
+
+    def final_ffn(way, k, value):
+        r = ffn.rows(way, k)
+        x = resid[r, :] + value
+        live = live_rows((1 - way) * half + k * ffn.size, ffn.size)
+        blk_own[ffn.local(k), :] = (x * live).astype(BF16)
+
+    def final_d2(way, k, value):
+        r = d2.rows(way, k)
+        x = resid[r, :]
+        scale = lax.rsqrt(jnp.mean(x * x, axis=-1, keepdims=True) + EPSILON)
+        h = x * scale
+        inner = jnp.mean(value * h, axis=-1, keepdims=True)
+        grad = gl[r, :].astype(F32) + scale * (value - h * inner)
+        rg_own[d2.local(k), :] = grad
+        attn_low[r, :] = grad.astype(BF16)
+
+    order = (0, 2, 1, 3)
+    for q in order:
+        r = slice(q * quarter, (q + 1) * quarter)
+        f_part[r, :] = mm_nt(act[0, r, :], wd[...]).astype(BF16)
+
+    def mid(f, _):
+        cols = pl.ds(pl.multiple_of(f * 256, 256), 256)
+        for i in (0, 1):
+            r = slice(i * half, (i + 1) * half)
+            g = mm(gl[r, :], wd[:, cols])
+            act[1, r, cols] = (g * act[1, r, cols].astype(F32)).astype(BF16)
+            act[2, r, cols] = (g * act[2, r, cols].astype(F32)).astype(BF16)
+
+        @pl.when(lax.rem(f, 3) == 0)
+        def _():
+            ffn.reduce(lax.div(f, 3), final_ffn)
+
+        return 0
+
+    lax.fori_loop(0, tiles, mid, 0)
+    done = -(-tiles // 3)
+    for n, q in enumerate(order):
+        r = slice(q * quarter, (q + 1) * quarter)
+        total = mm_nt(act[1, r, :], wg[...]) + mm_nt(act[2, r, :], wu[...])
+        d_part[r, :] = total.astype(BF16)
+        ffn.reduce(done + n, final_ffn)
+    done += len(order)
+
+    def turn(i, _):
+        r = pl.ds(pl.multiple_of(i * 128, 128), 128)
+        r2 = pl.ds(pl.multiple_of(rows + i * 128, 128), 128)
+        wu[:, r] = h2[r, :].T
+        wu[:, r2] = gl[r, :].T
+        return 0
+
+    last = n_tp - 1
+    per_step = 2
+    count = 3 * (width // block)
+
+    def stage_copy(n):
+        a, w = lax.div(n, width // block), lax.rem(n, width // block)
+        slot = lax.rem(n, 2)
+        return pltpu.make_async_copy(
+            stage.at[slot],
+            wgrads.at[a, pl.ds(pl.multiple_of(w * block, block), block)],
+            st_sem.at[slot],
+        )
+
+    def weight_grad(n):
+        a, w = lax.div(n, width // block), lax.rem(n, width // block)
+        slot = lax.rem(n, 2)
+
+        @pl.when(n >= 2)
+        def _():
+            stage_copy(n - 2).wait()
+
+        first = pl.multiple_of(jnp.where(a == 0, rows, 0), 128)
+        left = wu[pl.ds(pl.multiple_of(w * block, block), block), pl.ds(first, rows)]
+        for f in range(tiles):
+            cols = slice(f * 256, (f + 1) * 256)
+            stage[slot, :, cols] = mm(left, act[a, :, cols]).astype(BF16)
+        stage_copy(n).start()
+
+    def tail(step, _):
+        @pl.when(step + done < chunks + last)
+        def _():
+            ffn.reduce(step + done, final_ffn)
+
+        d2.reduce(step, final_d2)
+        back.step(step - last)
+
+        @pl.when(step == 0)
+        def _():
+            lax.fori_loop(0, rows // 128, turn, 0)
+
+        for n in range(per_step):
+
+            @pl.when(step * per_step + n < count)
+            def _():
+                weight_grad(step * per_step + n)
+
+        return 0
+
+    steps = max(chunks + 2 * last, -(-count // per_step), chunks + last - done)
+    lax.fori_loop(0, steps, tail, 0)
+    stage_copy(count - 2).wait()
+    stage_copy(count - 1).wait()
+    ffn.drain()
+    d2.drain()
+    back.drain()
+
+
+def call_b(mesh, chunks, seq_lengths, hidden_in, heads_all, out_grad, w_down, wo_full, wg_full, wu_full):
+    n_shard, n_tp = mesh.shape["shard"], mesh.shape["tp"]
+    rows, width = hidden_in.shape
+    block = w_down.shape[1]
+    padded = wg_full.shape[1]
+    half = rows // 2
+    vm = pl.BlockSpec(memory_space=pltpu.VMEM)
+    hbm = pl.BlockSpec(memory_space=pltpu.HBM)
+    sm = pl.BlockSpec(memory_space=pltpu.SMEM)
+    S = jax.ShapeDtypeStruct
+    dma = pltpu.SemaphoreType.DMA
+    return pl.pallas_call(
+        functools.partial(kernel_b, (n_shard, n_tp, chunks)),
+        out_shape=(
+            S((rows, width), BF16),
+            S((half, width), F32),
+            S((half, width), BF16),
+            S((3, width, padded), BF16),
+        ),
+        in_specs=[sm] + [vm] * 4 + [hbm] * 3,
+        out_specs=(vm, vm, vm, hbm),
+        scratch_shapes=[
+            pltpu.VMEM((width, width), BF16),
+            pltpu.VMEM((width, padded), BF16),
+            pltpu.VMEM((width, padded), BF16),
+            pltpu.VMEM((width, padded), BF16),
+            pltpu.VMEM((rows, width), F32),
+            pltpu.VMEM((rows, width), BF16),
+            pltpu.VMEM((rows, width), BF16),
+            pltpu.VMEM((3, rows, padded), BF16),
+            pltpu.VMEM((2, half, width), BF16),
+            pltpu.VMEM((2, half, width), BF16),
+            pltpu.VMEM((2, block, padded), BF16),
+            dma((1, 7)),
+            dma((1, 7)),
+            dma((2, chunks)),
+            dma((2, chunks)),
+            dma((2, chunks)),
+            dma((2, chunks)),
+            dma((2, chunks)),
+            dma((2, chunks)),
+            dma((3,)),
+            dma((2,)),
+        ],
+        compiler_params=pltpu.CompilerParams(
+            collective_id=1, has_side_effects=True, vmem_limit_bytes=VMEM_LIMIT
+        ),
+    )(seq_lengths, hidden_in, heads_all, out_grad, w_down.T, wo_full, wg_full, wu_full)
+
+
+class Scatter:
+    def __init__(self, at, source, land, relayed, final, tmp, tmp_sem, send, recv, index):
+        self.at, self.source, self.land = at, source, land
+        self.relayed, self.final = relayed, final
+        self.tmp, self.tmp_sem = tmp, tmp_sem
+        self.send, self.recv, self.index = send, recv, index
+        self.rows = land.shape[1]
+        self.direct, self.indirect = 1 + at.core, 2 - at.core
+        self.other = (
+            at.core * at.x[0] + (1 - at.core) * at.y[0],
+            at.core * at.x[1] + (1 - at.core) * at.y[1],
+            at.t,
+        )
+        names = (("own", "X", "Y", "D"), ("S", "SX", "SY", "SD"))
+        find = lambda n: at.own if n == "own" else at.slots[n]
+        self.mine = [find(n) for n in names[0]]
+        self.theirs = [find(n) for n in names[1]]
+
+    def block(self, slot):
+        return self.source.at[pl.ds(pl.multiple_of(slot * self.rows, self.rows), self.rows)]
+
+    def copy(self, k, src, dst, dev):
+        return remote(src, dst, self.send.at[self.index, k], self.recv.at[self.index, k], dev)
+
+    def share(self, j):
+        return self.copy(j, self.block(self.theirs[j]), self.land.at[j], self.at.sib)
+
+    def start(self):
+        for j in (3, 1, 2, 0):
+            self.share(j).start()
+
+    def slot(self, j):
+        if isinstance(j, int):
+            return self.mine[j]
+        return jnp.where(j == 1, self.mine[1], self.mine[2])
+
+    def arrived(self, j):
+        ref = self.land.at[j]
+        self.copy(j, ref, ref, self.at.sib).wait_recv()
+
+    def fetch(self, j):
+        return pltpu.make_async_copy(self.block(self.slot(j)), self.tmp, self.tmp_sem)
+
+    def add(self, j, extra=()):
+        self.fetch(j).start()
+        self.arrived(j)
+        self.fetch(j).wait()
+
+        def piece(i, _):
+            r = pl.ds(pl.multiple_of(i * 64, 64), 64)
+            value = self.land[j, r, :].astype(F32) + self.tmp[r, :].astype(F32)
+            for ref in extra:
+                value += ref[r, :].astype(F32)
+            self.land[j, r, :] = value.astype(BF16)
+            return 0
+
+        lax.fori_loop(0, self.rows // 64, piece, 0)
+
+    def hop(self, k):
+        at = self.at
+        if k == 4:
+            return self.copy(4, self.land.at[3], self.relayed, at.relay)
+        if k == 5:
+            return self.copy(5, self.land.at[self.direct], self.final.at[0], at.relay)
+        return self.copy(6, self.land.at[self.indirect], self.final.at[1], self.other)
+
+    def first(self):
+        self.add(3)
+        self.hop(4).start()
+        self.add(self.direct)
+        self.hop(5).start()
+
+    def second(self):
+        self.hop(4).wait_recv()
+        self.add(self.indirect, (self.relayed,))
+        self.hop(6).start()
+
+    def finish(self, use):
+        self.fetch(0).start()
+        self.arrived(0)
+        self.hop(5).wait_recv()
+        self.hop(6).wait_recv()
+        self.fetch(0).wait()
+
+        def piece(i, _):
+            r = pl.ds(pl.multiple_of(i * 64, 64), 64)
+            value = self.land[0, r, :].astype(F32) + self.tmp[r, :].astype(F32)
+            value += self.final[0, r, :].astype(F32) + self.final[1, r, :].astype(F32)
+            use(r, value)
+            return 0
+
+        lax.fori_loop(0, self.rows // 64, piece, 0)
+
+    def drain(self):
+        for j in range(4):
+            self.share(j).wait_send()
+        for k in (4, 5, 6):
+            self.hop(k).wait_send()
+
+
+def kernel_c(
+    shape,
+    length_ref,
+    attn_low,
+    rg_own,
+    hid_ref,
+    wqkv,
+    q_t,
+    kv_all,
+    inv_den,
+    proj_t,
+    gain_one_ref,
+    gain_two_ref,
+    q_gain_ref,
+    k_gain_ref,
+    wq_ref,
+    wk_ref,
+    wv_ref,
+    wg_ref,
+    wu_ref,
+    cos_ref,
+    sin_ref,
+    blk_own,
+    wgrads,
+    heads_hbm,
+    wo_hbm,
+    block_out,
+    inp,
+    g_query,
+    g_key,
+    g_value,
+    g_out,
+    g_gate,
+    g_up,
+    g_down,
+    small,
+    heads_own,
+    wo_own,
+    hg_t,
+    delta,
+    k_own,
+    v_own,
+    kt_own,
+    dq_t,
+    dkv,
+    dkv_send,
+    dkv_land,
+    gain_acc,
+    dqkv,
+    d_part,
+    land_d,
+    left_t,
+    part,
+    land_w,
+    rel_w,
+    fin_w,
+    land_p,
+    rel_p,
+    fin_p,
+    tmp_w,
+    tmp_p,
+    cols_acc,
+    qk,
+    qk_land,
+    tile,
+    s_send,
+    s_recv,
+    d_send,
+    d_recv,
+    b_send,
+    b_recv,
+    o_send,
+    o_recv,
+    e_send,
+    e_recv,
+    t_send,
+    t_recv,
+    loc_sem,
+):
+    n_shard, n_tp, chunks, hd = shape
+    at = Place(n_shard, n_tp)
+    c, t = at.c, at.t
+    rows, width = hid_ref.shape
+    q_cols, kv_cols = wq_ref.shape[1], wk_ref.shape[1]
+    q_heads, kv_heads = q_cols // hd, kv_cols // hd
+    group = q_heads // kv_heads
+    halfd = hd // 2
+    half = rows // 2
+    block = wq_ref.shape[0]
+    units = wg_ref.shape[1]
+    last = n_tp - 1
+    own_cols = pl.ds(pl.multiple_of(t * q_cols, q_cols), q_cols)
+    loads = [
+        pltpu.make_async_copy(heads_hbm.at[:, own_cols], heads_own, loc_sem.at[0]),
+        pltpu.make_async_copy(wo_hbm.at[:, own_cols], wo_own, loc_sem.at[1]),
+    ]
+    for cp in loads:
+        cp.start()
+    at.greet()
+    weights = [
+        Scatter(
+            at, wgrads.at[i], land_w.at[i], rel_w.at[i], fin_w.at[i], tmp_w,
+            loc_sem.at[2], s_send, s_recv, i,
+        )
+        for i in range(3)
+    ]
+    rest = Scatter(
+        at, part, land_p, rel_p, fin_p, tmp_p, loc_sem.at[3], s_send, s_recv, 3
+    )
+    for w in weights:
+        w.start()
+    d1 = Line(at, d_part, land_d, d_send, d_recv, chunks)
+    back = Back(d1, inp, b_send, b_recv)
+    back_block = Back(d1, block_out, o_send, o_recv, blk_own)
+
+    def keep(start):
+        return pltpu.make_async_copy(
+            blk_own, block_out.at[pl.ds(start, half)], loc_sem.at[4]
+        )
+
+    @pl.when(t == 0)
+    def _():
+        keep(0).start()
+
+    @pl.when(t == last)
+    def _():
+        keep(half).start()
+
+    back_block.step(0)
+    length = length_ref[0]
+    for cp in loads:
+        cp.wait()
+
+    def heads_grad(i, _):
+        r = pl.ds(pl.multiple_of(i * 256, 256), 256)
+        hg_t[:, r] = mm(attn_low[r, :], wo_own[...]).T.astype(BF16)
+        return 0
+
+    lax.fori_loop(0, rows // 256, heads_grad, 0)
+    for j in range(q_cols // 128):
+        cols = slice(j * 128, (j + 1) * 128)
+        both = heads_own[:, cols].astype(F32).T * hg_t[cols, :].astype(F32)
+        for n in range(128 // hd):
+            h = j * (128 // hd) + n
+            delta[h : h + 1, :] = jnp.sum(both[n * hd : (n + 1) * hd], axis=0, keepdims=True)
+    back_block.step(1)
+    weights[0].first()
+
+    def live_keys(index):
+        pos = index * rows + lax.broadcasted_iota(jnp.int32, (1, rows), 1)
+        return (pos < length).astype(F32)
+
+    def load_block(index, k_nat, v_nat, kt):
+        live = live_keys(index)
+        for g in range(kv_heads):
+            key = kv_all[index, g * hd : (g + 1) * hd, :].astype(F32)
+            k_nat[g] = key.T.astype(BF16)
+            kt[g] = (key * live).astype(BF16)
+            value = kv_all[index, kv_cols + g * hd : kv_cols + (g + 1) * hd, :]
+            v_nat[g] = value.astype(F32).T.astype(BF16)
+
+    below = lax.broadcasted_iota(jnp.int32, (256, 256), 0) <= lax.broadcasted_iota(
+        jnp.int32, (256, 256), 1
+    )
+
+    def segment(h, g, i, lo, hi, masked, k_nat, v_nat, kt):
+        cols = slice(i * 256, (i + 1) * 256)
+        hr = pl.ds(pl.multiple_of(h * hd, hd), hd)
+        qi, oi = q_t[hr, cols], hg_t[hr, cols]
+        p = jnp.exp(mm(k_nat[g, lo:hi, :], qi)) * inv_den[pl.ds(h, 1), cols]
+        if masked:
+            p = jnp.where(below, p, 0.0)
+        dp = mm(v_nat[g, lo:hi, :], oi)
+        ds = (p * (dp - delta[pl.ds(h, 1), cols])).astype(BF16)
+        dq_t[hr, cols] += mm(kt[g, :, lo:hi], ds)
+        dkv[g, :, lo:hi] += mm_nt(qi, ds)
+        dkv[kv_heads + g, :, lo:hi] += mm_nt(oi, p.astype(BF16))
+
+    dq_t[...] = jnp.zeros_like(dq_t)
+    dkv[...] = jnp.zeros_like(dkv)
+    give = remote(dkv_send, dkv_land, e_send.at[3], e_recv.at[3], at.x)
+
+    @pl.when(c == 1)
+    def _():
+        load_block(0, k_own, v_own, kt_own)
+
+        def one(h, _):
+            for i in range(rows // 256):
+                segment(h, h // group, i, 0, rows, False, k_own, v_own, kt_own)
+            return 0
+
+        lax.fori_loop(0, q_heads, one, 0)
+        live = live_keys(0)
+        for n in range(2 * kv_heads):
+            dkv_send[n] = (dkv[n] * live).astype(BF16)
+        give.start()
+        dkv[...] = jnp.zeros_like(dkv)
+
+    back_block.step(2)
+    weights[1].first()
+    weights[0].second()
+    load_block(c, k_own, v_own, kt_own)
+
+    def own_block(h, _):
+        for i in range(rows // 256):
+            segment(h, h // group, i, i * 256, (i + 1) * 256, True, k_own, v_own, kt_own)
+            if i:
+                segment(h, h // group, i, 0, i * 256, False, k_own, v_own, kt_own)
+
+        back_block.step(3 + h)
+        return 0
+
+    lax.fori_loop(0, q_heads, own_block, 0)
+    live = live_keys(c)
+    for n in range(2 * kv_heads):
+        dkv[n] = dkv[n] * live
+
+    @pl.when(c == 0)
+    def _():
+        give.wait_recv()
+        for n in range(2 * kv_heads):
+            dkv[n] += dkv_land[n].astype(F32)
+
+    here = pl.ds(pl.multiple_of(c * rows, rows), rows)
+    gain_acc[...] = jnp.zeros_like(gain_acc)
+
+    def through(which, row, grad, gain):
+        x = proj_t[pl.ds(pl.multiple_of(row, hd), hd), :]
+        scale = lax.rsqrt(jnp.mean(x * x, axis=0, keepdims=True) + EPSILON)
+        xh = x * scale
+        cosine, sine = cos_ref[:, here], sin_ref[:, here]
+        a, b = grad[:halfd], grad[halfd:]
+        grad = jnp.concatenate([a * cosine + b * sine, b * cosine - a * sine], axis=0)
+        gain_acc[which] += grad * xh
+        grad = grad * gain
+        inner = jnp.mean(grad * xh, axis=0, keepdims=True)
+        return scale * (grad - xh * inner)
+
+    q_gain, k_gain = column(q_gain_ref, hd), column(k_gain_ref, hd)
+    factor = 1.0 / math.sqrt(hd)
+
+    def query_back(h, _):
+        row = pl.multiple_of(h * hd, hd)
+        r = pl.ds(row, hd)
+        dq_t[r, :] = through(0, row, dq_t[r, :] * factor, q_gain)
+        return 0
+
+    lax.fori_loop(0, q_heads, query_back, 0)
+    dqkv[:, 0:q_cols] = dq_t[...].T.astype(BF16)
+    pair = jnp.concatenate(
+        [through(1, q_cols + g * hd, dkv[g], k_gain) for g in range(kv_heads)], axis=0
+    )
+    dqkv[:, q_cols : q_cols + kv_cols] = pair.T.astype(BF16)
+    pair = jnp.concatenate([dkv[kv_heads + g] for g in range(kv_heads)], axis=0)
+    dqkv[:, q_cols + kv_cols :] = pair.T.astype(BF16)
+    quarter = half // 2
+    for q in (0, 2, 1, 3):
+        r = slice(q * quarter, (q + 1) * quarter)
+        d_part[r, :] = mm_nt(dqkv[r, :], wqkv[...]).astype(BF16)
+
+    def as_row(v):
+        return jnp.broadcast_to(v, (v.shape[0], 128)).T[0:1, :]
+
+    qk[...] = jnp.zeros_like(qk)
+    for n in (0, 1):
+        qk[0, n : n + 1, 0:hd] = as_row(jnp.sum(gain_acc[n], axis=1, keepdims=True))
+
+    def trade(n):
+        dev = (at.sib, at.x, at.y)[n]
+        return remote(qk.at[n], qk_land.at[n], e_send.at[n], e_recv.at[n], dev)
+
+    def traded(n):
+        trade(n).wait_recv()
+        qk[n + 1] = qk[n] + qk_land[n]
+
+    weights[2].first()
+    weights[1].second()
+
+    def final(way, k, value):
+        r = d1.rows(way, k)
+        x = hid_ref[r, :].astype(F32)
+        scale = lax.rsqrt(jnp.mean(x * x, axis=-1, keepdims=True) + EPSILON)
+        h = x * scale
+        inner = jnp.mean(value * h, axis=-1, keepdims=True)
+        grad = rg_own[d1.local(k), :] + scale * (value - h * inner)
+        inp[r, :] = grad.astype(BF16)
+
+    def turn_hidden(i, _):
+        r = pl.ds(pl.multiple_of(i * 128, 128), 128)
+        x = hid_ref[r, :].astype(F32)
+        scale = lax.rsqrt(jnp.mean(x * x, axis=-1, keepdims=True) + EPSILON)
+        left_t[0, :, r] = (x * scale).astype(BF16).T
+        left_t[1, :, r] = attn_low[r, :].T
+        return 0
+
+    def weight_part(w, _):
+        r = pl.ds(pl.multiple_of(w * block, block), block)
+        part[r, 0 : dqkv.shape[1]] = mm(left_t[0, r, :], dqkv[...]).astype(BF16)
+        part[r, dqkv.shape[1] :] = mm(left_t[1, r, :], heads_own[...]).astype(BF16)
+        return 0
+
+    g_one = column(gain_one_ref, block)
+    g_two = column(gain_two_ref, block)
+    cols_acc[0] = jnp.broadcast_to(g_one, (block, 128))
+    cols_acc[1] = jnp.broadcast_to(g_two, (block, 128))
+
+    def use_down(r, value):
+        g_down[r, :] = value[:, 0:units]
+
+    def use_gate(r, value):
+        value = value[:, 0:units]
+        total = jnp.sum(wg_ref[r, :].astype(F32) * value, axis=1, keepdims=True)
+        cols_acc[3, r, :] = jnp.broadcast_to(total, (64, 128))
+        g_gate[r, :] = value * cols_acc[1, r, 0:1]
+
+    def use_up(r, value):
+        value = value[:, 0:units]
+        total = jnp.sum(wu_ref[r, :].astype(F32) * value, axis=1, keepdims=True)
+        cols_acc[3, r, :] += jnp.broadcast_to(total, (64, 128))
+        g_up[r, :] = value * cols_acc[1, r, 0:1]
+
+    def use_rest(r, value):
+        gain = cols_acc[0, r, 0:1]
+        vq = value[:, 0:q_cols]
+        vk = value[:, q_cols : q_cols + kv_cols]
+        vv = value[:, q_cols + kv_cols : q_cols + 2 * kv_cols]
+        total = jnp.sum(wq_ref[r, :].astype(F32) * vq, axis=1, keepdims=True)
+        total += jnp.sum(wk_ref[r, :].astype(F32) * vk, axis=1, keepdims=True)
+        total += jnp.sum(wv_ref[r, :].astype(F32) * vv, axis=1, keepdims=True)
+        cols_acc[2, r, :] = jnp.broadcast_to(total, (64, 128))
+        g_query[r, :] = vq * gain
+        g_key[r, :] = vk * gain
+        g_value[r, :] = vv * gain
+        g_out[r, :] = value[:, q_cols + 2 * kv_cols :]
+
+    def turn_all():
+        lax.fori_loop(0, rows // 128, turn_hidden, 0)
+
+    def parts():
+        lax.fori_loop(0, width // block, weight_part, 0)
+        rest.start()
+
+    events = {
+        0: (lambda: trade(0).start(), turn_all),
+        1: (parts, lambda: traded(0), lambda: trade(1).start()),
+        2: (rest.first, lambda: traded(1), lambda: trade(2).start()),
+        3: (weights[2].second, lambda: traded(2)),
+        4: (rest.second, lambda: weights[0].finish(use_down)),
+        7: (lambda: weights[1].finish(use_gate),),
+        10: (lambda: weights[2].finish(use_up),),
+        12: (lambda: rest.finish(use_rest),),
+    }
+
+    def tail(step, _):
+        d1.reduce(step, final)
+        back.step(step - last)
+        back_block.step(step + 3 + q_heads)
+        for when, todo in events.items():
+
+            @pl.when(step == when)
+            def _():
+                for thing in todo:
+                    thing()
+
+        return 0
+
+    lax.fori_loop(0, max(chunks + 2 * last, 13), tail, 0)
+
+    def give_tile(d, owner):
+        return remote(
+            tile.at[owner], tile.at[owner], t_send.at[d], t_recv.at[d],
+            at.z(lax.rem(t + d + 1, n_tp)),
+        )
+
+    tile[t] = jnp.zeros(tile.shape[1:], F32)
+    tile[t, 0:1, 0:block] = cols_acc[2].T[0:1, :]
+    tile[t, 1:2, 0:block] = cols_acc[3].T[0:1, :]
+    tile[t, 2:4, 0:128] = qk[3, 0:2, :]
+    for d in range(n_tp - 1):
+        give_tile(d, t).start()
+    for w in weights + [rest]:
+        w.drain()
+    d1.drain()
+    back.drain()
+    back_block.drain()
+
+    @pl.when(t == 0)
+    def _():
+        keep(0).wait()
+
+    @pl.when(t == last)
+    def _():
+        keep(half).wait()
+
+    @pl.when(c == 1)
+    def _():
+        give.wait_send()
+
+    for n in range(3):
+        trade(n).wait_send()
+    for d in range(n_tp - 1):
+        give_tile(d, lax.rem(t + n_tp - d - 1, n_tp)).wait_recv()
+    total = tile[0]
+    for n in range(1, n_tp):
+        total = total + tile[n]
+    small[...] = total
+    for d in range(n_tp - 1):
+        give_tile(d, t).wait_send()
+
+
+def call_c(mesh, chunks, args, kept):
+    (hidden_in, seq_lengths, attn_gain, ffn_gain, query_gain, key_gain,
+     w_query, w_key, w_value, w_gate, w_up) = args
+    (attn_low, rg_own, blk_own, wgrads, wqkv_full, wo_full, heads_all, q_t, kv_all, inv_den,
+     proj_t) = kept
+    n_shard, n_ctx, n_tp = mesh.shape["shard"], mesh.shape["ctx"], mesh.shape["tp"]
+    rows, width = hidden_in.shape
+    half = rows // 2
+    hd = query_gain.shape[0]
+    q_cols, kv_cols = w_query.shape[1], w_key.shape[1]
+    qkv_cols = q_cols + 2 * kv_cols
+    kv_heads = kv_cols // hd
+    block, units = w_gate.shape
+    padded = wgrads.shape[2]
+    cosine, sine = rope_tables(n_ctx * rows, hd)
+    vm = pl.BlockSpec(memory_space=pltpu.VMEM)
+    hbm = pl.BlockSpec(memory_space=pltpu.HBM)
+    sm = pl.BlockSpec(memory_space=pltpu.SMEM)
+    S = jax.ShapeDtypeStruct
+    V = pltpu.VMEM
+    dma = pltpu.SemaphoreType.DMA
+    return pl.pallas_call(
+        functools.partial(kernel_c, (n_shard, n_tp, chunks, hd)),
+        out_shape=(
+            S((rows, width), BF16),
+            S((rows, width), BF16),
+            S((block, q_cols), F32),
+            S((block, kv_cols), F32),
+            S((block, kv_cols), F32),
+            S((block, q_cols), F32),
+            S((block, units), F32),
+            S((block, units), F32),
+            S((block, units), F32),
+            S((8, 256), F32),
+        ),
+        in_specs=[sm] + [vm] * 19 + [hbm] * 4,
+        out_specs=(hbm,) + (vm,) * 9,
+        scratch_shapes=[
+            V((rows, q_cols), BF16),
+            V((width, q_cols), BF16),
+            V((q_cols, rows), BF16),
+            V((8, rows), F32),
+            V((kv_heads, rows, hd), BF16),
+            V((kv_heads, rows, hd), BF16),
+            V((kv_heads, hd, rows), BF16),
+            V((q_cols, rows), F32),
+            V((2 * kv_heads, hd, rows), F32),
+            V((2 * kv_heads, hd, rows), BF16),
+            V((2 * kv_heads, hd, rows), BF16),
+            V((2, hd, rows), F32),
+            V((rows, qkv_cols), BF16),
+            V((rows, width), BF16),
+            V((2, half, width), BF16),
+            V((2, width, rows), BF16),
+            V((width, qkv_cols + q_cols), BF16),
+            V((3, 4, block, padded), BF16),
+            V((3, block, padded), BF16),
+            V((3, 2, block, padded), BF16),
+            V((4, block, qkv_cols + q_cols), BF16),
+            V((block, qkv_cols + q_cols), BF16),
+            V((2, block, qkv_cols + q_cols), BF16),
+            V((block, padded), BF16),
+            V((block, qkv_cols + q_cols), BF16),
+            V((4, block, 128), F32),
+            V((4, 8, 128), F32),
+            V((3, 8, 128), F32),
+            V((n_tp, 8, 256), F32),
+            dma((4, 7)),
+            dma((4, 7)),
+            dma((2, chunks)),
+            dma((2, chunks)),
+            dma((2, chunks)),
+            dma((2, chunks)),
+            dma((2, chunks)),
+            dma((2, chunks)),
+            dma((4,)),
+            dma((4,)),
+            dma((n_tp - 1,)),
+            dma((n_tp - 1,)),
+            dma((5,)),
+        ],
+        compiler_params=pltpu.CompilerParams(
+            collective_id=2, has_side_effects=True, vmem_limit_bytes=VMEM_LIMIT
+        ),
+    )(
+        seq_lengths, attn_low, rg_own, hidden_in, wqkv_full, q_t, kv_all, inv_den, proj_t,
+        attn_gain.reshape(1, -1), ffn_gain.reshape(1, -1), query_gain.reshape(1, -1),
+        key_gain.reshape(1, -1), w_query, w_key, w_value, w_gate, w_up,
+        jnp.asarray(cosine), jnp.asarray(sine), blk_own, wgrads, heads_all, wo_full,
+    )
+
+
+CHUNKS = 8
 
 
 def fast_body(mesh, *args):
     (hidden_in, seq_lengths, attn_gain, ffn_gain, query_gain, key_gain,
      w_query, w_key, w_value, w_out, w_gate, w_up, w_down, out_grad) = args
-    (wqkv_full, wo_full, wg_full, wu_full, wd_full, heads_all, q_t, kv_all, inv_den,
-     proj_t) = call_a(mesh, args[:13])
-    rows = hidden_in.shape[0]
-    hd = query_gain.shape[0]
-    q_cols, kv_cols = w_query.shape[1], w_key.shape[1]
-    kv_heads, q_heads = kv_cols // hd, q_cols // hd
-    group = q_heads // kv_heads
-    scale = 1.0 / math.sqrt(hd)
-    t = lax.axis_index("tp")
-    positions = lax.axis_index("ctx") * rows + jnp.arange(rows, dtype=jnp.int32)
-    length = seq_lengths[0]
-    valid = (positions < length).astype(F32)[:, None]
-    hidden = hidden_in.astype(F32)
-
-    def rms(v):
-        return v * lax.rsqrt(jnp.mean(v * v, axis=-1, keepdims=True) + EPSILON)
-
-    def psum16(v):
-        return lax.psum(v.astype(BF16), "tp").astype(F32)
-
-    resid = hidden + back_product(heads_all, wo_full)
-    h2 = rms(resid).astype(BF16)
-    gate = forward_product(h2, wg_full)
-    up = forward_product(h2, wu_full)
-    middle = activation(gate, up).astype(BF16)
-    ffn = psum16(back_product(middle, wd_full))
-    block_out = (valid * (resid + ffn)).astype(BF16)
-    grad_top = valid * out_grad.astype(F32)
-    grad_low = grad_top.astype(BF16)
-    down_wgrad = outer_product(grad_low, middle)
-    mid_grad = forward_product(grad_low, wd_full)
-    _, pull_act = jax.vjp(activation, gate, up)
-    gate_low, up_low = (v.astype(BF16) for v in pull_act(mid_grad))
-    gate_wgrad = outer_product(h2, gate_low)
-    up_wgrad = outer_product(h2, up_low)
-    d2 = psum16(back_product(gate_low, wg_full) + back_product(up_low, wu_full))
-    _, pull_two = jax.vjp(rms, resid)
-    resid_grad = grad_top + pull_two(d2)[0]
-    attn_low = resid_grad.astype(BF16)
-    heads_own = lax.dynamic_slice_in_dim(heads_all, t * q_cols, q_cols, 1)
-    wo_own = lax.dynamic_slice_in_dim(wo_full, t * q_cols, q_cols, 1)
-    out_wgrad = outer_product(attn_low, heads_own)
-    heads_grad = forward_product(attn_low, wo_own).astype(BF16)
-    delta = jnp.sum(
-        (heads_grad.astype(F32) * heads_own.astype(F32)).reshape(rows, q_heads, hd), -1
-    ).T.reshape(kv_heads, group, 1, rows)
-    keys = kv_all[:, :kv_cols].reshape(-1, kv_heads, hd, rows)
-    values = kv_all[:, kv_cols:].reshape(-1, kv_heads, hd, rows)
-    q4 = q_t.reshape(kv_heads, group, hd, rows)
-    g4 = heads_grad.T.reshape(kv_heads, group, hd, rows)
-    score = jnp.einsum("ckds,kgdt->kgcst", keys, q4, preferred_element_type=F32)
-    pos_k = jnp.arange(keys.shape[0] * rows, dtype=jnp.int32).reshape(-1, rows, 1)
-    mask = (pos_k <= positions) & (pos_k < length)
-    probs = jnp.where(mask, jnp.exp(score), 0.0) * inv_den[:q_heads].reshape(
-        kv_heads, group, 1, 1, rows
-    )
-    prob_grad = jnp.einsum("ckds,kgdt->kgcst", values, g4, preferred_element_type=F32)
-    score_grad = (probs * (prob_grad - delta[:, :, None])).astype(BF16)
-    query_grad = (
-        jnp.einsum("kgcst,ckds->tkgd", score_grad, keys, preferred_element_type=F32) * scale
-    )
-    key_grads = jnp.einsum("kgcst,kgdt->cskd", score_grad, q4, preferred_element_type=F32)
-    value_grads = jnp.einsum(
-        "kgcst,kgdt->cskd", probs.astype(BF16), g4, preferred_element_type=F32
-    )
-    both = jnp.concatenate(
-        [key_grads.reshape(-1, kv_cols), value_grads.reshape(-1, kv_cols)], axis=1
-    )
-    both = lax.psum_scatter(both, "ctx", scatter_dimension=0, tiled=True)
-
-    def query_prep(proj, gain):
-        return head_prep(proj, gain, positions)
-
-    q_gain, k_gain = query_gain.astype(F32), key_gain.astype(F32)
-    proj = proj_t.T
-    _, pull_query = jax.vjp(query_prep, proj[:, :q_cols], q_gain)
-    dq, q_gain_grad = pull_query(query_grad.reshape(rows, q_heads, hd))
-    _, pull_key = jax.vjp(query_prep, proj[:, q_cols : q_cols + kv_cols], k_gain)
-    dk, k_gain_grad = pull_key(both[:, :kv_cols].reshape(rows, kv_heads, hd))
-    dqkv = jnp.concatenate([dq, dk, both[:, kv_cols:]], axis=1).astype(BF16)
-    h1 = rms(hidden).astype(BF16)
-    qkv_wgrad = outer_product(h1, dqkv)
-    d1 = psum16(back_product(dqkv, wqkv_full))
-    _, pull_one = jax.vjp(rms, hidden)
-    input_grad = resid_grad + pull_one(d1)[0]
-    q_sum, k_sum = lax.psum((q_gain_grad, k_gain_grad), ("shard", "ctx", "tp"))
-
-    def scatter(v):
-        v = lax.psum_scatter(
-            v.astype(BF16), ("shard", "ctx"), scatter_dimension=0, tiled=True
-        )
-        return v.astype(F32)
-
-    qkv_g, gate_g, up_g, down_g, out_g = (
-        scatter(v) for v in (qkv_wgrad, gate_wgrad, up_wgrad, down_wgrad, out_wgrad)
-    )
-    g_one, g_two = attn_gain.astype(F32)[:, None], ffn_gain.astype(F32)[:, None]
-    w_one = jnp.concatenate([w_query, w_key, w_value], axis=1).astype(F32)
-    gains = jnp.stack(
-        [
-            jnp.sum(w_one * qkv_g, axis=1),
-            jnp.sum(w_gate.astype(F32) * gate_g + w_up.astype(F32) * up_g, axis=1),
-        ]
-    )
-    gains = lax.psum(gains, "tp")
-    qkv_g = qkv_g * g_one
+    (wqkv_full, wo_full, wg_full, wu_full, heads_all, q_t, kv_all, inv_den,
+     proj_t) = call_a(mesh, args[:12])
+    attn_low, rg_own, blk_own, wgrads = call_b(
+        mesh, CHUNKS, seq_lengths, hidden_in, heads_all, out_grad, w_down, wo_full, wg_full, wu_full
+    )
+    (block_out, inp, g_query, g_key, g_value, g_out, g_gate, g_up, g_down, small) = call_c(
+        mesh, CHUNKS,
+        (hidden_in, seq_lengths, attn_gain, ffn_gain, query_gain, key_gain, w_query, w_key,
+         w_value, w_gate, w_up),
+        (attn_low, rg_own, blk_own, wgrads, wqkv_full, wo_full, heads_all, q_t, kv_all, inv_den,
+         proj_t),
+    )
+    block, hd = w_query.shape[0], query_gain.shape[0]
     return (
-        block_out, input_grad, gains[0], gains[1], q_sum, k_sum,
-        qkv_g[:, :q_cols], qkv_g[:, q_cols : q_cols + kv_cols], qkv_g[:, q_cols + kv_cols :],
-        out_g.T, gate_g * g_two, up_g * g_two, down_g.T,
+        block_out, inp.astype(F32), small[0, :block], small[1, :block], small[2, :hd],
+        small[3, :hd], g_query, g_key, g_value, g_out.T, g_gate, g_up, g_down.T,
     )
 
 

time: 845 us -> 425 us (0.50)
  waiting for transfers between devices: 428 us -> 0 us
  Pallas kernels: 124 us -> 406 us
  matrix products: 160 us -> 0 us
  blocking collectives: 51.3 us -> 0 us
  other arithmetic: 37.1 us -> 4.65 us
  between operations: 15.8 us -> 1.35 us
  local copies, waits for them, and re-layouts: 23 us -> 12.4 us
    pallas_call x0 -> x2, Pallas kernels: none -> 304 us  [the longest x1 152 us: call_c(): pl.pallas_call(functools.partial(kernel_c, (n_shard, n_tp, chunks, hd)),...]
    psum x2 -> x0, waiting for transfers between devices: 217 us -> none  [psum16(): return lax.psum(v.astype(BF16), 'tp').astype(F32)]
    reduce_scatter x6 -> x0, waiting for transfers between devices: 211 us -> none  [the longest x5 206 us: scatter(): lax.psum_scatter(v.astype(BF16), ('shard', 'ctx'), scatter_dimension=0, t...]
    dot_general x19 -> x0, matrix products: 160 us -> none  [the longest x5 36.5 us: back_product(): lax.dot_general(grad, weight, (((1,), (1,)), ((), ())), preferred_element...]
    psum x2 -> x0, blocking collectives: 51.3 us -> none  [the longest x1 39.6 us: fast_body(): q_sum, k_sum = lax.psum((q_gain_grad, k_gain_grad), ('shard', 'ctx', 'tp'))]
    pallas_call x1, Pallas kernels: 124 us -> 101 us  [call_a(): pl.pallas_call(functools.partial(kernel_a, (n_shard, n_tp, hd)), out_shap...]
    reduce_sum x7 -> x0, other arithmetic: 11.3 us -> none  [the longest x2 6.43 us: rms(): return v * lax.rsqrt(jnp.mean(v * v, axis=-1, keepdims=True) + EPSILON)]
  transfers between devices with their start and end apart: 8 -> 0, of which waited for: 8 -> 0; matrix products, arithmetic and copies ran while one was open for 11% -> 0% of each run, Pallas kernels for 0% -> 0%
where the time goes in v2:
time: 425 us; the launch traced here: 424 us
  Pallas kernels  406 us (96%)
  local copies, waits for them, and re-layouts  12.4 us (3%)
  other arithmetic  4.65 us (1%)
    pallas_call x1, Pallas kernels, call_c(): pl.pallas_call(functools.partial(kernel_c, (n_shard, n_tp, chunks, hd)),...  152 us
    pallas_call x1, Pallas kernels, call_b(): pl.pallas_call(functools.partial(kernel_b, (n_shard, n_tp, chunks)), out_...  152 us
    pallas_call x1, Pallas kernels, call_a(): pl.pallas_call(functools.partial(kernel_a, (n_shard, n_tp, hd)), out_shap...  101 us

profile of v2, /device:TPU:0, one launch (start us, length us, event | category | flops | bytes accessed | tf_op | source)
XLA Modules:
  0.0 423.9 jit_solution(8547837631436113334)
XLA Ops:
  1.3 1.2 reshape.42.gain_one_ref
  2.5 1.2 reshape.43.gain_two_ref
  3.7 101.4 %shard_map.273 = (bf16[1536,640]{1,0:T(8,128)(2,1)}, bf16[1536,1536]{1,0:T(8,128)(2,1)}, bf16[1536,1792]{1,0:T(8,128)(2,1)}, bf16[1536,1792]{1,0:T(8,128)(2,1)},...) custom-call(s32[1]{0:T(128)S(6)} %copy.39.length_ref, ...), custom_call_target="tpu_custom_call" | custom-call | tf_op jit(solution)/shard_map/pallas_call | solution.py:760
  105.2 151.6 %shard_map.274 = (bf16[768,1536]{1,0:T(8,128)(2,1)}, f32[384,1536]{1,0:T(8,128)}, bf16[384,1536]{1,0:T(8,128)(2,1)}, bf16[3,1536,1792]{2,1,0:T(8,128)(2,1)}) custom-call(s32[1]{0:T(128)S(6)} %copy.39.length_ref, bf16[768,1536]{1,0:T(8,128)(2,1)} %hid_ref.5, bf16[768,1536]{1,0:T(8,128)(2,1)} %get-tuple-element.36.heads_ref.heads_hbm, ...), custom_call_target="tpu_custom_call" | custom-call | tf_op jit(solution)/shard_map/pallas_call | solution.py:1147
  256.8 152.5 %shard_map.275 = (bf16[768,1536]{1,0:T(8,128)(2,1)}, bf16[768,1536]{1,0:T(8,128)(2,1)}, f32[192,384]{1,0:T(8,128)}, f32[192,128]{1,0:T(8,128)}, f32[192,128]{1,0...) custom-call(s32[1]{0:T(128)S(6)} %copy.39.length_ref, ...), custom_call_target="tpu_custom_call" | custom-call | tf_op jit(solution)/shard_map/pallas_call | solution.py:1717
  409.3 1.3 slice_bitcast_fusion
  410.5 1.3 fusion
  411.9 0.0 copy-start
  411.9 4.6 %convert_element_type.3 = f32[768,1536]{1,0:T(8,128)} convert(bf16[768,1536]{1,0:T(8,128)(2,1)} %get-tuple-element.50) | non-fusion elementwise | flops 1179648 | bytes 7077888 | tf_op jit(solution)/shard_map/convert_element_type | solution.py:1808
  416.5 0.0 copy-done
  416.5 0.0 copy-start.5
  416.5 0.0 copy-start.7
  416.5 0.0 copy-start.6
  416.5 0.0 copy-start.4
  416.6 0.0 copy-start.3
  416.6 1.4 copy.40
  418.0 0.0 copy-done.5
  418.0 0.0 copy-start.2
  418.0 0.7 copy.41
  418.7 0.0 copy-done.7
  418.7 0.6 copy.42
  419.3 0.0 copy-done.6
  419.3 0.6 copy.43
  420.0 0.0 copy-done.4
  420.0 0.7 copy.44
  420.7 0.0 copy-done.3
  420.7 0.0 copy-start.1
  420.7 1.1 copy.45
  421.8 0.0 copy-done.2
  421.8 1.1 copy.46
  422.9 0.0 copy-done.1
  422.9 1.1 copy.47
Async XLA Ops:
  411.9 4.7 %copy-start = (bf16[768,1536]{1,0:T(8,128)(2,1)S(1)}, bf16[768,1536]{1,0:T(8,128)(2,1)}, u32[]{:S(2)}) copy-start(bf16[768,1536]{1,0:T(8,128)(2,1)} %get-tuple-element.76) | copy-start | bytes 7077892
  416.5 1.4 copy-start.5
  416.5 2.2 copy-start.7
  416.5 2.8 copy-start.6
  416.5 3.4 copy-start.4
  416.6 4.1 copy-start.3
  418.0 3.8 copy-start.2
  420.7 2.2 copy-start.1

commit v3 on v2

--- a/solution.py
+++ b/solution.py
@@ -392,13 +392,15 @@
 
 
 class Gather:
-    def __init__(self, at, own, full, send, recv, index):
+    def __init__(self, at, own, full, send, recv, index, stride=0, first=0):
         self.at, self.own, self.full = at, own, full
         self.send, self.recv, self.index = send, recv, index
-        self.rows = own.shape[0]
+        self.rows, self.first = own.shape[0], first
+        self.stride = stride or self.rows
 
     def block(self, slot):
-        return self.full.at[pl.ds(pl.multiple_of(slot * self.rows, self.rows), self.rows)]
+        start = slot * self.stride + self.first
+        return self.full.at[pl.ds(pl.multiple_of(start, self.rows), self.rows)]
 
     def copy(self, role, src, slot, dev):
         k = ROLES.index(role)
@@ -468,21 +470,30 @@
     wo_ref,
     wg_ref,
     wu_ref,
+    wd_ref,
     cos_ref,
     sin_ref,
     wqkv_full,
     wo_full,
     wg_full,
     wu_full,
+    wd_full,
     heads_all,
     q_t,
     kv_all,
     inv_den,
     proj_t,
+    resid,
+    h2,
+    act_out,
     s_qkv,
     s_woz,
     s_wg,
     s_wu,
+    s_wd,
+    wg,
+    wu,
+    act,
     h1,
     k_own,
     k_off,
@@ -497,6 +508,7 @@
     h_recv,
     kv_sem,
     loc_sem,
+    act_sem,
 ):
     n_shard, n_tp, hd = shape
     at = Place(n_shard, n_tp)
@@ -516,10 +528,15 @@
     out = Gather(at, s_woz, wo_full, g_send, g_recv, 1)
     gate = Gather(at, s_wg, wg_full, g_send, g_recv, 2)
     up = Gather(at, s_wu, wu_full, g_send, g_recv, 3)
-    gathers = (qkv, out, gate, up)
+    down = Gather(at, s_wd, wd_full, g_send, g_recv, 4)
+    gathers = (qkv, out, gate, up, down)
     local = [
         pltpu.make_async_copy(g.own, g.block(at.own), loc_sem.at[i])
         for i, g in enumerate(gathers)
+    ]
+    loads = [
+        pltpu.make_async_copy(wg_full, wg, loc_sem.at[5]),
+        pltpu.make_async_copy(wu_full, wu, loc_sem.at[6]),
     ]
     qkv.start()
     local[0].start()
@@ -554,11 +571,12 @@
     for src, dst in ((wg_ref, s_wg), (wu_ref, s_wu)):
         dst[:, 0:units] = (src[...].astype(F32) * col_two).astype(BF16)
         dst[:, units:] = jnp.zeros((dst.shape[0], dst.shape[1] - units), BF16)
+    s_wd[:, 0:units] = wd_ref[...]
+    s_wd[:, units:] = jnp.zeros((s_wd.shape[0], s_wd.shape[1] - units), BF16)
     qkv.relay_last()
     for d in range(n_tp - 1):
         wo_part(d, lax.rem(t + n_tp - d - 1, n_tp)).wait_recv()
-    out.start_y()
-    out.start_s()
+    out.start()
     gate.start_y()
     local[0].wait()
     for cp in local[1:]:
@@ -596,7 +614,6 @@
     def _():
         kv_copy.start()
 
-    out.start_x()
     gate.start_x()
     gate.start_s()
 
@@ -639,6 +656,8 @@
         return 0
 
     lax.fori_loop(0, q_heads, own_block, 0)
+    out.relay()
+    up.start()
 
     @pl.when(c == 1)
     def _():
@@ -655,9 +674,6 @@
             return 0
 
         lax.fori_loop(0, q_heads, other_block, 0)
-
-    out.relay()
-    up.start()
 
     def chunk_cols(owner, j):
         return pl.ds(pl.multiple_of(owner * q_cols + j * 128, 128), 128)
@@ -706,13 +722,76 @@
                 out.relay_last()
             if step == 7:
                 up.relay()
-
-    gate.relay_last()
+                down.start()
+
+    out.finish()
+    local[1].wait()
+
+    def residual(i, _):
+        r = pl.ds(pl.multiple_of(i * 128, 128), 128)
+        x = hid_ref[r, :].astype(F32) + mm_nt(heads_all[r, :], wo_full[...])
+        resid[r, :] = x
+        scale = lax.rsqrt(jnp.mean(x * x, axis=-1, keepdims=True) + EPSILON)
+        h2[r, :] = (x * scale).astype(BF16)
+
+        @pl.when(i == 1)
+        def _():
+            gate.relay_last()
+
+        @pl.when(i == 3)
+        def _():
+            gate.finish()
+            local[2].wait()
+            loads[0].start()
+
+        return 0
+
+    lax.fori_loop(0, rows // 128, residual, 0)
     up.relay_last()
-    for g in gathers[1:]:
-        g.finish()
-    for cp in local[1:]:
-        cp.wait()
+    up.finish()
+    local[3].wait()
+    loads[1].start()
+    loads[0].wait()
+    loads[1].wait()
+    tiles = act.shape[2] // 256
+    half = rows // 2
+
+    def act_copy(f):
+        cols = pl.ds(pl.multiple_of(f * 256, 256), 256)
+        return pltpu.make_async_copy(
+            act.at[:, :, cols], act_out.at[:, :, cols], act_sem.at[f]
+        )
+
+    def gate_up(f, _):
+        cols = pl.ds(pl.multiple_of(f * 256, 256), 256)
+        for i in (0, 1):
+            r = slice(i * half, (i + 1) * half)
+            g = mm(h2[r, :], wg[:, cols])
+            u = mm(h2[r, :], wu[:, cols])
+            s = 1.0 / (1.0 + jnp.exp(-g))
+            silu = g * s
+            act[0, r, cols] = (silu * u).astype(BF16)
+            act[1, r, cols] = (u * (s * (1.0 + g * (1.0 - s)))).astype(BF16)
+            act[2, r, cols] = silu.astype(BF16)
+
+        act_copy(f).start()
+
+        @pl.when(f == tiles - 2)
+        def _():
+            down.relay()
+
+        return 0
+
+    lax.fori_loop(0, tiles, gate_up, 0)
+    down.relay_last()
+    down.finish()
+    local[4].wait()
+
+    def act_done(f, _):
+        act_copy(f).wait()
+        return 0
+
+    lax.fori_loop(0, tiles, act_done, 0)
     for owner in range(n_tp):
         for j in range(chunks):
 
@@ -741,7 +820,7 @@
 
 def call_a(mesh, args):
     (hidden_in, seq_lengths, attn_gain, ffn_gain, query_gain, key_gain,
-     w_query, w_key, w_value, w_out, w_gate, w_up) = args
+     w_query, w_key, w_value, w_out, w_gate, w_up, w_down) = args
     n_shard, n_ctx, n_tp = mesh.shape["shard"], mesh.shape["ctx"], mesh.shape["tp"]
     rows, width = hidden_in.shape
     hd = query_gain.shape[0]
@@ -764,33 +843,42 @@
             S((width, n_tp * q_cols), BF16),
             S((width, padded), BF16),
             S((width, padded), BF16),
+            S((width, padded), BF16),
             S((rows, n_tp * q_cols), BF16),
             S((q_cols, rows), BF16),
             S((n_ctx, 2 * kv_cols, rows), BF16),
             S((8, rows), F32),
             S((qkv_cols, rows), F32),
+            S((rows, width), F32),
+            S((rows, width), BF16),
+            S((3, rows, padded), BF16),
         ),
-        in_specs=[sm] + [vm] * 13,
-        out_specs=(vm, hbm, hbm, hbm, vm, vm, vm, vm, vm),
+        in_specs=[sm] + [vm] * 14,
+        out_specs=(vm, vm, hbm, hbm, hbm, vm, vm, vm, vm, vm, vm, vm, hbm),
         scratch_shapes=[
             pltpu.VMEM((block, qkv_cols), BF16),
             pltpu.VMEM((block, n_tp * q_cols), BF16),
             pltpu.VMEM((block, padded), BF16),
             pltpu.VMEM((block, padded), BF16),
+            pltpu.VMEM((block, padded), BF16),
+            pltpu.VMEM((width, padded), BF16),
+            pltpu.VMEM((width, padded), BF16),
+            pltpu.VMEM((3, rows, padded), BF16),
             pltpu.VMEM((rows, width), BF16),
             pltpu.VMEM((kv_heads, rows, hd), BF16),
             pltpu.VMEM((kv_heads, rows, hd), BF16),
             pltpu.VMEM((kv_heads, hd + 16, rows), BF16),
             pltpu.VMEM((kv_heads, hd + 16, rows), BF16),
             pltpu.VMEM((q_heads, hd + 16, rows), F32),
-            dma((4, 7)),
-            dma((4, 7)),
+            dma((5, 7)),
+            dma((5, 7)),
             dma((n_tp - 1,)),
             dma((n_tp - 1,)),
             dma((2, n_tp, chunks)),
             dma((2, n_tp, chunks)),
             dma((2,)),
-            dma((4,)),
+            dma((7,)),
+            dma((padded // 256,)),
         ],
         compiler_params=pltpu.CompilerParams(
             collective_id=0, has_side_effects=True, vmem_limit_bytes=VMEM_LIMIT
@@ -798,8 +886,11 @@
     )(
         seq_lengths, hidden_in, attn_gain.reshape(1, -1), ffn_gain.reshape(1, -1),
         query_gain.reshape(1, -1), key_gain.reshape(1, -1), w_query, w_key, w_value,
-        w_out.T, w_gate, w_up, jnp.asarray(cosine), jnp.asarray(sine),
-    )
+        w_out.T, w_gate, w_up, w_down.T, jnp.asarray(cosine), jnp.asarray(sine),
+    )
+
+
+LAG = 2
 
 
 class Line:
@@ -836,7 +927,7 @@
     def reduce(self, step, final):
         for way in (0, 1):
             pos = self.pos(way)
-            k = step - pos
+            k = step - pos * LAG
             live = jnp.logical_and(k >= 0, k < self.chunks)
 
             @pl.when(jnp.logical_and(live, pos > 0))
@@ -877,14 +968,14 @@
     def copy(self, way, k, first=False):
         line = self.line
         dst = self.whole.at[line.rows(way, k)]
-        src = self.source.at[line.local(k)] if first and self.source is not None else dst
+        src = self.source.at[way, line.local(k)] if first and self.source is not None else dst
         return remote(src, dst, self.send.at[way, k], self.recv.at[way, k], line.dev(way, -1))
 
     def step(self, step):
         line = self.line
         for way in (0, 1):
             pos = line.pos(way)
-            k = step - (line.last - pos)
+            k = step - (line.last - pos) * LAG
             live = jnp.logical_and(k >= 0, k < line.chunks)
 
             @pl.when(jnp.logical_and(live, pos < line.last))
@@ -912,21 +1003,126 @@
                 lax.fori_loop(0, line.chunks, one, 0)
 
 
+class Scatter:
+    def __init__(self, at, source, room, tmp_sem, send, recv, index):
+        self.at, self.source, self.room = at, source, room
+        self.tmp_sem, self.send, self.recv, self.index = tmp_sem, send, recv, index
+        self.rows = room.shape[0] // 8
+        self.tmp, self.relayed = self.land(7), self.land(4)
+        self.final = (self.land(5), self.land(6))
+        self.direct, self.indirect = 1 + at.core, 2 - at.core
+        self.other = (
+            at.core * at.x[0] + (1 - at.core) * at.y[0],
+            at.core * at.x[1] + (1 - at.core) * at.y[1],
+            at.t,
+        )
+        self.mine = [at.own] + [at.slots[n] for n in ("X", "Y", "D")]
+        self.theirs = [at.slots[n] for n in ("S", "SX", "SY", "SD")]
+
+    def land(self, j):
+        return self.room.at[pl.ds(pl.multiple_of(j * self.rows, self.rows), self.rows)]
+
+    def block(self, slot):
+        return self.source.at[pl.ds(pl.multiple_of(slot * self.rows, self.rows), self.rows)]
+
+    def copy(self, k, src, dst, dev):
+        return remote(src, dst, self.send.at[self.index, k], self.recv.at[self.index, k], dev)
+
+    def share(self, j):
+        return self.copy(j, self.block(self.theirs[j]), self.land(j), self.at.sib)
+
+    def start(self):
+        for j in (3, 1, 2, 0):
+            self.share(j).start()
+
+    def slot(self, j):
+        if isinstance(j, int):
+            return self.mine[j]
+        return jnp.where(j == 1, self.mine[1], self.mine[2])
+
+    def arrived(self, j):
+        ref = self.land(j)
+        self.copy(j, ref, ref, self.at.sib).wait_recv()
+
+    def fetch(self, j):
+        return pltpu.make_async_copy(self.block(self.slot(j)), self.tmp, self.tmp_sem)
+
+    def add(self, j, extra=()):
+        self.fetch(j).start()
+        self.arrived(j)
+        self.fetch(j).wait()
+        land = self.land(j)
+
+        def piece(i, _):
+            r = pl.ds(pl.multiple_of(i * 64, 64), 64)
+            value = land[r, :].astype(F32) + self.tmp[r, :].astype(F32)
+            for ref in extra:
+                value += ref[r, :].astype(F32)
+            land[r, :] = value.astype(BF16)
+            return 0
+
+        lax.fori_loop(0, self.rows // 64, piece, 0)
+
+    def hop(self, k):
+        at = self.at
+        if k == 4:
+            return self.copy(4, self.land(3), self.relayed, at.relay)
+        if k == 5:
+            return self.copy(5, self.land(self.direct), self.final[0], at.relay)
+        return self.copy(6, self.land(self.indirect), self.final[1], self.other)
+
+    def first(self):
+        self.add(3)
+        self.hop(4).start()
+        self.add(self.direct)
+        self.hop(5).start()
+
+    def second(self):
+        self.hop(4).wait_recv()
+        self.add(self.indirect, (self.relayed,))
+        self.hop(6).start()
+
+    def finish(self, use):
+        self.fetch(0).start()
+        self.arrived(0)
+        self.hop(5).wait_recv()
+        self.hop(6).wait_recv()
+        self.fetch(0).wait()
+        land = self.land(0)
+
+        def piece(i, _):
+            r = pl.ds(pl.multiple_of(i * 64, 64), 64)
+            value = land[r, :].astype(F32) + self.tmp[r, :].astype(F32)
+            value += self.final[0][r, :].astype(F32) + self.final[1][r, :].astype(F32)
+            use(r, value)
+            return 0
+
+        lax.fori_loop(0, self.rows // 64, piece, 0)
+
+    def drain(self):
+        for j in range(4):
+            self.share(j).wait_send()
+        for k in (4, 5, 6):
+            self.hop(k).wait_send()
+
+
 def kernel_b(
     shape,
     length_ref,
-    hid_ref,
-    heads_ref,
     og_ref,
-    wd_ref,
-    wo_hbm,
+    wd_hbm,
+    act_hbm,
     wg_hbm,
     wu_hbm,
+    h2_hbm,
+    resid_hbm,
     attn_low,
     rg_own,
-    blk_own,
+    gate_sum,
+    ffn_part,
     wgrads,
-    wo,
+    f_part,
+    d_part,
     wg,
     wu,
     wd,
@@ -934,39 +1130,33 @@
     h2,
     gl,
     act,
-    land_f,
     land_d,
     stage,
-    g_send,
-    g_recv,
-    f_send,
-    f_recv,
     d_send,
     d_recv,
     b_send,
     b_recv,
+    s_send,
+    s_recv,
     loc_sem,
     st_sem,
+    free_sem,
 ):
     n_shard, n_tp, chunks = shape
     at = Place(n_shard, n_tp)
-    rows, width = hid_ref.shape
-    units, padded = wd_ref.shape[1], wd.shape[1]
-    block = wd_ref.shape[0]
+    rows, width = og_ref.shape
+    padded = wd.shape[1]
+    block = stage.shape[1]
     half = rows // 2
     tiles = padded // 256
+    last = n_tp - 1
+    pairs = ((wd_hbm, wd), (act_hbm, act), (wg_hbm, wg), (wu_hbm, wu), (h2_hbm, h2), (resid_hbm, resid))
     loads = [
-        pltpu.make_async_copy(src, dst, loc_sem.at[i])
-        for i, (src, dst) in enumerate(((wo_hbm, wo), (wg_hbm, wg), (wu_hbm, wu)))
+        pltpu.make_async_copy(src, dst, loc_sem.at[i]) for i, (src, dst) in enumerate(pairs)
     ]
     for cp in loads:
         cp.start()
-    own = pl.ds(pl.multiple_of(at.own * block, block), block)
-    wd[own, 0:units] = wd_ref[...]
-    wd[own, units:] = jnp.zeros((block, padded - units), BF16)
     at.greet()
-    down = Gather(at, wd.at[own], wd, g_send, g_recv, 0)
-    down.start()
     length = length_ref[0]
 
     def live_rows(start, n):
@@ -981,93 +1171,82 @@
 
     lax.fori_loop(0, rows // 64, mask_grad, 0)
     loads[0].wait()
-
-    def residual(i, _):
-        r = pl.ds(pl.multiple_of(i * 128, 128), 128)
-        x = hid_ref[r, :].astype(F32) + mm_nt(heads_ref[r, :], wo[...])
-        resid[r, :] = x
-        scale = lax.rsqrt(jnp.mean(x * x, axis=-1, keepdims=True) + EPSILON)
-        h2[r, :] = (x * scale).astype(BF16)
-        return 0
-
-    lax.fori_loop(0, rows // 128, residual, 0)
     loads[1].wait()
-    loads[2].wait()
-
-    def gate_up(f, _):
-        cols = pl.ds(pl.multiple_of(f * 256, 256), 256)
-        for i in (0, 1):
-            r = slice(i * half, (i + 1) * half)
-            g = mm(h2[r, :], wg[:, cols])
-            u = mm(h2[r, :], wu[:, cols])
-            s = 1.0 / (1.0 + jnp.exp(-g))
-            silu = g * s
-            act[0, r, cols] = (silu * u).astype(BF16)
-            act[1, r, cols] = (u * (s * (1.0 + g * (1.0 - s)))).astype(BF16)
-            act[2, r, cols] = silu.astype(BF16)
-
-        @pl.when(f == 2)
-        def _():
-            down.relay()
-
-        @pl.when(f == tiles - 1)
-        def _():
-            down.relay_last()
-
-        return 0
-
-    lax.fori_loop(0, tiles, gate_up, 0)
-    down.finish()
-
-    f_part, d_part = wo.at[0:rows], wo.at[rows:]
+
     quarter = half // 2
-    ffn = Line(at, f_part, land_f, f_send, f_recv, chunks)
-    d2 = Line(at, d_part, land_d, d_send, d_recv, chunks)
-    back = Back(d2, attn_low, b_send, b_recv)
-
-    def final_ffn(way, k, value):
-        r = ffn.rows(way, k)
-        x = resid[r, :] + value
-        live = live_rows((1 - way) * half + k * ffn.size, ffn.size)
-        blk_own[ffn.local(k), :] = (x * live).astype(BF16)
-
-    def final_d2(way, k, value):
-        r = d2.rows(way, k)
-        x = resid[r, :]
-        scale = lax.rsqrt(jnp.mean(x * x, axis=-1, keepdims=True) + EPSILON)
-        h = x * scale
-        inner = jnp.mean(value * h, axis=-1, keepdims=True)
-        grad = gl[r, :].astype(F32) + scale * (value - h * inner)
-        rg_own[d2.local(k), :] = grad
-        attn_low[r, :] = grad.astype(BF16)
-
-    order = (0, 2, 1, 3)
-    for q in order:
-        r = slice(q * quarter, (q + 1) * quarter)
-        f_part[r, :] = mm_nt(act[0, r, :], wd[...]).astype(BF16)
-
-    def mid(f, _):
-        cols = pl.ds(pl.multiple_of(f * 256, 256), 256)
-        for i in (0, 1):
-            r = slice(i * half, (i + 1) * half)
+    lines, backs = [], []
+    for n in (0, 1):
+        r = pl.ds(n * half, half)
+        line = Line(at, d_part.at[r], land_d.at[n], d_send.at[n], d_recv.at[n], chunks)
+        lines.append(line)
+        backs.append(Back(line, attn_low.at[r], b_send.at[n], b_recv.at[n]))
+
+    def final_d2(n):
+        def final(way, k, value):
+            line = lines[n]
+            start = n * half + (1 - way) * quarter + k * line.size
+            r = pl.ds(pl.multiple_of(start, line.size), line.size)
+            x = resid[r, :]
+            scale = lax.rsqrt(jnp.mean(x * x, axis=-1, keepdims=True) + EPSILON)
+            h = x * scale
+            inner = jnp.mean(value * h, axis=-1, keepdims=True)
+            grad = gl[r, :].astype(F32) + scale * (value - h * inner)
+            rg_own[pl.ds(pl.multiple_of(n * quarter + k * line.size, line.size), line.size), :] = grad
+            attn_low[r, :] = grad.astype(BF16)
+
+        return final
+
+    def move(n, step):
+        lines[n].reduce(step, final_d2(n))
+        backs[n].step(step - last * LAG)
+
+    def moves(n, slot):
+        for i in range(LAG):
+            move(n, slot * LAG + i)
+
+    def mid(n):
+        r = slice(n * half, (n + 1) * half)
+
+        def one(f, _):
+            cols = pl.ds(pl.multiple_of(f * 256, 256), 256)
             g = mm(gl[r, :], wd[:, cols])
             act[1, r, cols] = (g * act[1, r, cols].astype(F32)).astype(BF16)
             act[2, r, cols] = (g * act[2, r, cols].astype(F32)).astype(BF16)
-
-        @pl.when(lax.rem(f, 3) == 0)
-        def _():
-            ffn.reduce(lax.div(f, 3), final_ffn)
-
-        return 0
-
-    lax.fori_loop(0, tiles, mid, 0)
-    done = -(-tiles // 3)
-    for n, q in enumerate(order):
+            if n == 1:
+
+                @pl.when(lax.rem(f, 4) == 2)
+                def _():
+                    moves(0, 1 + lax.div(f, 4))
+
+            return 0
+
+        lax.fori_loop(0, tiles, one, 0)
+
+    def back_part(q):
         r = slice(q * quarter, (q + 1) * quarter)
         total = mm_nt(act[1, r, :], wg[...]) + mm_nt(act[2, r, :], wu[...])
         d_part[r, :] = total.astype(BF16)
-        ffn.reduce(done + n, final_ffn)
-    done += len(order)
+
+    mid(0)
+    for cp in loads[2:]:
+        cp.wait()
+    back_part(0)
+    back_part(1)
+    moves(0, 0)
+    mid(1)
+    done = 1 + (tiles + 1) // 4
+    back_part(2)
+    moves(0, done)
+    back_part(3)
+    done = (done + 1) * LAG
+
+    peers = (at.sib, at.x, at.y)
+    for n, peer in enumerate(peers):
+        pl.semaphore_signal(free_sem.at[n], inc=1, device_id=peer, device_id_type=MESH)
+    gate = Scatter(at, wgrads.at[1], wg, loc_sem.at[0], s_send, s_recv, 0)
+
+    def free(n):
+        pl.semaphore_wait(free_sem.at[n], 1)
 
     def turn(i, _):
         r = pl.ds(pl.multiple_of(i * 128, 128), 128)
@@ -1076,22 +1255,22 @@
         wu[:, r2] = gl[r, :].T
         return 0
 
-    last = n_tp - 1
-    per_step = 2
-    count = 3 * (width // block)
+    blocks = width // block
+    per_step = -(-3 // LAG)
+    count = 3 * blocks
+    def weight_of(n):
+        return lax.rem(lax.div(n, blocks) + 1, 3)
 
     def stage_copy(n):
-        a, w = lax.div(n, width // block), lax.rem(n, width // block)
-        slot = lax.rem(n, 2)
+        w, slot = lax.rem(n, blocks), lax.rem(n, 2)
         return pltpu.make_async_copy(
             stage.at[slot],
-            wgrads.at[a, pl.ds(pl.multiple_of(w * block, block), block)],
+            wgrads.at[weight_of(n), pl.ds(pl.multiple_of(w * block, block), block)],
             st_sem.at[slot],
         )
 
     def weight_grad(n):
-        a, w = lax.div(n, width // block), lax.rem(n, width // block)
-        slot = lax.rem(n, 2)
+        a, w, slot = weight_of(n), lax.rem(n, blocks), lax.rem(n, 2)
 
         @pl.when(n >= 2)
         def _():
@@ -1104,13 +1283,36 @@
             stage[slot, :, cols] = mm(left, act[a, :, cols]).astype(BF16)
         stage_copy(n).start()
 
+    keeps = pltpu.make_async_copy(f_part, ffn_part, loc_sem.at[1])
+
+    def forward_part(q):
+        r = pl.ds(pl.multiple_of(q * quarter, quarter), quarter)
+        total = mm_nt(act[0, r, :], wd[...])
+        mine = (at.t == lax.rem(q, 2) * last).astype(F32)
+        f_part[r, :] = (total + resid[r, :] * mine).astype(BF16)
+
+    def use_gate(r, value):
+        gate_sum[r, :] = value.astype(BF16)
+
+    def start_gate():
+        free(0)
+        gate.start()
+
+    def first_gate():
+        free(1)
+        free(2)
+        gate.first()
+
+    events = {
+        3: start_gate,
+        4: first_gate,
+        7: gate.second,
+        9: lambda: gate.finish(use_gate),
+    }
+
     def tail(step, _):
-        @pl.when(step + done < chunks + last)
-        def _():
-            ffn.reduce(step + done, final_ffn)
-
-        d2.reduce(step, final_d2)
-        back.step(step - last)
+        move(0, step + done)
+        move(1, step)
 
         @pl.when(step == 0)
         def _():
@@ -1122,21 +1324,34 @@
             def _():
                 weight_grad(step * per_step + n)
 
+        for when, todo in events.items():
+
+            @pl.when(step == when * LAG)
+            def _():
+                todo()
+
+        @pl.when(jnp.logical_and(step >= 6 * LAG, step < 6 * LAG + 4))
+        def _():
+            forward_part(step - 6 * LAG)
+
         return 0
 
-    steps = max(chunks + 2 * last, -(-count // per_step), chunks + last - done)
+    steps = max(chunks + 2 * last * LAG, 9 * LAG + 1, 6 * LAG + 4, -(-count // per_step))
     lax.fori_loop(0, steps, tail, 0)
+    keeps.start()
     stage_copy(count - 2).wait()
     stage_copy(count - 1).wait()
-    ffn.drain()
-    d2.drain()
-    back.drain()
-
-
-def call_b(mesh, chunks, seq_lengths, hidden_in, heads_all, out_grad, w_down, wo_full, wg_full, wu_full):
+    gate.drain()
+    for n in (0, 1):
+        lines[n].drain()
+        backs[n].drain()
+    keeps.wait()
+
+
+def call_b(mesh, chunks, seq_lengths, out_grad, wd_full, act, wg_full, wu_full, h2, resid):
     n_shard, n_tp = mesh.shape["shard"], mesh.shape["tp"]
-    rows, width = hidden_in.shape
-    block = w_down.shape[1]
+    rows, width = out_grad.shape
+    block = width // (n_shard * mesh.shape["ctx"])
     padded = wg_full.shape[1]
     half = rows // 2
     vm = pl.BlockSpec(memory_space=pltpu.VMEM)
@@ -1149,13 +1364,15 @@
         out_shape=(
             S((rows, width), BF16),
             S((half, width), F32),
-            S((half, width), BF16),
+            S((block, padded), BF16),
+            S((rows, width), BF16),
             S((3, width, padded), BF16),
         ),
-        in_specs=[sm] + [vm] * 4 + [hbm] * 3,
-        out_specs=(vm, vm, vm, hbm),
+        in_specs=[sm, vm] + [hbm] * 6,
+        out_specs=(vm, vm, vm, hbm, hbm),
         scratch_shapes=[
-            pltpu.VMEM((width, width), BF16),
+            pltpu.VMEM((rows, width), BF16),
+            pltpu.VMEM((rows, width), BF16),
             pltpu.VMEM((width, padded), BF16),
             pltpu.VMEM((width, padded), BF16),
             pltpu.VMEM((width, padded), BF16),
@@ -1163,124 +1380,22 @@
             pltpu.VMEM((rows, width), BF16),
             pltpu.VMEM((rows, width), BF16),
             pltpu.VMEM((3, rows, padded), BF16),
-            pltpu.VMEM((2, half, width), BF16),
-            pltpu.VMEM((2, half, width), BF16),
+            pltpu.VMEM((2, 2, half // 2, width), BF16),
             pltpu.VMEM((2, block, padded), BF16),
+            dma((2, 2, chunks)),
+            dma((2, 2, chunks)),
+            dma((2, 2, chunks)),
+            dma((2, 2, chunks)),
             dma((1, 7)),
             dma((1, 7)),
-            dma((2, chunks)),
-            dma((2, chunks)),
-            dma((2, chunks)),
-            dma((2, chunks)),
-            dma((2, chunks)),
-            dma((2, chunks)),
-            dma((3,)),
+            dma((6,)),
             dma((2,)),
+            pltpu.SemaphoreType.REGULAR((3,)),
         ],
         compiler_params=pltpu.CompilerParams(
             collective_id=1, has_side_effects=True, vmem_limit_bytes=VMEM_LIMIT
         ),
-    )(seq_lengths, hidden_in, heads_all, out_grad, w_down.T, wo_full, wg_full, wu_full)
-
-
-class Scatter:
-    def __init__(self, at, source, land, relayed, final, tmp, tmp_sem, send, recv, index):
-        self.at, self.source, self.land = at, source, land
-        self.relayed, self.final = relayed, final
-        self.tmp, self.tmp_sem = tmp, tmp_sem
-        self.send, self.recv, self.index = send, recv, index
-        self.rows = land.shape[1]
-        self.direct, self.indirect = 1 + at.core, 2 - at.core
-        self.other = (
-            at.core * at.x[0] + (1 - at.core) * at.y[0],
-            at.core * at.x[1] + (1 - at.core) * at.y[1],
-            at.t,
-        )
-        names = (("own", "X", "Y", "D"), ("S", "SX", "SY", "SD"))
-        find = lambda n: at.own if n == "own" else at.slots[n]
-        self.mine = [find(n) for n in names[0]]
-        self.theirs = [find(n) for n in names[1]]
-
-    def block(self, slot):
-        return self.source.at[pl.ds(pl.multiple_of(slot * self.rows, self.rows), self.rows)]
-
-    def copy(self, k, src, dst, dev):
-        return remote(src, dst, self.send.at[self.index, k], self.recv.at[self.index, k], dev)
-
-    def share(self, j):
-        return self.copy(j, self.block(self.theirs[j]), self.land.at[j], self.at.sib)
-
-    def start(self):
-        for j in (3, 1, 2, 0):
-            self.share(j).start()
-
-    def slot(self, j):
-        if isinstance(j, int):
-            return self.mine[j]
-        return jnp.where(j == 1, self.mine[1], self.mine[2])
-
-    def arrived(self, j):
-        ref = self.land.at[j]
-        self.copy(j, ref, ref, self.at.sib).wait_recv()
-
-    def fetch(self, j):
-        return pltpu.make_async_copy(self.block(self.slot(j)), self.tmp, self.tmp_sem)
-
-    def add(self, j, extra=()):
-        self.fetch(j).start()
-        self.arrived(j)
-        self.fetch(j).wait()
-
-        def piece(i, _):
-            r = pl.ds(pl.multiple_of(i * 64, 64), 64)
-            value = self.land[j, r, :].astype(F32) + self.tmp[r, :].astype(F32)
-            for ref in extra:
-                value += ref[r, :].astype(F32)
-            self.land[j, r, :] = value.astype(BF16)
-            return 0
-
-        lax.fori_loop(0, self.rows // 64, piece, 0)
-
-    def hop(self, k):
-        at = self.at
-        if k == 4:
-            return self.copy(4, self.land.at[3], self.relayed, at.relay)
-        if k == 5:
-            return self.copy(5, self.land.at[self.direct], self.final.at[0], at.relay)
-        return self.copy(6, self.land.at[self.indirect], self.final.at[1], self.other)
-
-    def first(self):
-        self.add(3)
-        self.hop(4).start()
-        self.add(self.direct)
-        self.hop(5).start()
-
-    def second(self):
-        self.hop(4).wait_recv()
-        self.add(self.indirect, (self.relayed,))
-        self.hop(6).start()
-
-    def finish(self, use):
-        self.fetch(0).start()
-        self.arrived(0)
-        self.hop(5).wait_recv()
-        self.hop(6).wait_recv()
-        self.fetch(0).wait()
-
-        def piece(i, _):
-            r = pl.ds(pl.multiple_of(i * 64, 64), 64)
-            value = self.land[0, r, :].astype(F32) + self.tmp[r, :].astype(F32)
-            value += self.final[0, r, :].astype(F32) + self.final[1, r, :].astype(F32)
-            use(r, value)
-            return 0
-
-        lax.fori_loop(0, self.rows // 64, piece, 0)
-
-    def drain(self):
-        for j in range(4):
-            self.share(j).wait_send()
-        for k in (4, 5, 6):
-            self.hop(k).wait_send()
+    )(seq_lengths, out_grad, wd_full, act, wg_full, wu_full, h2, resid)
 
 
 def kernel_c(
@@ -1305,7 +1420,8 @@
     wu_ref,
     cos_ref,
     sin_ref,
-    blk_own,
+    gate_sum,
+    ffn_hbm,
     wgrads,
     heads_hbm,
     wo_hbm,
@@ -1315,7 +1431,6 @@
     g_key,
     g_value,
     g_out,
-    g_gate,
     g_up,
     g_down,
     small,
@@ -1332,24 +1447,22 @@
     dkv_land,
     gain_acc,
     dqkv,
+    f_part,
     d_part,
+    land_f,
     land_d,
     left_t,
     part,
-    land_w,
-    rel_w,
-    fin_w,
-    land_p,
-    rel_p,
-    fin_p,
-    tmp_w,
-    tmp_p,
+    room_w,
+    room_p,
     cols_acc,
     qk,
     qk_land,
     tile,
     s_send,
     s_recv,
+    f_send,
+    f_recv,
     d_send,
     d_recv,
     b_send,
@@ -1375,46 +1488,74 @@
     units = wg_ref.shape[1]
     last = n_tp - 1
     own_cols = pl.ds(pl.multiple_of(t * q_cols, q_cols), q_cols)
+    quarter = half // 2
     loads = [
         pltpu.make_async_copy(heads_hbm.at[:, own_cols], heads_own, loc_sem.at[0]),
         pltpu.make_async_copy(wo_hbm.at[:, own_cols], wo_own, loc_sem.at[1]),
+        pltpu.make_async_copy(ffn_hbm, f_part, loc_sem.at[2]),
     ]
     for cp in loads:
         cp.start()
     at.greet()
-    weights = [
-        Scatter(
-            at, wgrads.at[i], land_w.at[i], rel_w.at[i], fin_w.at[i], tmp_w,
-            loc_sem.at[2], s_send, s_recv, i,
+    down, up = (
+        Scatter(at, wgrads.at[k], room_w.at[i], loc_sem.at[3 + i], s_send, s_recv, i)
+        for i, k in enumerate((0, 2))
+    )
+    rest = Scatter(at, part, room_p, loc_sem.at[5], s_send, s_recv, 2)
+    down.start()
+    up.start()
+    f_lines, f_backs, lines, backs = [], [], [], []
+    for n in (0, 1):
+        r = pl.ds(n * half, half)
+        line = Line(at, f_part.at[r], land_f.at[n], f_send.at[n], f_recv.at[n], chunks)
+        f_lines.append(line)
+        f_backs.append(Back(line, block_out.at[r], o_send.at[n], o_recv.at[n], land_f.at[n]))
+        line = Line(at, d_part.at[r], land_d.at[n], d_send.at[n], d_recv.at[n], chunks)
+        lines.append(line)
+        backs.append(Back(line, inp.at[r], b_send.at[n], b_recv.at[n]))
+    length = length_ref[0]
+
+    def start_of(n, way, k):
+        size = lines[n].size
+        return pl.multiple_of(n * half + (1 - way) * quarter + k * size, size)
+
+    def final_ffn(n):
+        def final(way, k, value):
+            line = f_lines[n]
+            start = start_of(n, way, k)
+            pos = c * rows + start + lax.broadcasted_iota(jnp.int32, (line.size, 1), 0)
+            value = value * (pos < length).astype(F32)
+            land_f[n, way, line.local(k), :] = value.astype(BF16)
+
+        return final
+
+    def move_ffn(step):
+        for n in (0, 1):
+            f_lines[n].reduce(step - n * chunks, final_ffn(n))
+            f_backs[n].step(step - n * chunks - last * LAG)
+
+    def moves_ffn(slot):
+        for i in range(LAG):
+            move_ffn(slot * LAG + i)
+
+    def keep(n, way):
+        return pltpu.make_async_copy(
+            land_f.at[n, way],
+            block_out.at[pl.ds(start_of(n, way, 0), quarter)],
+            loc_sem.at[6 + n],
         )
-        for i in range(3)
-    ]
-    rest = Scatter(
-        at, part, land_p, rel_p, fin_p, tmp_p, loc_sem.at[3], s_send, s_recv, 3
-    )
-    for w in weights:
-        w.start()
-    d1 = Line(at, d_part, land_d, d_send, d_recv, chunks)
-    back = Back(d1, inp, b_send, b_recv)
-    back_block = Back(d1, block_out, o_send, o_recv, blk_own)
-
-    def keep(start):
-        return pltpu.make_async_copy(
-            blk_own, block_out.at[pl.ds(start, half)], loc_sem.at[4]
-        )
-
-    @pl.when(t == 0)
-    def _():
-        keep(0).start()
-
-    @pl.when(t == last)
-    def _():
-        keep(half).start()
-
-    back_block.step(0)
-    length = length_ref[0]
+
+    def keep_all(act):
+        for way in (0, 1):
+
+            @pl.when(t == (last if way == 0 else 0))
+            def _():
+                for n in (0, 1):
+                    act(keep(n, way))
+
     for cp in loads:
         cp.wait()
+    moves_ffn(0)
 
     def heads_grad(i, _):
         r = pl.ds(pl.multiple_of(i * 256, 256), 256)
@@ -1428,8 +1569,8 @@
         for n in range(128 // hd):
             h = j * (128 // hd) + n
             delta[h : h + 1, :] = jnp.sum(both[n * hd : (n + 1) * hd], axis=0, keepdims=True)
-    back_block.step(1)
-    weights[0].first()
+    moves_ffn(1)
+    down.first()
 
     def live_keys(index):
         pos = index * rows + lax.broadcasted_iota(jnp.int32, (1, rows), 1)
@@ -1472,6 +1613,11 @@
         def one(h, _):
             for i in range(rows // 256):
                 segment(h, h // group, i, 0, rows, False, k_own, v_own, kt_own)
+
+            @pl.when(lax.rem(h, 2) == 1)
+            def _():
+                moves_ffn(2 + lax.div(h, 2))
+
             return 0
 
         lax.fori_loop(0, q_heads, one, 0)
@@ -1481,9 +1627,16 @@
         give.start()
         dkv[...] = jnp.zeros_like(dkv)
 
-    back_block.step(2)
-    weights[1].first()
-    weights[0].second()
+    @pl.when(c == 0)
+    def _():
+        def one(h, _):
+            moves_ffn(2 + h)
+            return 0
+
+        lax.fori_loop(0, q_heads // 2, one, 0)
+
+    up.first()
+    down.second()
     load_block(c, k_own, v_own, kt_own)
 
     def own_block(h, _):
@@ -1492,10 +1645,15 @@
             if i:
                 segment(h, h // group, i, 0, i * 256, False, k_own, v_own, kt_own)
 
-        back_block.step(3 + h)
+
+        @pl.when(lax.rem(h, 2) == 1)
+        def _():
+            moves_ffn(2 + lax.div(q_heads, 2) + lax.div(h, 2))
+
         return 0
 
     lax.fori_loop(0, q_heads, own_block, 0)
+    moved = (2 + 2 * (q_heads // 2)) * LAG
     live = live_keys(c)
     for n in range(2 * kv_heads):
         dkv[n] = dkv[n] * live
@@ -1538,8 +1696,7 @@
     dqkv[:, q_cols : q_cols + kv_cols] = pair.T.astype(BF16)
     pair = jnp.concatenate([dkv[kv_heads + g] for g in range(kv_heads)], axis=0)
     dqkv[:, q_cols + kv_cols :] = pair.T.astype(BF16)
-    quarter = half // 2
-    for q in (0, 2, 1, 3):
+    for q in range(4):
         r = slice(q * quarter, (q + 1) * quarter)
         d_part[r, :] = mm_nt(dqkv[r, :], wqkv[...]).astype(BF16)
 
@@ -1558,16 +1715,22 @@
         trade(n).wait_recv()
         qk[n + 1] = qk[n] + qk_land[n]
 
-    weights[2].first()
-    weights[1].second()
-
-    def final(way, k, value):
-        r = d1.rows(way, k)
+    up.second()
+
+    def final_d1(n):
+        def final(way, k, value):
+            finish_rows(n, way, k, value)
+
+        return final
+
+    def finish_rows(n, way, k, value):
+        size = lines[n].size
+        r = pl.ds(start_of(n, way, k), size)
         x = hid_ref[r, :].astype(F32)
         scale = lax.rsqrt(jnp.mean(x * x, axis=-1, keepdims=True) + EPSILON)
         h = x * scale
         inner = jnp.mean(value * h, axis=-1, keepdims=True)
-        grad = rg_own[d1.local(k), :] + scale * (value - h * inner)
+        grad = rg_own[pl.ds(pl.multiple_of(n * quarter + k * size, size), size), :] + scale * (value - h * inner)
         inp[r, :] = grad.astype(BF16)
 
     def turn_hidden(i, _):
@@ -1592,11 +1755,15 @@
     def use_down(r, value):
         g_down[r, :] = value[:, 0:units]
 
-    def use_gate(r, value):
-        value = value[:, 0:units]
-        total = jnp.sum(wg_ref[r, :].astype(F32) * value, axis=1, keepdims=True)
-        cols_acc[3, r, :] = jnp.broadcast_to(total, (64, 128))
-        g_gate[r, :] = value * cols_acc[1, r, 0:1]
+    def gate_gain():
+        def piece(i, _):
+            r = pl.ds(pl.multiple_of(i * 64, 64), 64)
+            value = gate_sum[r, 0:units].astype(F32)
+            total = jnp.sum(wg_ref[r, :].astype(F32) * value, axis=1, keepdims=True)
+            cols_acc[3, r, :] = jnp.broadcast_to(total, (64, 128))
+            return 0
+
+        lax.fori_loop(0, block // 64, piece, 0)
 
     def use_up(r, value):
         value = value[:, 0:units]
@@ -1628,28 +1795,30 @@
     events = {
         0: (lambda: trade(0).start(), turn_all),
         1: (parts, lambda: traded(0), lambda: trade(1).start()),
-        2: (rest.first, lambda: traded(1), lambda: trade(2).start()),
-        3: (weights[2].second, lambda: traded(2)),
-        4: (rest.second, lambda: weights[0].finish(use_down)),
-        7: (lambda: weights[1].finish(use_gate),),
-        10: (lambda: weights[2].finish(use_up),),
-        12: (lambda: rest.finish(use_rest),),
+        2: (lambda: traded(1), lambda: trade(2).start(), gate_gain),
+        3: (rest.first, lambda: traded(2)),
+        5: (lambda: down.finish(use_down),),
+        6: (rest.second,),
+        8: (lambda: up.finish(use_up),),
+        10: (lambda: rest.finish(use_rest),),
     }
 
     def tail(step, _):
-        d1.reduce(step, final)
-        back.step(step - last)
-        back_block.step(step + 3 + q_heads)
+        for n in (0, 1):
+            lines[n].reduce(step - n * chunks, final_d1(n))
+            backs[n].step(step - n * chunks - last * LAG)
+        move_ffn(step + moved)
         for when, todo in events.items():
 
-            @pl.when(step == when)
+            @pl.when(step == when * LAG)
             def _():
                 for thing in todo:
                     thing()
 
         return 0
 
-    lax.fori_loop(0, max(chunks + 2 * last, 13), tail, 0)
+    lax.fori_loop(0, max(2 * chunks + 2 * last * LAG, 10 * LAG + 1), tail, 0)
+    keep_all(lambda cp: cp.start())
 
     def give_tile(d, owner):
         return remote(
@@ -1663,19 +1832,14 @@
     tile[t, 2:4, 0:128] = qk[3, 0:2, :]
     for d in range(n_tp - 1):
         give_tile(d, t).start()
-    for w in weights + [rest]:
+    for w in (down, up, rest):
         w.drain()
-    d1.drain()
-    back.drain()
-    back_block.drain()
-
-    @pl.when(t == 0)
-    def _():
-        keep(0).wait()
-
-    @pl.when(t == last)
-    def _():
-        keep(half).wait()
+    for n in (0, 1):
+        lines[n].drain()
+        backs[n].drain()
+        f_lines[n].drain()
+        f_backs[n].drain()
+    keep_all(lambda cp: cp.wait())
 
     @pl.when(c == 1)
     def _():
@@ -1696,11 +1860,11 @@
 def call_c(mesh, chunks, args, kept):
     (hidden_in, seq_lengths, attn_gain, ffn_gain, query_gain, key_gain,
      w_query, w_key, w_value, w_gate, w_up) = args
-    (attn_low, rg_own, blk_own, wgrads, wqkv_full, wo_full, heads_all, q_t, kv_all, inv_den,
+    (attn_low, rg_own, gate_sum, ffn_part, wgrads, wqkv_full, wo_full, heads_all, q_t, kv_all, inv_den,
      proj_t) = kept
     n_shard, n_ctx, n_tp = mesh.shape["shard"], mesh.shape["ctx"], mesh.shape["tp"]
     rows, width = hidden_in.shape
-    half = rows // 2
+    quarter = rows // 4
     hd = query_gain.shape[0]
     q_cols, kv_cols = w_query.shape[1], w_key.shape[1]
     qkv_cols = q_cols + 2 * kv_cols
@@ -1725,11 +1889,10 @@
             S((block, q_cols), F32),
             S((block, units), F32),
             S((block, units), F32),
-            S((block, units), F32),
             S((8, 256), F32),
         ),
-        in_specs=[sm] + [vm] * 19 + [hbm] * 4,
-        out_specs=(hbm,) + (vm,) * 9,
+        in_specs=[sm] + [vm] * 20 + [hbm] * 4,
+        out_specs=(hbm,) + (vm,) * 8,
         scratch_shapes=[
             V((rows, q_cols), BF16),
             V((width, q_cols), BF16),
@@ -1745,34 +1908,32 @@
             V((2, hd, rows), F32),
             V((rows, qkv_cols), BF16),
             V((rows, width), BF16),
-            V((2, half, width), BF16),
+            V((rows, width), BF16),
+            V((2, 2, quarter, width), BF16),
+            V((2, 2, quarter, width), BF16),
             V((2, width, rows), BF16),
             V((width, qkv_cols + q_cols), BF16),
-            V((3, 4, block, padded), BF16),
-            V((3, block, padded), BF16),
-            V((3, 2, block, padded), BF16),
-            V((4, block, qkv_cols + q_cols), BF16),
-            V((block, qkv_cols + q_cols), BF16),
-            V((2, block, qkv_cols + q_cols), BF16),
-            V((block, padded), BF16),
-            V((block, qkv_cols + q_cols), BF16),
+            V((2, 8 * block, padded), BF16),
+            V((8 * block, qkv_cols + q_cols), BF16),
             V((4, block, 128), F32),
             V((4, 8, 128), F32),
             V((3, 8, 128), F32),
             V((n_tp, 8, 256), F32),
-            dma((4, 7)),
-            dma((4, 7)),
-            dma((2, chunks)),
-            dma((2, chunks)),
-            dma((2, chunks)),
-            dma((2, chunks)),
-            dma((2, chunks)),
-            dma((2, chunks)),
+            dma((3, 7)),
+            dma((3, 7)),
+            dma((2, 2, chunks)),
+            dma((2, 2, chunks)),
+            dma((2, 2, chunks)),
+            dma((2, 2, chunks)),
+            dma((2, 2, chunks)),
+            dma((2, 2, chunks)),
+            dma((2, 2, chunks)),
+            dma((2, 2, chunks)),
             dma((4,)),
             dma((4,)),
             dma((n_tp - 1,)),
             dma((n_tp - 1,)),
-            dma((5,)),
+            dma((8,)),
         ],
         compiler_params=pltpu.CompilerParams(
             collective_id=2, has_side_effects=True, vmem_limit_bytes=VMEM_LIMIT
@@ -1781,29 +1942,30 @@
         seq_lengths, attn_low, rg_own, hidden_in, wqkv_full, q_t, kv_all, inv_den, proj_t,
         attn_gain.reshape(1, -1), ffn_gain.reshape(1, -1), query_gain.reshape(1, -1),
         key_gain.reshape(1, -1), w_query, w_key, w_value, w_gate, w_up,
-        jnp.asarray(cosine), jnp.asarray(sine), blk_own, wgrads, heads_all, wo_full,
-    )
-
-
-CHUNKS = 8
+        jnp.asarray(cosine), jnp.asarray(sine), gate_sum, ffn_part, wgrads, heads_all, wo_full,
+    )
+
+
+CHUNKS = 6
 
 
 def fast_body(mesh, *args):
     (hidden_in, seq_lengths, attn_gain, ffn_gain, query_gain, key_gain,
      w_query, w_key, w_value, w_out, w_gate, w_up, w_down, out_grad) = args
-    (wqkv_full, wo_full, wg_full, wu_full, heads_all, q_t, kv_all, inv_den,
-     proj_t) = call_a(mesh, args[:12])
-    attn_low, rg_own, blk_own, wgrads = call_b(
-        mesh, CHUNKS, seq_lengths, hidden_in, heads_all, out_grad, w_down, wo_full, wg_full, wu_full
-    )
-    (block_out, inp, g_query, g_key, g_value, g_out, g_gate, g_up, g_down, small) = call_c(
+    (wqkv_full, wo_full, wg_full, wu_full, wd_full, heads_all, q_t, kv_all, inv_den, proj_t,
+     resid, h2, act) = call_a(mesh, args[:13])
+    attn_low, rg_own, gate_sum, ffn_part, wgrads = call_b(
+        mesh, CHUNKS, seq_lengths, out_grad, wd_full, act, wg_full, wu_full, h2, resid
+    )
+    (block_out, inp, g_query, g_key, g_value, g_out, g_up, g_down, small) = call_c(
         mesh, CHUNKS,
         (hidden_in, seq_lengths, attn_gain, ffn_gain, query_gain, key_gain, w_query, w_key,
          w_value, w_gate, w_up),
-        (attn_low, rg_own, blk_own, wgrads, wqkv_full, wo_full, heads_all, q_t, kv_all, inv_den,
+        (attn_low, rg_own, gate_sum, ffn_part, wgrads, wqkv_full, wo_full, heads_all, q_t, kv_all, inv_den,
          proj_t),
     )
     block, hd = w_query.shape[0], query_gain.shape[0]
+    g_gate = gate_sum[:, : w_gate.shape[1]].astype(F32) * ffn_gain.astype(F32)[:, None]
     return (
         block_out, inp.astype(F32), small[0, :block], small[1, :block], small[2, :hd],
         small[3, :hd], g_query, g_key, g_value, g_out.T, g_gate, g_up, g_down.T,

time: 425 us -> 401 us (0.944)
  Pallas kernels: 406 us -> 380 us
    pallas_call x1, Pallas kernels: 152 us -> 100 us  [call_b(): pl.pallas_call(functools.partial(kernel_b, (n_shard, n_tp, chunks)), out_...]
    pallas_call x1, Pallas kernels: 101 us -> 134 us  [call_a(): pl.pallas_call(functools.partial(kernel_a, (n_shard, n_tp, hd)), out_shap...]
    pallas_call x1, Pallas kernels: 152 us -> 146 us  [call_c(): pl.pallas_call(functools.partial(kernel_c, (n_shard, n_tp, chunks, hd)),...]
where the time goes in v3:
time: 401 us; the launch traced here: 399 us
  Pallas kernels  380 us (95%)
  local copies, waits for them, and re-layouts  11.4 us (3%)
  other arithmetic  5.89 us (1%)
    pallas_call x1, Pallas kernels, call_c(): pl.pallas_call(functools.partial(kernel_c, (n_shard, n_tp, chunks, hd)),...  146 us
    pallas_call x1, Pallas kernels, call_a(): pl.pallas_call(functools.partial(kernel_a, (n_shard, n_tp, hd)), out_shap...  134 us
    pallas_call x1, Pallas kernels, call_b(): pl.pallas_call(functools.partial(kernel_b, (n_shard, n_tp, chunks)), out_...  100 us

profile of v3, /device:TPU:0, one launch (start us, length us, event | category | flops | bytes accessed | tf_op | source)
XLA Modules:
  0.0 398.7 jit_solution(17965383162103449148)
XLA Ops:
  1.3 1.2 reshape.43.gain_one_ref
  2.5 1.2 reshape.44.gain_two_ref
  3.7 134.4 %shard_map.273 = (bf16[1536,640]{1,0:T(8,128)(2,1)}, bf16[1536,1536]{1,0:T(8,128)(2,1)}, bf16[1536,1792]{1,0:T(8,128)(2,1)}, bf16[1536,1792]{1,0:T(8,128)(2,1)},...) custom-call(s32[1]{0:T(128)S(6)} %copy.38.length_ref, ...), custom_call_target="tpu_custom_call" | custom-call | tf_op jit(solution)/shard_map/pallas_call | solution.py:839
  138.2 100.1 %shard_map.274 = (bf16[768,1536]{1,0:T(8,128)(2,1)}, f32[384,1536]{1,0:T(8,128)}, bf16[192,1792]{1,0:T(8,128)(2,1)}, bf16[768,1536]{1,0:T(8,128)(2,1)}, bf16[3,1536,1792]{2,1,0:T(8,128)(2,1)}) custom-call(s32[1]{0:T(128)S(6)} %copy.38.length_ref, bf16[768,1536]{1,0:T(8,128)(2,1)} %og_ref.1, bf16[1536,1792]{1,0:T(8,128)(2,1)} %get-tuple-element.40.wd_hbm, ...), custom_call_target="tpu_custom_call" | custom-call | tf_op jit(solution)/shard_map/pallas_call | solution.py:1362
  238.2 145.6 %shard_map.275 = (bf16[768,1536]{1,0:T(8,128)(2,1)}, bf16[768,1536]{1,0:T(8,128)(2,1)}, f32[192,384]{1,0:T(8,128)}, f32[192,128]{1,0:T(8,128)}, f32[192,128]{1,0...) custom-call(s32[1]{0:T(128)S(6)} %copy.38.length_ref, ...), custom_call_target="tpu_custom_call" | custom-call | tf_op jit(solution)/shard_map/pallas_call | solution.py:1881
  383.9 0.0 copy-start.8
  383.9 0.0 copy-start
  383.9 0.0 copy-start.1
  383.9 4.6 %convert_element_type.9 = f32[768,1536]{1,0:T(8,128)} convert(bf16[768,1536]{1,0:T(8,128)(2,1)} %get-tuple-element.59) | non-fusion elementwise | flops 1179648 | bytes 7077888 | tf_op jit(solution)/shard_map/convert_element_type | solution.py:1970
  388.6 1.3 fusion
  389.9 1.3 slice_bitcast_fusion
  391.2 0.0 copy-done.8
  391.2 0.0 copy-done
  391.2 1.2 convert_multiply_fusion
  392.4 0.0 copy-done.1
  392.4 0.0 copy-start.5
  392.4 0.0 copy-start.7
  392.4 0.0 copy-start.4
  392.4 0.0 copy-start.3
  392.5 1.4 copy.39
  393.9 0.0 copy-done.5
  393.9 0.7 copy.40
  394.6 0.0 copy-done.7
  394.6 0.6 copy.41
  395.2 0.0 copy-done.6
  395.2 0.6 copy.42
  395.9 0.0 copy-done.4
  395.9 0.7 copy.43
  396.6 0.0 copy-done.3
  396.6 1.1 copy.44
  397.7 0.0 copy-done.2
  397.7 1.1 copy.45
  (3 shorter events, 0.0 us)
Async XLA Ops:
  383.9 7.3 %copy-start.8 = (bf16[192]{0:T(256)(128)(2,1)S(1)}, bf16[192]{0:T(256)(128)(2,1)}, u32[]{:S(2)}) copy-start(bf16[192]{0:T(256)(128)(2,1)} %param.21) | copy-start | bytes 1156
  383.9 7.3 %copy-start = (bf16[192,1792]{1,0:T(8,128)(2,1)S(1)}, bf16[192,1792]{1,0:T(8,128)(2,1)}, u32[]{:S(2)}) copy-start(bf16[192,1792]{1,0:T(8,128)(2,1)} %get-tuple-element.53.gate_sum) | copy-start | bytes 2064388
  383.9 8.5 %copy-start.1 = (bf16[768,1536]{1,0:T(8,128)(2,1)S(1)}, bf16[768,1536]{1,0:T(8,128)(2,1)}, u32[]{:S(2)}) copy-start(bf16[768,1536]{1,0:T(8,128)(2,1)} %get-tuple-element.84) | copy-start | bytes 7077892
  392.4 1.4 copy-start.5
  392.4 2.2 copy-start.7
  392.4 2.8 copy-start.6
  392.4 3.4 copy-start.4
  392.4 4.1 %copy-start.3 = (f32[192,1728]{1,0:T(8,128)S(1)}, f32[192,1728]{1,0:T(8,128)}, u32[]{:S(2)}) copy-start(f32[192,1728]{1,0:T(8,128)} %get-tuple-element.95) | copy-start | bytes 3981316
  393.9 3.8 copy-start.2

commit v4 on v3

--- a/solution.py
+++ b/solution.py
@@ -452,7 +452,7 @@
 
 
 def column(row_ref, n):
-    wide = jnp.broadcast_to(row_ref[...].astype(F32), (8, n))
+    wide = jnp.broadcast_to(row_ref[...].astype(F32)[None, :], (8, n))
     return wide.T[:, 0:1]
 
 
@@ -473,19 +473,28 @@
     wd_ref,
     cos_ref,
     sin_ref,
-    wqkv_full,
-    wo_full,
+    wqkv_out,
+    wo_out,
     wg_full,
     wu_full,
     wd_full,
+    heads_out,
+    q_out,
+    kv_out,
+    inv_den,
+    proj_out,
+    resid_out,
+    h2t_out,
+    act_out,
+    wqkv_full,
+    wo_full,
     heads_all,
     q_t,
     kv_all,
-    inv_den,
     proj_t,
     resid,
     h2,
-    act_out,
+    h2t,
     s_qkv,
     s_woz,
     s_wg,
@@ -509,6 +518,7 @@
     kv_sem,
     loc_sem,
     act_sem,
+    out_sem,
 ):
     n_shard, n_tp, hd = shape
     at = Place(n_shard, n_tp)
@@ -519,8 +529,23 @@
     group = q_heads // kv_heads
     half = hd // 2
     at.greet()
-
-    col_one = column(gain_one_ref, gain_one_ref.shape[1])
+    leaving = [
+        pltpu.make_async_copy(src, dst, out_sem.at[i])
+        for i, (src, dst) in enumerate(
+            (
+                (wqkv_full, wqkv_out),
+                (proj_t, proj_out),
+                (q_t, q_out),
+                (kv_all, kv_out),
+                (heads_all, heads_out),
+                (wo_full, wo_out),
+                (resid, resid_out),
+                (h2t, h2t_out),
+            )
+        )
+    ]
+
+    col_one = column(gain_one_ref, gain_one_ref.shape[0])
     s_qkv[:, 0:q_cols] = (wq_ref[...].astype(F32) * col_one).astype(BF16)
     s_qkv[:, q_cols : q_cols + kv_cols] = (wk_ref[...].astype(F32) * col_one).astype(BF16)
     s_qkv[:, q_cols + kv_cols :] = (wv_ref[...].astype(F32) * col_one).astype(BF16)
@@ -566,7 +591,7 @@
 
     lax.fori_loop(0, rows // 64, norm_one, 0)
     qkv.relay()
-    col_two = column(gain_two_ref, gain_two_ref.shape[1])
+    col_two = column(gain_two_ref, gain_two_ref.shape[0])
     units = wg_ref.shape[1]
     for src, dst in ((wg_ref, s_wg), (wu_ref, s_wu)):
         dst[:, 0:units] = (src[...].astype(F32) * col_two).astype(BF16)
@@ -589,6 +614,8 @@
         return 0
 
     lax.fori_loop(0, rows // 256, project, 0)
+    leaving[0].start()
+    leaving[1].start()
     here = pl.ds(pl.multiple_of(c * rows, rows), rows)
     k_gain = column(k_gain_ref, hd)
     q_gain = column(q_gain_ref, hd)
@@ -623,6 +650,7 @@
         return 0
 
     lax.fori_loop(0, q_heads, prep_q, 0)
+    leaving[2].start()
     length = length_ref[0]
 
     def load_block(index, k_nat, v_ext):
@@ -675,6 +703,12 @@
 
         lax.fori_loop(0, q_heads, other_block, 0)
 
+    @pl.when(c == 0)
+    def _():
+        kv_all[1 - c] = jnp.zeros(kv_all.shape[1:], BF16)
+
+    leaving[3].start()
+
     def chunk_cols(owner, j):
         return pl.ds(pl.multiple_of(owner * q_cols + j * 128, 128), 128)
 
@@ -726,13 +760,17 @@
 
     out.finish()
     local[1].wait()
+    leaving[4].start()
+    leaving[5].start()
 
     def residual(i, _):
         r = pl.ds(pl.multiple_of(i * 128, 128), 128)
         x = hid_ref[r, :].astype(F32) + mm_nt(heads_all[r, :], wo_full[...])
         resid[r, :] = x
         scale = lax.rsqrt(jnp.mean(x * x, axis=-1, keepdims=True) + EPSILON)
-        h2[r, :] = (x * scale).astype(BF16)
+        h = (x * scale).astype(BF16)
+        h2[r, :] = h
+        h2t[:, r] = h.T
 
         @pl.when(i == 1)
         def _():
@@ -747,6 +785,8 @@
         return 0
 
     lax.fori_loop(0, rows // 128, residual, 0)
+    leaving[6].start()
+    leaving[7].start()
     up.relay_last()
     up.finish()
     local[3].wait()
@@ -809,7 +849,9 @@
     @pl.when(c == 0)
     def _():
         kv_copy.wait_send()
-        kv_all[1 - c] = jnp.zeros(kv_all.shape[1:], BF16)
+
+    for cp in leaving:
+        cp.wait()
 
 
 def rope_tables(positions, hd):
@@ -850,12 +892,21 @@
             S((8, rows), F32),
             S((qkv_cols, rows), F32),
             S((rows, width), F32),
-            S((rows, width), BF16),
+            S((width, rows), BF16),
             S((3, rows, padded), BF16),
         ),
         in_specs=[sm] + [vm] * 14,
-        out_specs=(vm, vm, hbm, hbm, hbm, vm, vm, vm, vm, vm, vm, vm, hbm),
+        out_specs=(hbm,) * 8 + (vm,) + (hbm,) * 4,
         scratch_shapes=[
+            pltpu.VMEM((width, qkv_cols), BF16),
+            pltpu.VMEM((width, n_tp * q_cols), BF16),
+            pltpu.VMEM((rows, n_tp * q_cols), BF16),
+            pltpu.VMEM((q_cols, rows), BF16),
+            pltpu.VMEM((n_ctx, 2 * kv_cols, rows), BF16),
+            pltpu.VMEM((qkv_cols, rows), F32),
+            pltpu.VMEM((rows, width), F32),
+            pltpu.VMEM((rows, width), BF16),
+            pltpu.VMEM((width, rows), BF16),
             pltpu.VMEM((block, qkv_cols), BF16),
             pltpu.VMEM((block, n_tp * q_cols), BF16),
             pltpu.VMEM((block, padded), BF16),
@@ -879,13 +930,14 @@
             dma((2,)),
             dma((7,)),
             dma((padded // 256,)),
+            dma((8,)),
         ],
         compiler_params=pltpu.CompilerParams(
             collective_id=0, has_side_effects=True, vmem_limit_bytes=VMEM_LIMIT
         ),
     )(
-        seq_lengths, hidden_in, attn_gain.reshape(1, -1), ffn_gain.reshape(1, -1),
-        query_gain.reshape(1, -1), key_gain.reshape(1, -1), w_query, w_key, w_value,
+        seq_lengths, hidden_in, attn_gain, ffn_gain,
+        query_gain, key_gain, w_query, w_key, w_value,
         w_out.T, w_gate, w_up, w_down.T, jnp.asarray(cosine), jnp.asarray(sine),
     )
 
@@ -894,9 +946,9 @@
 
 
 class Line:
-    def __init__(self, at, part, landing, send, recv, chunks):
+    def __init__(self, at, part, landing, send, recv, chunks, folds=1):
         self.at, self.part, self.landing = at, part, landing
-        self.send, self.recv, self.chunks = send, recv, chunks
+        self.send, self.recv, self.chunks, self.folds = send, recv, chunks, folds
         self.half = landing.shape[1]
         self.size = self.half // chunks
         self.last = at.n_tp - 1
@@ -912,8 +964,17 @@
         return pl.ds(pl.multiple_of(k * self.size, self.size), self.size)
 
     def rows(self, way, k):
-        start = (1 - way) * self.half + k * self.size
-        return pl.ds(pl.multiple_of(start, self.size), self.size)
+        return pl.ds(self.start(way, k), self.size)
+
+    def start(self, way, k):
+        fold = self.half // self.folds
+        if self.folds == 1:
+            first = (1 - way) * fold + k * self.size
+        else:
+            per = self.chunks // self.folds
+            group = lax.div(k, per)
+            first = (2 * group + 1 - way) * fold + (k - group * per) * self.size
+        return pl.multiple_of(first, self.size)
 
     def copy(self, way, k):
         return remote(
@@ -1034,6 +1095,7 @@
     def start(self):
         for j in (3, 1, 2, 0):
             self.share(j).start()
+        self.fetch(3).start()
 
     def slot(self, j):
         if isinstance(j, int):
@@ -1048,7 +1110,6 @@
         return pltpu.make_async_copy(self.block(self.slot(j)), self.tmp, self.tmp_sem)
 
     def add(self, j, extra=()):
-        self.fetch(j).start()
         self.arrived(j)
         self.fetch(j).wait()
         land = self.land(j)
@@ -1073,17 +1134,19 @@
 
     def first(self):
         self.add(3)
+        self.fetch(self.direct).start()
         self.hop(4).start()
         self.add(self.direct)
+        self.fetch(self.indirect).start()
         self.hop(5).start()
 
     def second(self):
         self.hop(4).wait_recv()
         self.add(self.indirect, (self.relayed,))
+        self.fetch(0).start()
         self.hop(6).start()
 
     def finish(self, use):
-        self.fetch(0).start()
         self.arrived(0)
         self.hop(5).wait_recv()
         self.hop(6).wait_recv()
@@ -1114,7 +1177,7 @@
     act_hbm,
     wg_hbm,
     wu_hbm,
-    h2_hbm,
+    h2t_hbm,
     resid_hbm,
     attn_low,
     rg_own,
@@ -1127,7 +1190,7 @@
     wu,
     wd,
     resid,
-    h2,
+    left_t,
     gl,
     act,
     land_d,
@@ -1139,6 +1202,7 @@
     s_send,
     s_recv,
     loc_sem,
+    tile_sem,
     st_sem,
     free_sem,
 ):
@@ -1150,7 +1214,25 @@
     half = rows // 2
     tiles = padded // 256
     last = n_tp - 1
-    pairs = ((wd_hbm, wd), (act_hbm, act), (wg_hbm, wg), (wu_hbm, wu), (h2_hbm, h2), (resid_hbm, resid))
+    def tile_load(f):
+        cols = pl.ds(pl.multiple_of(f * 256, 256), 256)
+        return (
+            pltpu.make_async_copy(wd_hbm.at[:, cols], wd.at[:, cols], tile_sem.at[0, f]),
+            pltpu.make_async_copy(
+                act_hbm.at[1:3, :, cols], act.at[1:3, :, cols], tile_sem.at[1, f]
+            ),
+        )
+
+    for f in range(tiles):
+        for cp in tile_load(f):
+            cp.start()
+    pairs = (
+        (wg_hbm, wg),
+        (wu_hbm, wu),
+        (resid_hbm, resid),
+        (act_hbm.at[0], act.at[0]),
+        (h2t_hbm, left_t.at[:, pl.ds(0, rows)]),
+    )
     loads = [
         pltpu.make_async_copy(src, dst, loc_sem.at[i]) for i, (src, dst) in enumerate(pairs)
     ]
@@ -1164,14 +1246,14 @@
         return (pos < length).astype(F32)
 
     def mask_grad(i, _):
-        start = pl.multiple_of(i * 64, 64)
-        r = pl.ds(start, 64)
-        gl[r, :] = (og_ref[r, :].astype(F32) * live_rows(start, 64)).astype(BF16)
+        start = pl.multiple_of(i * 128, 128)
+        r = pl.ds(start, 128)
+        low = (og_ref[r, :].astype(F32) * live_rows(start, 128)).astype(BF16)
+        gl[r, :] = low
+        left_t[:, pl.ds(pl.multiple_of(rows + start, 128), 128)] = low.T
         return 0
 
-    lax.fori_loop(0, rows // 64, mask_grad, 0)
-    loads[0].wait()
-    loads[1].wait()
+    lax.fori_loop(0, rows // 128, mask_grad, 0)
 
     quarter = half // 2
     lines, backs = [], []
@@ -1209,6 +1291,9 @@
 
         def one(f, _):
             cols = pl.ds(pl.multiple_of(f * 256, 256), 256)
+            if n == 0:
+                for cp in tile_load(f):
+                    cp.wait()
             g = mm(gl[r, :], wd[:, cols])
             act[1, r, cols] = (g * act[1, r, cols].astype(F32)).astype(BF16)
             act[2, r, cols] = (g * act[2, r, cols].astype(F32)).astype(BF16)
@@ -1228,7 +1313,7 @@
         d_part[r, :] = total.astype(BF16)
 
     mid(0)
-    for cp in loads[2:]:
+    for cp in loads:
         cp.wait()
     back_part(0)
     back_part(1)
@@ -1248,15 +1333,8 @@
     def free(n):
         pl.semaphore_wait(free_sem.at[n], 1)
 
-    def turn(i, _):
-        r = pl.ds(pl.multiple_of(i * 128, 128), 128)
-        r2 = pl.ds(pl.multiple_of(rows + i * 128, 128), 128)
-        wu[:, r] = h2[r, :].T
-        wu[:, r2] = gl[r, :].T
-        return 0
-
     blocks = width // block
-    per_step = -(-3 // LAG)
+    per_step = PER_STEP
     count = 3 * blocks
     def weight_of(n):
         return lax.rem(lax.div(n, blocks) + 1, 3)
@@ -1277,7 +1355,7 @@
             stage_copy(n - 2).wait()
 
         first = pl.multiple_of(jnp.where(a == 0, rows, 0), 128)
-        left = wu[pl.ds(pl.multiple_of(w * block, block), block), pl.ds(first, rows)]
+        left = left_t[pl.ds(pl.multiple_of(w * block, block), block), pl.ds(first, rows)]
         for f in range(tiles):
             cols = slice(f * 256, (f + 1) * 256)
             stage[slot, :, cols] = mm(left, act[a, :, cols]).astype(BF16)
@@ -1303,21 +1381,19 @@
         free(2)
         gate.first()
 
+    total = chunks + 2 * last * LAG
+    begin = (blocks + 2 * per_step - 1) // per_step
     events = {
-        3: start_gate,
-        4: first_gate,
-        7: gate.second,
-        9: lambda: gate.finish(use_gate),
+        begin: start_gate,
+        begin + total // 12: first_gate,
+        begin + total // 4: gate.second,
+        total - 3: lambda: gate.finish(use_gate),
     }
 
     def tail(step, _):
         move(0, step + done)
         move(1, step)
 
-        @pl.when(step == 0)
-        def _():
-            lax.fori_loop(0, rows // 128, turn, 0)
-
         for n in range(per_step):
 
             @pl.when(step * per_step + n < count)
@@ -1326,17 +1402,17 @@
 
         for when, todo in events.items():
 
-            @pl.when(step == when * LAG)
+            @pl.when(step == when)
             def _():
                 todo()
 
-        @pl.when(jnp.logical_and(step >= 6 * LAG, step < 6 * LAG + 4))
+        @pl.when(jnp.logical_and(step >= total - 10, step < total - 6))
         def _():
-            forward_part(step - 6 * LAG)
+            forward_part(step - (total - 10))
 
         return 0
 
-    steps = max(chunks + 2 * last * LAG, 9 * LAG + 1, 6 * LAG + 4, -(-count // per_step))
+    steps = max(total, -(-count // per_step))
     lax.fori_loop(0, steps, tail, 0)
     keeps.start()
     stage_copy(count - 2).wait()
@@ -1348,7 +1424,7 @@
     keeps.wait()
 
 
-def call_b(mesh, chunks, seq_lengths, out_grad, wd_full, act, wg_full, wu_full, h2, resid):
+def call_b(mesh, chunks, seq_lengths, out_grad, wd_full, act, wg_full, wu_full, h2t, resid):
     n_shard, n_tp = mesh.shape["shard"], mesh.shape["tp"]
     rows, width = out_grad.shape
     block = width // (n_shard * mesh.shape["ctx"])
@@ -1377,7 +1453,7 @@
             pltpu.VMEM((width, padded), BF16),
             pltpu.VMEM((width, padded), BF16),
             pltpu.VMEM((rows, width), F32),
-            pltpu.VMEM((rows, width), BF16),
+            pltpu.VMEM((width, 2 * rows), BF16),
             pltpu.VMEM((rows, width), BF16),
             pltpu.VMEM((3, rows, padded), BF16),
             pltpu.VMEM((2, 2, half // 2, width), BF16),
@@ -1388,27 +1464,24 @@
             dma((2, 2, chunks)),
             dma((1, 7)),
             dma((1, 7)),
-            dma((6,)),
+            dma((5,)),
+            dma((2, padded // 256)),
             dma((2,)),
             pltpu.SemaphoreType.REGULAR((3,)),
         ],
         compiler_params=pltpu.CompilerParams(
             collective_id=1, has_side_effects=True, vmem_limit_bytes=VMEM_LIMIT
         ),
-    )(seq_lengths, out_grad, wd_full, act, wg_full, wu_full, h2, resid)
+    )(seq_lengths, out_grad, wd_full, act, wg_full, wu_full, h2t, resid)
 
 
 def kernel_c(
     shape,
     length_ref,
     attn_low,
-    rg_own,
-    hid_ref,
-    wqkv,
     q_t,
     kv_all,
     inv_den,
-    proj_t,
     gain_one_ref,
     gain_two_ref,
     q_gain_ref,
@@ -1416,11 +1489,15 @@
     wq_ref,
     wk_ref,
     wv_ref,
-    wg_ref,
-    wu_ref,
     cos_ref,
     sin_ref,
-    gate_sum,
+    rg_hbm,
+    hid_hbm,
+    wqkv_hbm,
+    proj_hbm,
+    wg_hbm,
+    wu_hbm,
+    gate_hbm,
     ffn_hbm,
     wgrads,
     heads_hbm,
@@ -1434,6 +1511,13 @@
     g_up,
     g_down,
     small,
+    rg_own,
+    hid_ref,
+    wqkv,
+    proj_t,
+    wg_ref,
+    wu_ref,
+    gate_sum,
     heads_own,
     wo_own,
     hg_t,
@@ -1478,14 +1562,14 @@
     n_shard, n_tp, chunks, hd = shape
     at = Place(n_shard, n_tp)
     c, t = at.c, at.t
-    rows, width = hid_ref.shape
+    rows, width = hid_hbm.shape
     q_cols, kv_cols = wq_ref.shape[1], wk_ref.shape[1]
     q_heads, kv_heads = q_cols // hd, kv_cols // hd
     group = q_heads // kv_heads
     halfd = hd // 2
     half = rows // 2
     block = wq_ref.shape[0]
-    units = wg_ref.shape[1]
+    units = wg_hbm.shape[1]
     last = n_tp - 1
     own_cols = pl.ds(pl.multiple_of(t * q_cols, q_cols), q_cols)
     quarter = half // 2
@@ -1494,6 +1578,20 @@
         pltpu.make_async_copy(wo_hbm.at[:, own_cols], wo_own, loc_sem.at[1]),
         pltpu.make_async_copy(ffn_hbm, f_part, loc_sem.at[2]),
     ]
+    late = [
+        pltpu.make_async_copy(src, dst, loc_sem.at[8 + i])
+        for i, (src, dst) in enumerate(
+            (
+                (proj_hbm, proj_t),
+                (wqkv_hbm, wqkv),
+                (hid_hbm, hid_ref),
+                (rg_hbm, rg_own),
+                (wg_hbm, wg_ref),
+                (wu_hbm, wu_ref),
+                (gate_hbm, gate_sum),
+            )
+        )
+    ]
     for cp in loads:
         cp.start()
     at.greet()
@@ -1504,44 +1602,30 @@
     rest = Scatter(at, part, room_p, loc_sem.at[5], s_send, s_recv, 2)
     down.start()
     up.start()
-    f_lines, f_backs, lines, backs = [], [], [], []
-    for n in (0, 1):
-        r = pl.ds(n * half, half)
-        line = Line(at, f_part.at[r], land_f.at[n], f_send.at[n], f_recv.at[n], chunks)
-        f_lines.append(line)
-        f_backs.append(Back(line, block_out.at[r], o_send.at[n], o_recv.at[n], land_f.at[n]))
-        line = Line(at, d_part.at[r], land_d.at[n], d_send.at[n], d_recv.at[n], chunks)
-        lines.append(line)
-        backs.append(Back(line, inp.at[r], b_send.at[n], b_recv.at[n]))
+    ffn = Line(at, f_part, land_f, f_send, f_recv, chunks, 2)
+    ffn_back = Back(ffn, block_out, o_send, o_recv, land_f)
+    d1 = Line(at, d_part, land_d, d_send, d_recv, chunks, 2)
+    back = Back(d1, inp, b_send, b_recv)
     length = length_ref[0]
 
-    def start_of(n, way, k):
-        size = lines[n].size
-        return pl.multiple_of(n * half + (1 - way) * quarter + k * size, size)
-
-    def final_ffn(n):
-        def final(way, k, value):
-            line = f_lines[n]
-            start = start_of(n, way, k)
-            pos = c * rows + start + lax.broadcasted_iota(jnp.int32, (line.size, 1), 0)
-            value = value * (pos < length).astype(F32)
-            land_f[n, way, line.local(k), :] = value.astype(BF16)
-
-        return final
+    def final_ffn(way, k, value):
+        pos = c * rows + ffn.start(way, k)
+        pos += lax.broadcasted_iota(jnp.int32, (ffn.size, 1), 0)
+        value = value * (pos < length).astype(F32)
+        land_f[way, ffn.local(k), :] = value.astype(BF16)
 
     def move_ffn(step):
-        for n in (0, 1):
-            f_lines[n].reduce(step - n * chunks, final_ffn(n))
-            f_backs[n].step(step - n * chunks - last * LAG)
+        ffn.reduce(step, final_ffn)
+        ffn_back.step(step - last * LAG)
 
     def moves_ffn(slot):
-        for i in range(LAG):
-            move_ffn(slot * LAG + i)
+        for i in range(PER_SLOT):
+            move_ffn(slot * PER_SLOT + i)
 
     def keep(n, way):
         return pltpu.make_async_copy(
-            land_f.at[n, way],
-            block_out.at[pl.ds(start_of(n, way, 0), quarter)],
+            land_f.at[way, pl.ds(n * quarter, quarter)],
+            block_out.at[pl.ds((2 * n + 1 - way) * quarter, quarter)],
             loc_sem.at[6 + n],
         )
 
@@ -1556,6 +1640,8 @@
     for cp in loads:
         cp.wait()
     moves_ffn(0)
+    for cp in late:
+        cp.start()
 
     def heads_grad(i, _):
         r = pl.ds(pl.multiple_of(i * 256, 256), 256)
@@ -1653,7 +1739,7 @@
         return 0
 
     lax.fori_loop(0, q_heads, own_block, 0)
-    moved = (2 + 2 * (q_heads // 2)) * LAG
+    moved = (2 + 2 * (q_heads // 2)) * PER_SLOT
     live = live_keys(c)
     for n in range(2 * kv_heads):
         dkv[n] = dkv[n] * live
@@ -1666,6 +1752,8 @@
 
     here = pl.ds(pl.multiple_of(c * rows, rows), rows)
     gain_acc[...] = jnp.zeros_like(gain_acc)
+    for cp in late:
+        cp.wait()
 
     def through(which, row, grad, gain):
         x = proj_t[pl.ds(pl.multiple_of(row, hd), hd), :]
@@ -1696,10 +1784,6 @@
     dqkv[:, q_cols : q_cols + kv_cols] = pair.T.astype(BF16)
     pair = jnp.concatenate([dkv[kv_heads + g] for g in range(kv_heads)], axis=0)
     dqkv[:, q_cols + kv_cols :] = pair.T.astype(BF16)
-    for q in range(4):
-        r = slice(q * quarter, (q + 1) * quarter)
-        d_part[r, :] = mm_nt(dqkv[r, :], wqkv[...]).astype(BF16)
-
     def as_row(v):
         return jnp.broadcast_to(v, (v.shape[0], 128)).T[0:1, :]
 
@@ -1717,21 +1801,22 @@
 
     up.second()
 
-    def final_d1(n):
-        def final(way, k, value):
-            finish_rows(n, way, k, value)
-
-        return final
-
-    def finish_rows(n, way, k, value):
-        size = lines[n].size
-        r = pl.ds(start_of(n, way, k), size)
+    def final_d1(way, k, value):
+        r = d1.rows(way, k)
         x = hid_ref[r, :].astype(F32)
         scale = lax.rsqrt(jnp.mean(x * x, axis=-1, keepdims=True) + EPSILON)
         h = x * scale
         inner = jnp.mean(value * h, axis=-1, keepdims=True)
-        grad = rg_own[pl.ds(pl.multiple_of(n * quarter + k * size, size), size), :] + scale * (value - h * inner)
+        grad = rg_own[d1.local(k), :] + scale * (value - h * inner)
         inp[r, :] = grad.astype(BF16)
+
+    ahead = LAG
+    for q in range(4):
+        r = slice(q * quarter, (q + 1) * quarter)
+        d_part[r, :] = mm_nt(dqkv[r, :], wqkv[...]).astype(BF16)
+        if q == 1:
+            for step in range(ahead):
+                d1.reduce(step, final_d1)
 
     def turn_hidden(i, _):
         r = pl.ds(pl.multiple_of(i * 128, 128), 128)
@@ -1804,20 +1889,19 @@
     }
 
     def tail(step, _):
-        for n in (0, 1):
-            lines[n].reduce(step - n * chunks, final_d1(n))
-            backs[n].step(step - n * chunks - last * LAG)
+        d1.reduce(step + ahead, final_d1)
+        back.step(step + ahead - last * LAG)
         move_ffn(step + moved)
         for when, todo in events.items():
 
-            @pl.when(step == when * LAG)
+            @pl.when(step == when * PER_SLOT)
             def _():
                 for thing in todo:
                     thing()
 
         return 0
 
-    lax.fori_loop(0, max(2 * chunks + 2 * last * LAG, 10 * LAG + 1), tail, 0)
+    lax.fori_loop(0, max(chunks + 2 * last * LAG, 10 * PER_SLOT + 1), tail, 0)
     keep_all(lambda cp: cp.start())
 
     def give_tile(d, owner):
@@ -1834,11 +1918,8 @@
         give_tile(d, t).start()
     for w in (down, up, rest):
         w.drain()
-    for n in (0, 1):
-        lines[n].drain()
-        backs[n].drain()
-        f_lines[n].drain()
-        f_backs[n].drain()
+    for thing in (d1, back, ffn, ffn_back):
+        thing.drain()
     keep_all(lambda cp: cp.wait())
 
     @pl.when(c == 1)
@@ -1891,9 +1972,16 @@
             S((block, units), F32),
             S((8, 256), F32),
         ),
-        in_specs=[sm] + [vm] * 20 + [hbm] * 4,
+        in_specs=[sm] + [vm] * 13 + [hbm] * 11,
         out_specs=(hbm,) + (vm,) * 8,
         scratch_shapes=[
+            V((rows // 2, width), F32),
+            V((rows, width), BF16),
+            V((width, qkv_cols), BF16),
+            V((qkv_cols, rows), F32),
+            V((block, units), BF16),
+            V((block, units), BF16),
+            V((block, padded), BF16),
             V((rows, q_cols), BF16),
             V((width, q_cols), BF16),
             V((q_cols, rows), BF16),
@@ -1909,8 +1997,8 @@
             V((rows, qkv_cols), BF16),
             V((rows, width), BF16),
             V((rows, width), BF16),
-            V((2, 2, quarter, width), BF16),
-            V((2, 2, quarter, width), BF16),
+            V((2, 2 * quarter, width), BF16),
+            V((2, 2 * quarter, width), BF16),
             V((2, width, rows), BF16),
             V((width, qkv_cols + q_cols), BF16),
             V((2, 8 * block, padded), BF16),
@@ -1921,44 +2009,47 @@
             V((n_tp, 8, 256), F32),
             dma((3, 7)),
             dma((3, 7)),
-            dma((2, 2, chunks)),
-            dma((2, 2, chunks)),
-            dma((2, 2, chunks)),
-            dma((2, 2, chunks)),
-            dma((2, 2, chunks)),
-            dma((2, 2, chunks)),
-            dma((2, 2, chunks)),
-            dma((2, 2, chunks)),
+            dma((2, chunks)),
+            dma((2, chunks)),
+            dma((2, chunks)),
+            dma((2, chunks)),
+            dma((2, chunks)),
+            dma((2, chunks)),
+            dma((2, chunks)),
+            dma((2, chunks)),
             dma((4,)),
             dma((4,)),
             dma((n_tp - 1,)),
             dma((n_tp - 1,)),
-            dma((8,)),
+            dma((15,)),
         ],
         compiler_params=pltpu.CompilerParams(
             collective_id=2, has_side_effects=True, vmem_limit_bytes=VMEM_LIMIT
         ),
     )(
-        seq_lengths, attn_low, rg_own, hidden_in, wqkv_full, q_t, kv_all, inv_den, proj_t,
-        attn_gain.reshape(1, -1), ffn_gain.reshape(1, -1), query_gain.reshape(1, -1),
-        key_gain.reshape(1, -1), w_query, w_key, w_value, w_gate, w_up,
-        jnp.asarray(cosine), jnp.asarray(sine), gate_sum, ffn_part, wgrads, heads_all, wo_full,
+        seq_lengths, attn_low, q_t, kv_all, inv_den,
+        attn_gain, ffn_gain, query_gain, key_gain, w_query, w_key, w_value,
+        jnp.asarray(cosine), jnp.asarray(sine), rg_own, hidden_in, wqkv_full, proj_t,
+        w_gate, w_up, gate_sum, ffn_part, wgrads, heads_all, wo_full,
     )
 
 
 CHUNKS = 6
+CHUNKS_C = 12
+PER_STEP = 3
+PER_SLOT = 2
 
 
 def fast_body(mesh, *args):
     (hidden_in, seq_lengths, attn_gain, ffn_gain, query_gain, key_gain,
      w_query, w_key, w_value, w_out, w_gate, w_up, w_down, out_grad) = args
     (wqkv_full, wo_full, wg_full, wu_full, wd_full, heads_all, q_t, kv_all, inv_den, proj_t,
-     resid, h2, act) = call_a(mesh, args[:13])
+     resid, h2t, act) = call_a(mesh, args[:13])
     attn_low, rg_own, gate_sum, ffn_part, wgrads = call_b(
-        mesh, CHUNKS, seq_lengths, out_grad, wd_full, act, wg_full, wu_full, h2, resid
+        mesh, CHUNKS, seq_lengths, out_grad, wd_full, act, wg_full, wu_full, h2t, resid
     )
     (block_out, inp, g_query, g_key, g_value, g_out, g_up, g_down, small) = call_c(
-        mesh, CHUNKS,
+        mesh, CHUNKS_C,
         (hidden_in, seq_lengths, attn_gain, ffn_gain, query_gain, key_gain, w_query, w_key,
          w_value, w_gate, w_up),
         (attn_low, rg_own, gate_sum, ffn_part, wgrads, wqkv_full, wo_full, heads_all, q_t, kv_all, inv_den,

time: 401 us -> 377 us (0.940)
  Pallas kernels: 380 us -> 360 us
    pallas_call x1, Pallas kernels: 146 us -> 135 us  [call_c(): pl.pallas_call(functools.partial(kernel_c, (n_shard, n_tp, chunks, hd)),...]
    pallas_call x1, Pallas kernels: 134 us -> 129 us  [call_a(): pl.pallas_call(functools.partial(kernel_a, (n_shard, n_tp, hd)), out_shap...]
    pallas_call x1, Pallas kernels: 100 us -> 95.7 us  [call_b(): pl.pallas_call(functools.partial(kernel_b, (n_shard, n_tp, chunks)), out_...]
where the time goes in v4:
time: 377 us; the launch traced here: 376 us
  Pallas kernels  360 us (95%)
  local copies, waits for them, and re-layouts  8.92 us (2%)
  other arithmetic  5.89 us (2%)
    pallas_call x1, Pallas kernels, call_c(): pl.pallas_call(functools.partial(kernel_c, (n_shard, n_tp, chunks, hd)),...  135 us
    pallas_call x1, Pallas kernels, call_a(): pl.pallas_call(functools.partial(kernel_a, (n_shard, n_tp, hd)), out_shap...  129 us
    pallas_call x1, Pallas kernels, call_b(): pl.pallas_call(functools.partial(kernel_b, (n_shard, n_tp, chunks)), out_...  95.7 us

profile of v4, /device:TPU:0, one launch (start us, length us, event | category | flops | bytes accessed | tf_op | source)
XLA Modules:
  0.0 376.2 jit_solution(8633699021404003868)
XLA Ops:
  1.3 129.1 %shard_map.273 = (bf16[1536,640]{1,0:T(8,128)(2,1)}, bf16[1536,1536]{1,0:T(8,128)(2,1)}, bf16[1536,1792]{1,0:T(8,128)(2,1)}, bf16[1536,1792]{1,0:T(8,128)(2,1)},...) custom-call(s32[1]{0:T(128)S(6)} %copy.38.length_ref, ...), custom_call_target="tpu_custom_call" | custom-call | tf_op jit(solution)/shard_map/pallas_call | solution.py:881
  130.4 95.7 %shard_map.274 = (bf16[768,1536]{1,0:T(8,128)(2,1)}, f32[384,1536]{1,0:T(8,128)}, bf16[192,1792]{1,0:T(8,128)(2,1)}, bf16[768,1536]{1,0:T(8,128)(2,1)}, bf16[3,1536,1792]{2,1,0:T(8,128)(2,1)}) custom-call(s32[1]{0:T(128)S(6)} %copy.38.length_ref, bf16[768,1536]{1,0:T(8,128)(2,1)} %og_ref.1, bf16[1536,1792]{1,0:T(8,128)(2,1)} %get-tuple-element.40.wd_hbm, ...), custom_call_target="tpu_custom_call" | custom-call | tf_op jit(solution)/shard_map/pallas_call | solution.py:1438
  226.1 135.2 %shard_map.275 = (bf16[768,1536]{1,0:T(8,128)(2,1)}, bf16[768,1536]{1,0:T(8,128)(2,1)}, f32[192,384]{1,0:T(8,128)}, f32[192,128]{1,0:T(8,128)}, f32[192,128]{1,0...) custom-call(s32[1]{0:T(128)S(6)} %copy.38.length_ref, ...), custom_call_target="tpu_custom_call" | custom-call | tf_op jit(solution)/shard_map/pallas_call | solution.py:1962
  361.3 0.0 copy-start.8
  361.3 0.0 copy-start
  361.3 0.0 copy-start.1
  361.3 4.6 %convert_element_type.9 = f32[768,1536]{1,0:T(8,128)} convert(bf16[768,1536]{1,0:T(8,128)(2,1)} %get-tuple-element.59) | non-fusion elementwise | flops 1179648 | bytes 7077888 | tf_op jit(solution)/shard_map/convert_element_type | solution.py:2061
  366.0 1.3 fusion
  367.3 1.3 slice_bitcast_fusion
  368.6 0.0 copy-done.8
  368.6 0.0 copy-done
  368.6 1.2 convert_multiply_fusion
  369.8 0.0 copy-done.1
  369.8 0.0 copy-start.5
  369.9 0.0 copy-start.7
  369.9 0.0 copy-start.6
  369.9 0.0 copy-start.4
  369.9 0.0 copy-start.3
  369.9 1.4 copy.39
  371.3 0.0 copy-done.5
  371.3 0.0 copy-start.2
  371.3 0.7 copy.40
  372.0 0.0 copy-done.7
  372.0 0.6 copy.41
  372.6 0.0 copy-done.6
  372.7 0.6 copy.42
  373.3 0.0 copy-done.4
  373.3 0.7 copy.43
  374.0 0.0 copy-done.3
  374.0 1.1 copy.44
  375.1 0.0 copy-done.2
  375.1 1.1 copy.45
  (1 shorter events, 0.0 us)
Async XLA Ops:
  361.3 7.3 %copy-start.8 = (bf16[192]{0:T(256)(128)(2,1)S(1)}, bf16[192]{0:T(256)(128)(2,1)}, u32[]{:S(2)}) copy-start(bf16[192]{0:T(256)(128)(2,1)} %gain_two_ref.3) | copy-start | bytes 1156
  361.3 7.3 %copy-start = (bf16[192,1792]{1,0:T(8,128)(2,1)S(1)}, bf16[192,1792]{1,0:T(8,128)(2,1)}, u32[]{:S(2)}) copy-start(bf16[192,1792]{1,0:T(8,128)(2,1)} %get-tuple-element.53.gate_hbm) | copy-start | bytes 2064388
  361.3 8.5 %copy-start.1 = (bf16[768,1536]{1,0:T(8,128)(2,1)S(1)}, bf16[768,1536]{1,0:T(8,128)(2,1)}, u32[]{:S(2)}) copy-start(bf16[768,1536]{1,0:T(8,128)(2,1)} %get-tuple-element.84) | copy-start | bytes 7077892
  369.8 1.4 copy-start.5
  369.9 2.2 copy-start.7
  369.9 2.8 copy-start.6
  369.9 3.4 copy-start.4
  369.9 4.1 %copy-start.3 = (f32[192,1728]{1,0:T(8,128)S(1)}, f32[192,1728]{1,0:T(8,128)}, u32[]{:S(2)}) copy-start(f32[192,1728]{1,0:T(8,128)} %get-tuple-element.95) | copy-start | bytes 3981316
  371.3 3.8 %copy-start.2 = (f32[192,1728]{1,0:T(8,128)S(1)}, f32[192,1728]{1,0:T(8,128)}, u32[]{:S(2)}) copy-start(f32[192,1728]{1,0:T(8,128)} %get-tuple-element.66) | copy-start | bytes 3981316

commit v5 on v4

--- a/solution.py
+++ b/solution.py
@@ -1180,10 +1180,12 @@
     h2t_hbm,
     resid_hbm,
     attn_low,
+    rg_out,
+    gate_out,
+    ffn_part,
+    wgrads,
     rg_own,
     gate_sum,
-    ffn_part,
-    wgrads,
     f_part,
     d_part,
     wg,
@@ -1381,13 +1383,23 @@
         free(2)
         gate.first()
 
+    leaving = [
+        pltpu.make_async_copy(rg_own, rg_out, loc_sem.at[2]),
+        pltpu.make_async_copy(gate_sum, gate_out, loc_sem.at[3]),
+    ]
+
+    def finish_gate():
+        gate.finish(use_gate)
+        leaving[1].start()
+
     total = chunks + 2 * last * LAG
     begin = (blocks + 2 * per_step - 1) // per_step
     events = {
         begin: start_gate,
         begin + total // 12: first_gate,
         begin + total // 4: gate.second,
-        total - 3: lambda: gate.finish(use_gate),
+        total - 4: leaving[0].start,
+        total - 3: finish_gate,
     }
 
     def tail(step, _):
@@ -1422,6 +1434,8 @@
         lines[n].drain()
         backs[n].drain()
     keeps.wait()
+    for cp in leaving:
+        cp.wait()
 
 
 def call_b(mesh, chunks, seq_lengths, out_grad, wd_full, act, wg_full, wu_full, h2t, resid):
@@ -1445,8 +1459,10 @@
             S((3, width, padded), BF16),
         ),
         in_specs=[sm, vm] + [hbm] * 6,
-        out_specs=(vm, vm, vm, hbm, hbm),
+        out_specs=(vm, hbm, hbm, hbm, hbm),
         scratch_shapes=[
+            pltpu.VMEM((half, width), F32),
+            pltpu.VMEM((block, padded), BF16),
             pltpu.VMEM((rows, width), BF16),
             pltpu.VMEM((rows, width), BF16),
             pltpu.VMEM((width, padded), BF16),
@@ -1504,13 +1520,19 @@
     wo_hbm,
     block_out,
     inp,
+    query_out,
+    key_out,
+    value_out,
+    out_out,
+    up_out,
+    down_out,
+    small,
     g_query,
     g_key,
     g_value,
     g_out,
     g_up,
     g_down,
-    small,
     rg_own,
     hid_ref,
     wqkv,
@@ -1558,6 +1580,7 @@
     t_send,
     t_recv,
     loc_sem,
+    out_sem,
 ):
     n_shard, n_tp, chunks, hd = shape
     at = Place(n_shard, n_tp)
@@ -1877,16 +1900,50 @@
         lax.fori_loop(0, width // block, weight_part, 0)
         rest.start()
 
+    leaving = [
+        pltpu.make_async_copy(src, dst, out_sem.at[i])
+        for i, (src, dst) in enumerate(
+            (
+                (g_down, down_out),
+                (g_up, up_out),
+                (g_query, query_out),
+                (g_key, key_out),
+                (g_value, value_out),
+                (g_out, out_out),
+            )
+        )
+    ]
+
+    def finish_rest():
+        rest.finish(use_rest)
+        for cp in leaving[2:]:
+            cp.start()
+
     events = {
         0: (lambda: trade(0).start(), turn_all),
         1: (parts, lambda: traded(0), lambda: trade(1).start()),
         2: (lambda: traded(1), lambda: trade(2).start(), gate_gain),
-        3: (rest.first, lambda: traded(2)),
-        5: (lambda: down.finish(use_down),),
-        6: (rest.second,),
-        8: (lambda: up.finish(use_up),),
-        10: (lambda: rest.finish(use_rest),),
+        4: (rest.first, lambda: traded(2)),
+        8: (lambda: down.finish(use_down), leaving[0].start),
+        10: (rest.second,),
+        14: (lambda: up.finish(use_up), leaving[1].start),
+        18: (finish_rest,),
+        19: (lambda: give_tiles(),),
     }
+
+    def give_tile(d, owner):
+        return remote(
+            tile.at[owner], tile.at[owner], t_send.at[d], t_recv.at[d],
+            at.z(lax.rem(t + d + 1, n_tp)),
+        )
+
+    def give_tiles():
+        tile[t] = jnp.zeros(tile.shape[1:], F32)
+        tile[t, 0:1, 0:block] = cols_acc[2].T[0:1, :]
+        tile[t, 1:2, 0:block] = cols_acc[3].T[0:1, :]
+        tile[t, 2:4, 0:128] = qk[3, 0:2, :]
+        for d in range(n_tp - 1):
+            give_tile(d, t).start()
 
     def tail(step, _):
         d1.reduce(step + ahead, final_d1)
@@ -1894,33 +1951,23 @@
         move_ffn(step + moved)
         for when, todo in events.items():
 
-            @pl.when(step == when * PER_SLOT)
+            @pl.when(step == when)
             def _():
                 for thing in todo:
                     thing()
 
         return 0
 
-    lax.fori_loop(0, max(chunks + 2 * last * LAG, 10 * PER_SLOT + 1), tail, 0)
+    lax.fori_loop(0, max(chunks + 2 * last * LAG, 20), tail, 0)
     keep_all(lambda cp: cp.start())
 
-    def give_tile(d, owner):
-        return remote(
-            tile.at[owner], tile.at[owner], t_send.at[d], t_recv.at[d],
-            at.z(lax.rem(t + d + 1, n_tp)),
-        )
-
-    tile[t] = jnp.zeros(tile.shape[1:], F32)
-    tile[t, 0:1, 0:block] = cols_acc[2].T[0:1, :]
-    tile[t, 1:2, 0:block] = cols_acc[3].T[0:1, :]
-    tile[t, 2:4, 0:128] = qk[3, 0:2, :]
-    for d in range(n_tp - 1):
-        give_tile(d, t).start()
     for w in (down, up, rest):
         w.drain()
     for thing in (d1, back, ffn, ffn_back):
         thing.drain()
     keep_all(lambda cp: cp.wait())
+    for cp in leaving:
+        cp.wait()
 
     @pl.when(c == 1)
     def _():
@@ -1973,8 +2020,14 @@
             S((8, 256), F32),
         ),
         in_specs=[sm] + [vm] * 13 + [hbm] * 11,
-        out_specs=(hbm,) + (vm,) * 8,
+        out_specs=(hbm, vm) + (hbm,) * 6 + (vm,),
         scratch_shapes=[
+            V((block, q_cols), F32),
+            V((block, kv_cols), F32),
+            V((block, kv_cols), F32),
+            V((block, q_cols), F32),
+            V((block, units), F32),
+            V((block, units), F32),
             V((rows // 2, width), F32),
             V((rows, width), BF16),
             V((width, qkv_cols), BF16),
@@ -2022,6 +2075,7 @@
             dma((n_tp - 1,)),
             dma((n_tp - 1,)),
             dma((15,)),
+            dma((6,)),
         ],
         compiler_params=pltpu.CompilerParams(
             collective_id=2, has_side_effects=True, vmem_limit_bytes=VMEM_LIMIT
@@ -2036,7 +2090,7 @@
 
 CHUNKS = 6
 CHUNKS_C = 12
-PER_STEP = 3
+PER_STEP = 4
 PER_SLOT = 2
 
 

time: 377 us -> 372 us (0.987)
  Pallas kernels: 360 us -> 355 us
where the time goes in v5:
time: 372 us; the launch traced here: 371 us
  Pallas kernels  355 us (95%)
  local copies, waits for them, and re-layouts  8.92 us (2%)
  other arithmetic  5.89 us (2%)
    pallas_call x1, Pallas kernels, call_c(): pl.pallas_call(functools.partial(kernel_c, (n_shard, n_tp, chunks, hd)),...  132 us
    pallas_call x1, Pallas kernels, call_a(): pl.pallas_call(functools.partial(kernel_a, (n_shard, n_tp, hd)), out_shap...  129 us
    pallas_call x1, Pallas kernels, call_b(): pl.pallas_call(functools.partial(kernel_b, (n_shard, n_tp, chunks)), out_...  94.3 us

profile of v5, /device:TPU:0, one launch (start us, length us, event | category | flops | bytes accessed | tf_op | source)
XLA Modules:
  0.0 371.5 jit_solution(7110702247458013587)
XLA Ops:
  1.3 129.1 %shard_map.273 = (bf16[1536,640]{1,0:T(8,128)(2,1)}, bf16[1536,1536]{1,0:T(8,128)(2,1)}, bf16[1536,1792]{1,0:T(8,128)(2,1)}, bf16[1536,1792]{1,0:T(8,128)(2,1)},...) custom-call(s32[1]{0:T(128)S(6)} %copy.38.length_ref, ...), custom_call_target="tpu_custom_call" | custom-call | tf_op jit(solution)/shard_map/pallas_call | solution.py:881
  130.4 94.3 %shard_map.274 = (bf16[768,1536]{1,0:T(8,128)(2,1)}, f32[384,1536]{1,0:T(8,128)}, bf16[192,1792]{1,0:T(8,128)(2,1)}, bf16[768,1536]{1,0:T(8,128)(2,1)}, bf16[3,1536,1792]{2,1,0:T(8,128)(2,1)}) custom-call(s32[1]{0:T(128)S(6)} %copy.38.length_ref, bf16[768,1536]{1,0:T(8,128)(2,1)} %og_ref.1, bf16[1536,1792]{1,0:T(8,128)(2,1)} %get-tuple-element.40.wd_hbm, ...), custom_call_target="tpu_custom_call" | custom-call | tf_op jit(solution)/shard_map/pallas_call | solution.py:1452
  224.7 131.9 %shard_map.275 = (bf16[768,1536]{1,0:T(8,128)(2,1)}, bf16[768,1536]{1,0:T(8,128)(2,1)}, f32[192,384]{1,0:T(8,128)}, f32[192,128]{1,0:T(8,128)}, f32[192,128]{1,0...) custom-call(s32[1]{0:T(128)S(6)} %copy.38.length_ref, ...), custom_call_target="tpu_custom_call" | custom-call | tf_op jit(solution)/shard_map/pallas_call | solution.py:2009
  356.6 0.0 copy-start.8
  356.6 0.0 copy-start
  356.6 0.0 copy-start.1
  356.6 4.6 %convert_element_type.9 = f32[768,1536]{1,0:T(8,128)} convert(bf16[768,1536]{1,0:T(8,128)(2,1)} %get-tuple-element.59) | non-fusion elementwise | flops 1179648 | bytes 7077888 | tf_op jit(solution)/shard_map/convert_element_type | solution.py:2115
  361.3 1.3 fusion
  362.6 1.3 slice_bitcast_fusion
  363.9 0.0 copy-done.8
  363.9 0.0 copy-done
  363.9 1.2 convert_multiply_fusion
  365.1 0.0 copy-done.1
  365.1 0.0 copy-start.5
  365.1 0.0 copy-start.7
  365.1 0.0 copy-start.6
  365.1 0.0 copy-start.4
  365.2 0.0 copy-start.3
  365.2 1.4 copy.39
  366.6 0.0 copy-done.5
  366.6 0.0 copy-start.2
  366.6 0.7 copy.40
  367.3 0.0 copy-done.7
  367.3 0.6 copy.41
  367.9 0.0 copy-done.6
  367.9 0.6 copy.42
  368.6 0.0 copy-done.4
  368.6 0.7 copy.43
  369.3 0.0 copy-done.3
  369.3 1.1 copy.44
  370.4 0.0 copy-done.2
  370.4 1.1 copy.45
  (1 shorter events, 0.0 us)
Async XLA Ops:
  356.6 7.3 %copy-start.8 = (bf16[192]{0:T(256)(128)(2,1)S(1)}, bf16[192]{0:T(256)(128)(2,1)}, u32[]{:S(2)}) copy-start(bf16[192]{0:T(256)(128)(2,1)} %gain_two_ref.3) | copy-start | bytes 1156
  356.6 7.3 %copy-start = (bf16[192,1792]{1,0:T(8,128)(2,1)S(1)}, bf16[192,1792]{1,0:T(8,128)(2,1)}, u32[]{:S(2)}) copy-start(bf16[192,1792]{1,0:T(8,128)(2,1)} %get-tuple-element.53.gate_hbm) | copy-start | bytes 2064388
  356.6 8.5 %copy-start.1 = (bf16[768,1536]{1,0:T(8,128)(2,1)S(1)}, bf16[768,1536]{1,0:T(8,128)(2,1)}, u32[]{:S(2)}) copy-start(bf16[768,1536]{1,0:T(8,128)(2,1)} %get-tuple-element.84) | copy-start | bytes 7077892
  365.1 1.4 copy-start.5
  365.1 2.2 copy-start.7
  365.1 2.8 copy-start.6
  365.1 3.4 copy-start.4
  365.2 4.1 %copy-start.3 = (f32[192,1728]{1,0:T(8,128)S(1)}, f32[192,1728]{1,0:T(8,128)}, u32[]{:S(2)}) copy-start(f32[192,1728]{1,0:T(8,128)} %get-tuple-element.95) | copy-start | bytes 3981316
  366.6 3.8 %copy-start.2 = (f32[192,1728]{1,0:T(8,128)S(1)}, f32[192,1728]{1,0:T(8,128)}, u32[]{:S(2)}) copy-start(f32[192,1728]{1,0:T(8,128)} %get-tuple-element.66) | copy-start | bytes 3981316

commit v6 on v5

--- a/solution.py
+++ b/solution.py
@@ -816,7 +816,7 @@
 
         act_copy(f).start()
 
-        @pl.when(f == tiles - 2)
+        @pl.when(f == tiles // 2 - 1)
         def _():
             down.relay()
 

time: 372 us -> 367 us (0.987)
  Pallas kernels: 355 us -> 351 us
    pallas_call x1, Pallas kernels: 129 us -> 124 us  [call_a(): pl.pallas_call(functools.partial(kernel_a, (n_shard, n_tp, hd)), out_shap...]
where the time goes in v6:
time: 367 us
  Pallas kernels  351 us (96%)
  local copies, waits for them, and re-layouts  8.92 us (2%)
  other arithmetic  5.89 us (2%)
    pallas_call x1, Pallas kernels, call_c(): pl.pallas_call(functools.partial(kernel_c, (n_shard, n_tp, chunks, hd)),...  132 us
    pallas_call x1, Pallas kernels, call_a(): pl.pallas_call(functools.partial(kernel_a, (n_shard, n_tp, hd)), out_shap...  124 us
    pallas_call x1, Pallas kernels, call_b(): pl.pallas_call(functools.partial(kernel_b, (n_shard, n_tp, chunks)), out_...  94.4 us

profile of v6, /device:TPU:0, one launch (start us, length us, event | category | flops | bytes accessed | tf_op | source)
XLA Modules:
  0.0 366.8 jit_solution(10893963609185881000)
XLA Ops:
  1.3 124.4 %shard_map.273 = (bf16[1536,640]{1,0:T(8,128)(2,1)}, bf16[1536,1536]{1,0:T(8,128)(2,1)}, bf16[1536,1792]{1,0:T(8,128)(2,1)}, bf16[1536,1792]{1,0:T(8,128)(2,1)},...) custom-call(s32[1]{0:T(128)S(6)} %copy.38.length_ref, ...), custom_call_target="tpu_custom_call" | custom-call | tf_op jit(solution)/shard_map/pallas_call | solution.py:881
  125.7 94.4 %shard_map.274 = (bf16[768,1536]{1,0:T(8,128)(2,1)}, f32[384,1536]{1,0:T(8,128)}, bf16[192,1792]{1,0:T(8,128)(2,1)}, bf16[768,1536]{1,0:T(8,128)(2,1)}, bf16[3,1536,1792]{2,1,0:T(8,128)(2,1)}) custom-call(s32[1]{0:T(128)S(6)} %copy.38.length_ref, bf16[768,1536]{1,0:T(8,128)(2,1)} %og_ref.1, bf16[1536,1792]{1,0:T(8,128)(2,1)} %get-tuple-element.40.wd_hbm, ...), custom_call_target="tpu_custom_call" | custom-call | tf_op jit(solution)/shard_map/pallas_call | solution.py:1452
  220.1 131.9 %shard_map.275 = (bf16[768,1536]{1,0:T(8,128)(2,1)}, bf16[768,1536]{1,0:T(8,128)(2,1)}, f32[192,384]{1,0:T(8,128)}, f32[192,128]{1,0:T(8,128)}, f32[192,128]{1,0...) custom-call(s32[1]{0:T(128)S(6)} %copy.38.length_ref, ...), custom_call_target="tpu_custom_call" | custom-call | tf_op jit(solution)/shard_map/pallas_call | solution.py:2009
  351.9 0.0 copy-start.8
  352.0 0.0 copy-start
  352.0 0.0 copy-start.1
  352.0 4.6 %convert_element_type.9 = f32[768,1536]{1,0:T(8,128)} convert(bf16[768,1536]{1,0:T(8,128)(2,1)} %get-tuple-element.59) | non-fusion elementwise | flops 1179648 | bytes 7077888 | tf_op jit(solution)/shard_map/convert_element_type | solution.py:2115
  356.6 1.3 fusion
  358.0 1.3 slice_bitcast_fusion
  359.2 0.0 copy-done.8
  359.2 0.0 copy-done
  359.2 1.2 convert_multiply_fusion
  360.5 0.0 copy-done.1
  360.5 0.0 copy-start.5
  360.5 0.0 copy-start.7
  360.5 0.0 copy-start.6
  360.5 0.0 copy-start.4
  360.5 0.0 copy-start.3
  360.5 1.4 copy.39
  361.9 0.0 copy-done.5
  361.9 0.0 copy-start.2
  361.9 0.7 copy.40
  362.6 0.0 copy-done.7
  362.6 0.6 copy.41
  363.3 0.0 copy-done.6
  363.3 0.6 copy.42
  363.9 0.0 copy-done.4
  363.9 0.7 copy.43
  364.6 0.0 copy-done.3
  364.7 1.1 copy.44
  365.7 0.0 copy-done.2
  365.7 1.1 copy.45
  (1 shorter events, 0.0 us)
Async XLA Ops:
  351.9 7.3 %copy-start.8 = (bf16[192]{0:T(256)(128)(2,1)S(1)}, bf16[192]{0:T(256)(128)(2,1)}, u32[]{:S(2)}) copy-start(bf16[192]{0:T(256)(128)(2,1)} %gain_two_ref.3) | copy-start | bytes 1156
  352.0 7.3 %copy-start = (bf16[192,1792]{1,0:T(8,128)(2,1)S(1)}, bf16[192,1792]{1,0:T(8,128)(2,1)}, u32[]{:S(2)}) copy-start(bf16[192,1792]{1,0:T(8,128)(2,1)} %get-tuple-element.53.gate_hbm) | copy-start | bytes 2064388
  352.0 8.5 %copy-start.1 = (bf16[768,1536]{1,0:T(8,128)(2,1)S(1)}, bf16[768,1536]{1,0:T(8,128)(2,1)}, u32[]{:S(2)}) copy-start(bf16[768,1536]{1,0:T(8,128)(2,1)} %get-tuple-element.84) | copy-start | bytes 7077892
  360.5 1.4 copy-start.5
  360.5 2.2 copy-start.7
  360.5 2.8 copy-start.6
  360.5 3.4 copy-start.4
  360.5 4.1 %copy-start.3 = (f32[192,1728]{1,0:T(8,128)S(1)}, f32[192,1728]{1,0:T(8,128)}, u32[]{:S(2)}) copy-start(f32[192,1728]{1,0:T(8,128)} %get-tuple-element.95) | copy-start | bytes 3981316
  361.9 3.8 %copy-start.2 = (f32[192,1728]{1,0:T(8,128)S(1)}, f32[192,1728]{1,0:T(8,128)}, u32[]{:S(2)}) copy-start(f32[192,1728]{1,0:T(8,128)} %get-tuple-element.66) | copy-start | bytes 3981316
